TPU v7x, 512 devices: a whole 4x8x8 slice. The times are simulated.
512 devices in a mesh: tile: 64 (over x, z, core), trc: 8 (over y).
Axes of the slice: x: 4, y: 8, z: 8, core: 2. Of those that a mesh axis runs over, the one named last changes fastest.
Arguments:
- cotangent: float32 [56, 16, 128, 1024], P('trc', None, 'tile'), may hold values from -0.5 to 2.5
- uptake_rate: bfloat16 [56, 8, 128, 1024], P('trc', None, 'tile'), may hold values from 0.049804688 to 2
- nutrient: float32 [8, 128, 1024], P(None, 'tile'), may hold values from 0.02 to 5
- depth_levels: int32 [128, 1024], P('tile'), may hold values from 0 to 16, as said below
- region_ids: int32 [128, 1024], P('tile'), may hold values from 0 to 63
- uptake_matrix: bfloat16 [56, 56], replicated, may hold values from -0.75 to 0.75
- province_rates: float32 [64, 56], P(None, 'trc'), may hold values from 0.2 to 2
- half_saturation: float32 [56], P('trc'), may hold values from 0.1 to 1
- biharmonic: float32 [56], P('trc'), may hold values from 0.003 to 0.025
- sinking: float32 [56], P('trc'), may hold values from 0.05 to 0.6
Outputs:
- tracer_grad: float32 [56, 16, 128, 1024], P('trc', None, 'tile')
- rate_grad: float32 [64, 56], P('tile', 'trc')
Inputs may be any that keep to these rules, and one draw needn't show every extreme that they name: `depth_levels`: on some device every column is wet and one of its columns has all 16 levels wet; every device has at least 256 wet columns, and some devices have dry ones.
All inputs are finite; a program needn't handle non-finite values.
Results may differ from a plain program's by a relative error of at most 0.0014.
Values may be sent and summed in bfloat16 or wider, within the bound.
No kernel may reach another device: no remote copies, remote signals or barrier semaphores. Data moves between devices by JAX's collectives and lax.ppermute only.
A program may use at most 64 MiB of HBM per device.

v0:
```python
import jax
import jax.numpy as jnp
from jax import lax
from jax.sharding import PartitionSpec as P


def padded(cells, sides, width):
    for axis, dim in sides:
        count = lax.axis_size(axis)
        ends = count - 1
        head = lax.slice_in_dim(cells, 0, width, axis=dim)
        tail = lax.slice_in_dim(cells, cells.shape[dim] - width, cells.shape[dim], axis=dim)
        cells = jnp.concatenate(
            [
                lax.ppermute(tail, axis, [(i, (i + 1) % count) for i in range(ends)]),
                cells,
                lax.ppermute(head, axis, [((i + 1) % count, i) for i in range(ends)]),
            ],
            axis=dim,
        )
    return cells


def laplacian(extended, extended_wet):
    centre = extended[:, :, 1:-1]
    centre_wet = extended_wet[:, 1:-1]
    northern = extended[:, :, 2:]
    southern = extended[:, :, :-2]
    north_wet = extended_wet[:, 2:]
    south_wet = extended_wet[:, :-2]
    eastern = jnp.roll(centre, -1, 3)
    western = jnp.roll(centre, 1, 3)
    east_wet = jnp.roll(centre_wet, -1, 2)
    west_wet = jnp.roll(centre_wet, 1, 2)
    return centre_wet * (
        north_wet * (northern - centre)
        + south_wet * (southern - centre)
        + east_wet * (eastern - centre)
        + west_wet * (western - centre)
    )


def body(
    cotangent,
    uptake_rate,
    nutrient,
    depth_levels,
    region_ids,
    uptake_matrix,
    province_rates,
    half_saturation,
    biharmonic,
    sinking,
):
    own_count, levels, band_rows, zonal = cotangent.shape
    sunlit = uptake_rate.shape[1]
    columns = band_rows * zonal
    provinces = province_rates.shape[0]
    level_ids = lax.broadcasted_iota(jnp.int32, (levels, band_rows, zonal), 0)
    wet_mask = (level_ids < depth_levels[None]).astype(jnp.float32)
    grad_wet = cotangent * wet_mask[None]
    limiter = nutrient[None] / (nutrient[None] + half_saturation[:, None, None, None])
    province_ids = lax.broadcasted_iota(jnp.int32, (provinces, columns), 0)
    one_hot = (region_ids.reshape(1, columns) == province_ids).astype(jnp.float32)
    rate_cells = lax.dot_general(
        province_rates,
        one_hot,
        (((0,), (0,)), ((), ())),
        precision=lax.Precision.HIGHEST,
        preferred_element_type=jnp.float32,
    )
    weighted = (
        rate_cells.reshape(own_count, 1, band_rows, zonal) * limiter * grad_wet[:, :sunlit]
    ).astype(jnp.bfloat16)
    flat_weighted = weighted.reshape(own_count, sunlit * columns)
    first_tracer = lax.axis_index("trc") * own_count
    column_term = jnp.sum(limiter * uptake_rate.astype(jnp.float32) * grad_wet[:, :sunlit], axis=1)
    province_part = lax.dot_general(
        one_hot,
        column_term.reshape(own_count, columns),
        (((1,), (1,)), ((), ())),
        precision=lax.Precision.HIGHEST,
        preferred_element_type=jnp.float32,
    )
    rate_grad = lax.psum_scatter(province_part, "tile", scatter_dimension=0, tiled=True) * (
        1.0 / (sunlit * columns)
    )
    coeff_cols = lax.dynamic_slice_in_dim(uptake_matrix, first_tracer, own_count, 1)
    cross_feed = lax.dot_general(
        coeff_cols,
        lax.all_gather(flat_weighted, "trc", axis=0, tiled=True),
        (((0,), (0,)), ((), ())),
        preferred_element_type=jnp.float32,
    )
    cross_cells = cross_feed.reshape(own_count, sunlit, band_rows, zonal)
    grad_top = grad_wet[:, :sunlit] + wet_mask[None, :sunlit] * cross_cells
    grad_mid = jnp.concatenate([grad_top, grad_wet[:, sunlit:]], axis=1)
    coupling = sinking[:, None, None, None] * (wet_mask[:-1] * wet_mask[1:])[None]
    grad_col = grad_mid + jnp.concatenate(
        [
            coupling * (grad_mid[:, 1:] - grad_mid[:, :-1]),
            jnp.zeros((own_count, 1, band_rows, zonal), jnp.float32),
        ],
        axis=1,
    )
    stacked = jnp.concatenate([grad_col, wet_mask[None]], axis=0)
    extended = padded(stacked, (("tile", 2),), 1)
    extended_wet = extended[own_count]
    lap_once = laplacian(extended[:own_count], extended_wet)
    lap_extended = padded(lap_once.astype(jnp.bfloat16), (("tile", 2),), 1).astype(lap_once.dtype)
    lap_twice = laplacian(lap_extended, extended_wet)
    tracer_grad = grad_col - biharmonic[:, None, None, None] * lap_twice
    return (tracer_grad, rate_grad)


def solution(mesh):
    return jax.shard_map(
        body,
        mesh=mesh,
        in_specs=(
            P("trc", None, "tile", None),
            P("trc", None, "tile", None),
            P(None, "tile", None),
            P("tile", None),
            P("tile", None),
            P(),
            P(None, "trc"),
            P("trc"),
            P("trc"),
            P("trc"),
        ),
        out_specs=(P("trc", None, "tile", None), P("tile", "trc")),
        check_vma=False,
    )
```

profile of v0, /device:TPU:1, one launch (start us, length us, event | category | flops | bytes accessed | tf_op | source)
XLA Modules:
  0.0 344.0 jit_solution(9027510290453217033)
XLA Ops:
  7.2 0.8 fusion.32
  8.0 0.9 copy.13
  8.9 0.7 copy.26
  9.7 1.0 convolution_bitcast_fusion
  10.7 1.5 copy_multiply_fusion
  12.2 0.4 multiply_reduce_fusion
  12.8 0.9 reshape.43
  13.7 1.4 dynamic-slice
  15.1 0.7 slice_multiply_fusion
  15.8 43.5 %all-gather.3.cloned.1.call-done = bf16[8,7,16384]{2,1,0:T(8,128)(2,1)} async-done(((bf16[1,7,16384]{2,1,0:T(8,128)(2,1)}), bf16[8,7,16384]{2,1,0:T(8,128)(2,1)}) %all-gather.3.cloned.1.call-update) | async-done | bytes 1835024 | tf_op jit(solution)/shard_map/all_gather | solution.py:91
  59.2 2.3 reshape.44
  61.6 1.3 fusion.34
  62.9 1.5 reshape.41
  65.1 7.5 %collective-permute-start = (f32[8,16,1,1024]{3,1,2,0:T(8,128)S(1)}, f32[8,16,1,1024]{3,1,2,0:T(8,128)S(1)}, u32[]{:S(2)}, u32[]{:S(2)}) collective-permute-start(f32[8,16,1,1024]{3,1,2,0:T(8,128)S(1)} %get-tuple-element.7), channel_id=1, source_target_pairs={{0,8},{8,16},{16,24},{24,32},{32,40},{40,48},{48,56},{56,64},{64,7... | collective-permute-start | bytes 1572872 | tf_op jit(solution)/shard_map/ppermute | solution.py:15
  72.6 1.9 collective-permute-start.1
  75.0 3.7 %collective-permute-done = f32[8,16,1,1024]{3,1,2,0:T(8,128)S(1)} collective-permute-done((f32[8,16,1,1024]{3,1,2,0:T(8,128)S(1)}, f32[8,16,1,1024]{3,1,2,0:T(8,128)S(1)}, u32[]{:S(2)}, u32[]{:S(2)}) %collective-permute-start) | collective-permute-done | bytes 524320 | tf_op jit(solution)/shard_map/ppermute | solution.py:15
  78.7 4.4 %collective-permute-done.1 = f32[8,16,1,1024]{3,1,2,0:T(8,128)S(1)} collective-permute-done((f32[8,16,1,1024]{3,1,2,0:T(8,128)S(1)}, f32[8,16,1,1024]{3,1,2,0:T(8,128)S(1)}, u32[]{:S(2)}, u32[]{:S(2)}) %collective-permute-start.1) | collective-permute-done | bytes 524320 | tf_op jit(solution)/shard_map/ppermute | solution.py:17
  83.4 0.6 fusion.19
  84.0 1.9 collective-permute-start.3
  86.0 3.6 %collective-permute-start.2 = (bf16[7,16,1,1024]{3,1,2,0:T(8,128)(2,1)S(1)}, bf16[7,16,1,1024]{3,1,2,0:T(8,128)(2,1)S(1)}, u32[]{:S(2)}, u32[]{:S(2)}) collective-permute-start(bf16[7,16,1,1024]{3,1,2,0:T(8,128)(2,1)S(1)} %get-tuple-element.17), channel_id=1, source_target_pairs={{0,8},{8,16},{16,24},{24,32},{32,40},{40,48},{48,56},{56,64},{64,7... | collective-permute-start | bytes 688136 | tf_op jit(solution)/shard_map/ppermute | solution.py:15
  90.0 242.9 %all-reduce.1 = f32[64,7]{1,0:T(8,128)S(1)} all-reduce(f32[64,7]{1,0:T(8,128)S(1)} %fusion.27), channel_id=2, replica_groups=mesh['tile'=64,'trc'=8] {'tile'}, use_global_device_ids=true, to_apply=%region_1.0.clone | all-reduce | flops 448 | bytes 3584
  332.9 1.2 dynamic-slice_multiply_fusion
  334.9 0.6 fusion.11
  335.5 1.6 copy.17
  (46 shorter events, 3.0 us)
Async XLA Ops:
  7.2 54.4 %copy-start = (bf16[56,56]{1,0:T(8,128)(2,1)S(1)}, bf16[56,56]{1,0:T(8,128)(2,1)}, u32[]{:S(2)}) copy-start(bf16[56,56]{1,0:T(8,128)(2,1)} %param.15) | copy-start | bytes 18820
  7.2 5.0 %copy-start.3 = (bf16[7,8,2,1024]{3,2,1,0:T(2,128)(2,1)S(1)}, bf16[7,8,2,1024]{3,2,1,0:T(2,128)(2,1)}, u32[]{:S(2)}) copy-start(bf16[7,8,2,1024]{3,2,1,0:T(2,128)(2,1)} %param.11) | copy-start | bytes 688132
  7.2 5.0 %copy-start.7 = (f32[7]{0:T(128)S(1)}, f32[7]{0:T(128)}, u32[]{:S(2)}) copy-start(f32[7]{0:T(128)} %param.17) | copy-start | bytes 88
  7.2 52.0 %all-gather.3.cloned.1.call-start = ((), (), s32[]{:S(2)}) async-start(), calls=%async_computation | async-start | bytes 2359296 | tf_op jit(solution)/shard_map/all_gather | solution.py:91
  8.0 7.1 %copy-start.1 = (f32[16,2,1024]{2,0,1:T(8,128)}, f32[16,2,1024]{2,0,1:T(8,128)S(1)}, u32[]{:S(2)}) copy-start(f32[16,2,1024]{2,0,1:T(8,128)S(1)} %fusion.32) | copy-start | bytes 393220
  9.6 1.0 copy-start.5
  12.2 2.9 copy-start.4
  61.5 2.8 slice-start
  61.6 3.0 copy-start.8
  62.9 1.7 copy-start.2
  65.1 13.6 %collective-permute-start = (f32[8,16,1,1024]{3,1,2,0:T(8,128)S(1)}, f32[8,16,1,1024]{3,1,2,0:T(8,128)S(1)}, u32[]{:S(2)}, u32[]{:S(2)}) collective-permute-start(f32[8,16,1,1024]{3,1,2,0:T(8,128)S(1)} %get-tuple-element.7), channel_id=1, source_target_pairs={{0,8},{8,16},{16,24},{24,32},{32,40},{40,48},{48,56},{56,64},{64,7... | collective-permute-start | bytes 1572872 | tf_op jit(solution)/shard_map/ppermute | solution.py:15
  72.6 10.5 %collective-permute-start.1 = (f32[8,16,1,1024]{3,1,2,0:T(8,128)S(1)}, f32[8,16,1,1024]{3,1,2,0:T(8,128)S(1)}, u32[]{:S(2)}, u32[]{:S(2)}) collective-permute-start(f32[8,16,1,1024]{3,1,2,0:T(8,128)S(1)} %get-tuple-element.6), channel_id=1, source_target_pairs={{8,0},{16,8},{24,16},{32,24},{40,32},{48,40},{56,48},{64,56},{72,6... | collective-permute-start | bytes 1572872 | tf_op jit(solution)/shard_map/ppermute | solution.py:17
  83.4 6.2 %copy-start.6 = (s32[1,8,2,128]{3,1,2,0:T(8,128)S(1)}, s32[1,8,2,128]{3,1,2,0:T(8,128)}, u32[]{:S(2)}) copy-start(s32[1,8,2,128]{3,1,2,0:T(8,128)} %copy-done.5) | copy-start | bytes 24580
  84.0 250.0 %collective-permute-start.3 = (bf16[7,16,1,1024]{3,1,2,0:T(8,128)(2,1)S(1)}, bf16[7,16,1,1024]{3,1,2,0:T(8,128)(2,1)S(1)}, u32[]{:S(2)}, u32[]{:S(2)}) collective-permute-start(bf16[7,16,1,1024]{3,1,2,0:T(8,128)(2,1)S(1)} %get-tuple-element.18), channel_id=1, source_target_pairs={{8,0},{16,8},{24,16},{32,24},{40,32},{48,40},{56,48},{64,56},{72,6... | collective-permute-start | bytes 688136 | tf_op jit(solution)/shard_map/ppermute | solution.py:17
  86.0 248.1 %collective-permute-start.2 = (bf16[7,16,1,1024]{3,1,2,0:T(8,128)(2,1)S(1)}, bf16[7,16,1,1024]{3,1,2,0:T(8,128)(2,1)S(1)}, u32[]{:S(2)}, u32[]{:S(2)}) collective-permute-start(bf16[7,16,1,1024]{3,1,2,0:T(8,128)(2,1)S(1)} %get-tuple-element.17), channel_id=1, source_target_pairs={{0,8},{8,16},{16,24},{24,32},{32,40},{40,48},{48,56},{56,64},{64,7... | collective-permute-start | bytes 688136 | tf_op jit(solution)/shard_map/ppermute | solution.py:15
  334.2 0.7 copy-start.9
Sparse Core Ops, SparseCore 0:
  13.8 45.3 all-gather.2
where the time goes:
time: 348 us; the launch traced here: 344 us
  blocking collectives  243 us (70%)
  waiting for transfers between devices  51.6 us (15%)
  starting transfers between devices  15 us (4%)
  between operations  14.4 us (4%)
  local copies, waits for them, and re-layouts  10.8 us (3%)
  other arithmetic  6.74 us (2%)
    unnamed x1, blocking collectives  243 us
    all_gather x1, waiting for transfers between devices, body(): lax.all_gather(flat_weighted, 'trc', axis=0, tiled=True)  43.5 us
    ppermute x2, starting transfers between devices, padded(): lax.ppermute(tail, axis, [(i, (i + 1) % count) for i in range(ends)])  11.1 us
    unnamed x27, local copies, waits for them, and re-layouts  8.02 us
  transfers between devices with their start and end apart: 5, of which 3 were waited for; matrix products, arithmetic and copies ran while one was open for 1% of the time, Pallas kernels for 0%

commit v1 on v0

v1 whole, which is shorter than its diff:
```python
import jax
import jax.numpy as jnp
from jax import lax
from jax.sharding import PartitionSpec as P

SCALE = 256.0


def shifted_sum(values, wet):
    eastern = jnp.roll(values, -1, 3)
    western = jnp.roll(values, 1, 3)
    east_wet = jnp.roll(wet, -1, 2)
    west_wet = jnp.roll(wet, 1, 2)
    return east_wet * (eastern - values) + west_wet * (western - values)


def laplacian(extended, extended_wet):
    centre = extended[:, :, 1:-1]
    centre_wet = extended_wet[:, 1:-1]
    return centre_wet * (
        extended_wet[:, 2:] * (extended[:, :, 2:] - centre)
        + extended_wet[:, :-2] * (extended[:, :, :-2] - centre)
        + shifted_sum(centre, centre_wet)
    )


def body(
    cotangent,
    uptake_rate,
    nutrient,
    depth_levels,
    region_ids,
    uptake_matrix,
    province_rates,
    half_saturation,
    biharmonic,
    sinking,
):
    own_count, levels, band_rows, zonal = cotangent.shape
    sunlit = uptake_rate.shape[1]
    columns = band_rows * zonal
    provinces = province_rates.shape[0]
    tiles = lax.axis_size("tile")
    up = [(i, i + 1) for i in range(tiles - 1)]
    down = [(i + 1, i) for i in range(tiles - 1)]
    depth_float = depth_levels.astype(jnp.float32)
    depth_south = lax.ppermute(depth_float, "tile", up)
    depth_north = lax.ppermute(depth_float, "tile", down)
    level_ids = lax.broadcasted_iota(jnp.int32, (levels, band_rows, zonal), 0)
    wet_mask = (level_ids < depth_levels[None]).astype(jnp.float32)
    grad_wet = cotangent * wet_mask[None]
    limiter = nutrient[None] / (nutrient[None] + half_saturation[:, None, None, None])
    province_ids = lax.broadcasted_iota(jnp.int32, (provinces, columns), 0)
    one_hot = (region_ids.reshape(1, columns) == province_ids).astype(jnp.float32)
    rate_cells = lax.dot_general(
        province_rates,
        one_hot,
        (((0,), (0,)), ((), ())),
        precision=lax.Precision.HIGHEST,
        preferred_element_type=jnp.float32,
    )
    weighted = (
        rate_cells.reshape(own_count, 1, band_rows, zonal) * limiter * grad_wet[:, :sunlit]
    ).astype(jnp.bfloat16)
    by_level = weighted.transpose(1, 0, 2, 3).reshape(sunlit, own_count, columns)
    all_tracers = lax.all_to_all(by_level, "trc", 0, 0, tiled=True)
    column_term = jnp.sum(limiter * uptake_rate.astype(jnp.float32) * grad_wet[:, :sunlit], axis=1)
    province_part = lax.dot_general(
        one_hot,
        column_term.reshape(own_count, columns),
        (((1,), (1,)), ((), ())),
        precision=lax.Precision.HIGHEST,
        preferred_element_type=jnp.float32,
    )
    own_parts = lax.all_to_all(province_part, "tile", 0, 0, tiled=True)
    rate_grad = jnp.sum(own_parts, axis=0, keepdims=True) * (1.0 / (sunlit * columns))
    fed = lax.dot_general(
        uptake_matrix,
        all_tracers.reshape(sunlit * own_count, columns),
        (((0,), (0,)), ((), ())),
        preferred_element_type=jnp.float32,
    )
    fed = (fed * SCALE).astype(jnp.float16).reshape(sunlit, own_count, columns)
    fed = lax.all_to_all(fed, "trc", 0, 0, tiled=True)
    cross_cells = (fed.astype(jnp.float32) * (1.0 / SCALE)).reshape(sunlit, own_count, band_rows, zonal)
    cross_cells = cross_cells.transpose(1, 0, 2, 3)
    grad_top = grad_wet[:, :sunlit] + wet_mask[None, :sunlit] * cross_cells
    grad_mid = jnp.concatenate([grad_top, grad_wet[:, sunlit:]], axis=1)
    coupling = sinking[:, None, None, None] * (wet_mask[:-1] * wet_mask[1:])[None]
    grad_col = grad_mid + jnp.concatenate(
        [
            coupling * (grad_mid[:, 1:] - grad_mid[:, :-1]),
            jnp.zeros((own_count, 1, band_rows, zonal), jnp.float32),
        ],
        axis=1,
    )
    halo = grad_col.astype(jnp.bfloat16)
    south = lax.ppermute(halo, "tile", up).astype(jnp.float32)
    north = lax.ppermute(halo, "tile", down).astype(jnp.float32)
    extended = jnp.concatenate([south, grad_col, north], axis=2)
    extended_depth = jnp.concatenate([depth_south, depth_float, depth_north], axis=0)
    row_levels = lax.broadcasted_iota(jnp.int32, (levels,) + extended_depth.shape, 0)
    extended_wet = (row_levels.astype(jnp.float32) < extended_depth[None]).astype(jnp.float32)
    lap_once = laplacian(extended, extended_wet)
    lap_twice = laplacian(lap_once, extended_wet[:, 1:-1])
    tracer_grad = grad_col - biharmonic[:, None, None, None] * lap_twice
    return (tracer_grad, rate_grad)


def solution(mesh):
    return jax.shard_map(
        body,
        mesh=mesh,
        in_specs=(
            P("trc", None, "tile", None),
            P("trc", None, "tile", None),
            P(None, "tile", None),
            P("tile", None),
            P("tile", None),
            P(),
            P(None, "trc"),
            P("trc"),
            P("trc"),
            P("trc"),
        ),
        out_specs=(P("trc", None, "tile", None), P("tile", "trc")),
        check_vma=False,
    )
```

time: 348 us -> 103 us (0.30)
  the two profiles are of different devices: /device:TPU:1 before, /device:TPU:2 now
where the time goes in v1:
time: 103 us
  starting transfers between devices  36.3 us (35%)
  waiting for transfers between devices  35.4 us (34%)
  other arithmetic  20 us (19%)
  local copies, waits for them, and re-layouts  7.8 us (8%)
  matrix products  2.18 us (2%)
    all_to_all x1, waiting for transfers between devices, body(): all_tracers = lax.all_to_all(by_level, 'trc', 0, 0, tiled=True)  10.8 us
    ppermute x1, starting transfers between devices, body(): depth_north = lax.ppermute(depth_float, 'tile', down)  10.4 us
    all_to_all x1, waiting for transfers between devices, body(): fed = lax.all_to_all(fed, 'trc', 0, 0, tiled=True)  9.17 us
    all_to_all x1, starting transfers between devices, body(): own_parts = lax.all_to_all(province_part, 'tile', 0, 0, tiled=True)  8.33 us
    all_to_all x1, starting transfers between devices, body(): all_tracers = lax.all_to_all(by_level, 'trc', 0, 0, tiled=True)  7.1 us
    all_to_all x1, waiting for transfers between devices, body(): own_parts = lax.all_to_all(province_part, 'tile', 0, 0, tiled=True)  6.86 us
    ppermute x1, waiting for transfers between devices, body(): south = lax.ppermute(halo, 'tile', up).astype(jnp.float32)  5.59 us
    mul x1, other arithmetic, laplacian(): centre_wet * (extended_wet[:, 2:] * (extended[:, :, 2:] - centre) + exten...  4.64 us
  transfers between devices with their start and end apart: 7, of which 5 were waited for; matrix products, arithmetic and copies ran while one was open for 10% of the time, Pallas kernels for 0%

profile of v1, /device:TPU:2, one launch (start us, length us, event | category | flops | bytes accessed | tf_op | source)
XLA Modules:
  0.0 102.6 jit_solution(6434256033265274141)
XLA Ops:
  1.4 1.9 %collective-permute-start = (f32[2,1024]{1,0:T(2,128)S(1)}, f32[2,1024]{1,0:T(2,128)S(1)}, u32[]{:S(2)}, u32[]{:S(2)}) collective-permute-start(f32[2,1024]{1,0:T(2,128)S(1)} %convert_element_type.48), channel_id=1, source_target_pairs={{0,8},{8,16},{16,24},{24,32},{32,40},{40,48},{48,56},{56,64},{64,7... | collective-permute-start | bytes 24584 | tf_op jit(solution)/shard_map/ppermute | solution.py:47
  3.3 10.4 %collective-permute-start.1 = (f32[2,1024]{1,0:T(2,128)S(1)}, f32[2,1024]{1,0:T(2,128)S(1)}, u32[]{:S(2)}, u32[]{:S(2)}) collective-permute-start(f32[2,1024]{1,0:T(2,128)S(1)} %convert_element_type.48), channel_id=1, source_target_pairs={{8,0},{16,8},{24,16},{32,24},{40,32},{48,40},{56,48},{64,56},{72,6... | collective-permute-start | bytes 24584 | tf_op jit(solution)/shard_map/ppermute | solution.py:48
  15.2 1.0 convolution_bitcast_fusion
  16.2 1.3 %broadcast_multiply_fusion = f32[7,4,8,1024]{3,2,1,0:T(8,128)S(1)} fusion(f32[7,4,8,1024]{3,2,1,0:T(8,128)} %bitcast.32, f32[4,8,1024]{2,1,0:T(8,128)S(1)} %bitcast.31), kind=kLoop, calls=%fused_computation.53 | loop fusion | flops 229376 | bytes 1966080 | tf_op jit(solution)/shard_map/mul | solution.py:51
  18.3 1.0 fusion.26
  19.3 8.3 %all-to-all-start.2 = ((f32[64,1,7]{2,1,0:T(1,128)}), f32[64,1,7]{2,1,0:T(1,128)S(1)}, u32[]{:S(2)}, u32[]{:S(2)}) async-start(f32[64,1,7]{2,1,0:T(1,128)} %bitcast.6), calls=%async_computation.2 | async-start | bytes 65536 | tf_op jit(solution)/shard_map/all_to_all | solution.py:75
  29.3 6.9 %all-to-all-done.2 = f32[64,1,7]{2,1,0:T(1,128)S(1)} async-done(((f32[64,1,7]{2,1,0:T(1,128)}), f32[64,1,7]{2,1,0:T(1,128)S(1)}, u32[]{:S(2)}, u32[]{:S(2)}) %all-to-all-start.2) | async-done | bytes 1824 | tf_op jit(solution)/shard_map/all_to_all | solution.py:75
  36.2 7.1 %all-to-all-start = ((bf16[8,7,2048]{2,1,0:T(8,128)(2,1)}), bf16[8,7,2048]{2,1,0:T(8,128)(2,1)S(1)}, u32[]{:S(2)}, u32[]{:S(2)}) async-start(bf16[8,7,2048]{2,1,0:T(8,128)(2,1)} %copy.23), calls=%async_computation | async-start | bytes 524288 | tf_op jit(solution)/shard_map/all_to_all | solution.py:66
  44.4 10.8 %all-to-all-done = bf16[8,7,2048]{2,1,0:T(8,128)(2,1)S(1)} async-done(((bf16[8,7,2048]{2,1,0:T(8,128)(2,1)}), bf16[8,7,2048]{2,1,0:T(8,128)(2,1)S(1)}, u32[]{:S(2)}, u32[]{:S(2)}) %all-to-all-start) | async-done | bytes 229408 | tf_op jit(solution)/shard_map/all_to_all | solution.py:66
  56.3 4.0 %all-to-all-start.1 = ((f16[8,7,2048]{2,1,0:T(8,128)(2,1)}), f16[8,7,2048]{2,1,0:T(8,128)(2,1)}, u32[]{:S(2)}, u32[]{:S(2)}) async-start(f16[8,7,2048]{2,1,0:T(8,128)(2,1)} %reshape.60), calls=%async_computation.1 | async-start | bytes 524288 | tf_op jit(solution)/shard_map/all_to_all | solution.py:84
  60.4 0.9 pad_maximum_fusion.8
  61.7 9.2 %all-to-all-done.1 = f16[8,7,2048]{2,1,0:T(8,128)(2,1)} async-done(((f16[8,7,2048]{2,1,0:T(8,128)(2,1)}), f16[8,7,2048]{2,1,0:T(8,128)(2,1)}, u32[]{:S(2)}, u32[]{:S(2)}) %all-to-all-start.1) | async-done | bytes 229408 | tf_op jit(solution)/shard_map/all_to_all | solution.py:84
  70.9 1.1 %convert_multiply_fusion = f32[8,7,2048]{2,0,1:T(8,128)S(1)} fusion(f16[8,7,2048]{2,1,0:T(8,128)(2,1)} %all-to-all-done.1), kind=kLoop, calls=%fused_computation.50 | loop fusion | flops 229376 | bytes 688128 | tf_op jit(solution)/shard_map/mul | solution.py:85
  72.7 1.4 %fusion.24 = f32[7,15,2,1024]{3,2,1,0:T(2,128)S(1)} fusion(f32[7,8,2,1024]{3,2,1,0:T(2,128)S(1)} %bitcast_add_fusion, f32[7,8,2,1024]{3,2,1,0:T(2,128)S(1)} %get-tuple-element.12, f32[15,2,1024]{2,1,0:T(2,128)} %slice_multiply_fusion, f32[7]{0:T(128)} %param.19), kind=kLoop, calls=%fused_computation.43 | loop fusion | flops 1075200 | bytes 1900572 | tf_op jit(solution)/shard_map/mul | solution.py:92
  74.1 0.9 fusion.30
  75.0 1.9 %collective-permute-start.2 = (bf16[7,16,2,1024]{3,2,1,0:T(2,128)(2,1)S(1)}, bf16[7,16,2,1024]{3,2,1,0:T(2,128)(2,1)S(1)}, u32[]{:S(2)}, u32[]{:S(2)}) collective-permute-start(bf16[7,16,2,1024]{3,2,1,0:T(2,128)(2,1)S(1)} %get-tuple-element.2), channel_id=1, source_target_pairs={{8,0},{16,8},{24,16},{32,24},{40,32},{48,40},{56,48},{64,56},{72,6... | collective-permute-start | bytes 1376264 | tf_op jit(solution)/shard_map/ppermute | solution.py:99
  76.9 2.6 %collective-permute-start.3 = (bf16[7,16,2,1024]{3,2,1,0:T(2,128)(2,1)S(1)}, bf16[7,16,2,1024]{3,2,1,0:T(2,128)(2,1)S(1)}, u32[]{:S(2)}, u32[]{:S(2)}) collective-permute-start(bf16[7,16,2,1024]{3,2,1,0:T(2,128)(2,1)S(1)} %get-tuple-element.2), channel_id=1, source_target_pairs={{0,8},{8,16},{16,24},{24,32},{32,40},{40,48},{48,56},{56,64},{64,7... | collective-permute-start | bytes 1376264 | tf_op jit(solution)/shard_map/ppermute | solution.py:98
  79.9 3.0 %collective-permute-done.2 = bf16[7,16,2,1024]{3,2,1,0:T(2,128)(2,1)S(1)} collective-permute-done((bf16[7,16,2,1024]{3,2,1,0:T(2,128)(2,1)S(1)}, bf16[7,16,2,1024]{3,2,1,0:T(2,128)(2,1)S(1)}, u32[]{:S(2)}, u32[]{:S(2)}) %collective-permute-start.2) | collective-permute-done | bytes 458784 | tf_op jit(solution)/shard_map/ppermute | solution.py:99
  83.2 5.6 %collective-permute-done.3 = bf16[7,16,2,1024]{3,2,1,0:T(2,128)(2,1)S(1)} collective-permute-done((bf16[7,16,2,1024]{3,2,1,0:T(2,128)(2,1)S(1)}, bf16[7,16,2,1024]{3,2,1,0:T(2,128)(2,1)S(1)}, u32[]{:S(2)}, u32[]{:S(2)}) %collective-permute-start.3) | collective-permute-done | bytes 458784 | tf_op jit(solution)/shard_map/ppermute | solution.py:98
  89.2 1.2 %pad_maximum_fusion = f32[7,16,6,1024]{3,2,1,0:T(8,128)S(1)} fusion(f32[7,16,2,1024]{3,2,1,0:T(2,128)S(1)} %convert_element_type.51, f32[7,16,2,1024]{3,2,1,0:T(2,128)S(1)} %get-tuple-element.3, f32[7,16,2,1024]{3,2,1,0:T(2,128)S(1)} %convert_element_type.52), kind=kLoop, calls=%fused_computation | loop fusion | flops 1376256 | bytes 5505024 | tf_op jit(solution)/shard_map/concatenate | solution.py:100
  90.3 1.8 %fusion.32 = (f32[7,16,4,1023]{3,2,1,0:T(4,128)S(1)}, f32[7,16,4,1023]{3,2,1,0:T(4,128)S(1)}) fusion(f32[7,16,6,1024]{3,2,1,0:T(8,128)S(1)} %pad_maximum_fusion), kind=kLoop, calls=%fused_computation.68 | loop fusion | bytes 7332864 | tf_op jit(solution)/shard_map/jit(_roll_static)/slice | solution.py:11
  92.2 4.6 %fusion.7 = f32[7,16,4,1024]{3,2,1,0:T(4,128)S(1)} fusion(f32[7,16,2,1024]{3,2,1,0:T(2,128)S(1)} %convert_element_type.51, f32[7,16,2,1024]{3,2,1,0:T(2,128)S(1)} %get-tuple-element.3, f32[7,16,2,1024]{3,2,1,0:T(2,128)S(1)} %convert_element_type.52, f32[7,16,6,1024]{3,2,1,0:T(8,128)S(1)} %pad_maximum_fusion, f32[7,16,4,1023]{3,2,1,0:T(4,128)S(1)} %get-tuple-element.5, ...), kind=kLoop, calls=%fused_computation.11 | loop fusion | flops 9175040 | bytes 11399680 | tf_op jit(solution)/shard_map/mul | solution.py:20
  96.8 1.8 %fusion.33 = (f32[7,16,2,1023]{3,2,1,0:T(2,128)S(1)}, f32[7,16,2,1023]{3,2,1,0:T(2,128)S(1)}) fusion(f32[7,16,4,1024]{3,2,1,0:T(4,128)S(1)} %fusion.7), kind=kLoop, calls=%fused_computation.69 | loop fusion | bytes 3666432 | tf_op jit(solution)/shard_map/jit(_roll_static)/slice | solution.py:10
  98.8 3.8 %multiply_subtract_fusion = f32[7,16,2,1024]{3,2,1,0:T(2,128)} fusion(f32[7,16,2,1024]{3,2,1,0:T(2,128)S(1)} %get-tuple-element.3, f32[7,16,2,1023]{3,2,1,0:T(2,128)S(1)} %get-tuple-element.7, f32[7,16,2,1]{3,2,1,0:T(2,128)S(1)} %get-tuple-element.9, f32[7,16,2,1]{3,2,1,0:T(2,128)S(1)} %get-tuple-element.8, f32[7,16,2,1023]{3,2,1,0:T(2,128)S(1)} %get-tuple-element.6, ...), kind=kLoop, calls=%fused_computation.40 | loop fusion | flops 3670016 | bytes 7077916 | tf_op jit(solution)/shard_map/sub | solution.py:106
  (44 shorter events, 9.3 us)
Async XLA Ops:
  0.6 54.6 %copy-start = (bf16[56,56]{1,0:T(8,128)(2,1)S(1)}, bf16[56,56]{1,0:T(8,128)(2,1)}, u32[]{:S(2)}) copy-start(bf16[56,56]{1,0:T(8,128)(2,1)} %param.15) | copy-start | bytes 18820
  0.6 16.8 %copy-start.2 = (bf16[7,8,2,1024]{3,2,1,0:T(2,128)(2,1)S(1)}, bf16[7,8,2,1024]{3,2,1,0:T(2,128)(2,1)}, u32[]{:S(2)}) copy-start(bf16[7,8,2,1024]{3,2,1,0:T(2,128)(2,1)} %param.11) | copy-start | bytes 688132
  0.7 16.8 %copy-start.3 = (f32[8,2,1024]{2,1,0:T(2,128)S(1)}, f32[8,2,1024]{2,1,0:T(2,128)}, u32[]{:S(2)}) copy-start(f32[8,2,1024]{2,1,0:T(2,128)} %param.12) | copy-start | bytes 196612
  0.7 16.8 %copy-start.4 = (f32[7]{0:T(128)S(1)}, f32[7]{0:T(128)}, u32[]{:S(2)}) copy-start(f32[7]{0:T(128)} %param.17) | copy-start | bytes 88
  1.4 42.4 %collective-permute-start = (f32[2,1024]{1,0:T(2,128)S(1)}, f32[2,1024]{1,0:T(2,128)S(1)}, u32[]{:S(2)}, u32[]{:S(2)}) collective-permute-start(f32[2,1024]{1,0:T(2,128)S(1)} %convert_element_type.48), channel_id=1, source_target_pairs={{0,8},{8,16},{16,24},{24,32},{32,40},{40,48},{48,56},{56,64},{64,7... | collective-permute-start | bytes 24584 | tf_op jit(solution)/shard_map/ppermute | solution.py:47
  3.3 40.5 %collective-permute-start.1 = (f32[2,1024]{1,0:T(2,128)S(1)}, f32[2,1024]{1,0:T(2,128)S(1)}, u32[]{:S(2)}, u32[]{:S(2)}) collective-permute-start(f32[2,1024]{1,0:T(2,128)S(1)} %convert_element_type.48), channel_id=1, source_target_pairs={{8,0},{16,8},{24,16},{32,24},{40,32},{48,40},{56,48},{64,56},{72,6... | collective-permute-start | bytes 24584 | tf_op jit(solution)/shard_map/ppermute | solution.py:48
  19.3 16.9 %all-to-all-start.2 = ((f32[64,1,7]{2,1,0:T(1,128)}), f32[64,1,7]{2,1,0:T(1,128)S(1)}, u32[]{:S(2)}, u32[]{:S(2)}) async-start(f32[64,1,7]{2,1,0:T(1,128)} %bitcast.6), calls=%async_computation.2 | async-start | bytes 65536 | tf_op jit(solution)/shard_map/all_to_all | solution.py:75
  36.2 19.0 %all-to-all-start = ((bf16[8,7,2048]{2,1,0:T(8,128)(2,1)}), bf16[8,7,2048]{2,1,0:T(8,128)(2,1)S(1)}, u32[]{:S(2)}, u32[]{:S(2)}) async-start(bf16[8,7,2048]{2,1,0:T(8,128)(2,1)} %copy.23), calls=%async_computation | async-start | bytes 524288 | tf_op jit(solution)/shard_map/all_to_all | solution.py:66
  56.3 14.5 %all-to-all-start.1 = ((f16[8,7,2048]{2,1,0:T(8,128)(2,1)}), f16[8,7,2048]{2,1,0:T(8,128)(2,1)}, u32[]{:S(2)}, u32[]{:S(2)}) async-start(f16[8,7,2048]{2,1,0:T(8,128)(2,1)} %reshape.60), calls=%async_computation.1 | async-start | bytes 524288 | tf_op jit(solution)/shard_map/all_to_all | solution.py:84
  75.0 7.9 %collective-permute-start.2 = (bf16[7,16,2,1024]{3,2,1,0:T(2,128)(2,1)S(1)}, bf16[7,16,2,1024]{3,2,1,0:T(2,128)(2,1)S(1)}, u32[]{:S(2)}, u32[]{:S(2)}) collective-permute-start(bf16[7,16,2,1024]{3,2,1,0:T(2,128)(2,1)S(1)} %get-tuple-element.2), channel_id=1, source_target_pairs={{8,0},{16,8},{24,16},{32,24},{40,32},{48,40},{56,48},{64,56},{72,6... | collective-permute-start | bytes 1376264 | tf_op jit(solution)/shard_map/ppermute | solution.py:99
  76.9 11.9 %collective-permute-start.3 = (bf16[7,16,2,1024]{3,2,1,0:T(2,128)(2,1)S(1)}, bf16[7,16,2,1024]{3,2,1,0:T(2,128)(2,1)S(1)}, u32[]{:S(2)}, u32[]{:S(2)}) collective-permute-start(bf16[7,16,2,1024]{3,2,1,0:T(2,128)(2,1)S(1)} %get-tuple-element.2), channel_id=1, source_target_pairs={{0,8},{8,16},{16,24},{24,32},{32,40},{40,48},{48,56},{56,64},{64,7... | collective-permute-start | bytes 1376264 | tf_op jit(solution)/shard_map/ppermute | solution.py:98
  96.8 2.0 %copy-start.1 = (f32[16,2,1024]{2,1,0:T(2,128)S(1)}, f32[16,2,1024]{2,1,0:T(2,128)}, u32[]{:S(2)}) copy-start(f32[16,2,1024]{2,1,0:T(2,128)} %get-tuple-element.30) | copy-start | bytes 393220
  96.8 2.0 %copy-start.5 = (f32[7]{0:T(128)S(1)}, f32[7]{0:T(128)}, u32[]{:S(2)}) copy-start(f32[7]{0:T(128)} %param.18) | copy-start | bytes 88

commit v2 on v1

v2 whole, which is shorter than its diff:
```python
import jax
import jax.numpy as jnp
from jax import lax
from jax.experimental import pallas as pl
from jax.experimental.pallas import tpu as pltpu
from jax.sharding import PartitionSpec as P

SCALE = 256.0
LANES = 128
ROWS = 2
BF16 = jnp.bfloat16
F32 = jnp.float32
VMEM = pl.BlockSpec(memory_space=pltpu.VMEM)
SMEM = pl.BlockSpec(memory_space=pltpu.SMEM)
PARAMS = pltpu.CompilerParams(vmem_limit_bytes=40 * 1024 * 1024)


def row(ref, *at):
    *lead, r = at
    blocks = ref.shape[-2] // ROWS
    return ref[(*lead, pl.ds(r, blocks, stride=ROWS), slice(None))]


def wet_at(depth, level):
    return (depth > level).astype(F32)


def weighted_kernel(cot_ref, nutrient_ref, depth_ref, region_ref, rates_ref, half_ref, out_ref, table_ref):
    own, sunlit = out_ref.shape[1], out_ref.shape[0]
    blocks = cot_ref.shape[2] // ROWS
    provinces = rates_ref.shape[1]
    table_ref[...] = jnp.zeros(table_ref.shape, F32)
    table_ref[0:own, 0:provinces] = rates_ref[...]
    depth = [row(depth_ref, r) for r in range(ROWS)]
    region = [row(region_ref, r) for r in range(ROWS)]
    for t in range(own):
        line = jnp.broadcast_to(table_ref[t : t + 1, :], (blocks, LANES))
        rates = [jnp.take_along_axis(line, region[r], axis=1) for r in range(ROWS)]
        half = half_ref[t]
        for k in range(sunlit):
            rows = []
            for r in range(ROWS):
                food = row(nutrient_ref, k, r)
                limiter = food / (food + half)
                grad = row(cot_ref, t, k, r) * wet_at(depth[r], k)
                rows.append(rates[r] * limiter * grad)
            out_ref[k, t] = jnp.concatenate(rows, axis=0).astype(BF16)


def province_kernel(cot_ref, uptake_ref, nutrient_ref, depth_ref, region_ref, half_ref, out_ref, hot_ref, term_ref, parts_ref):
    provinces, own = out_ref.shape
    sunlit = nutrient_ref.shape[0]
    lines = depth_ref.shape[0]
    depth = depth_ref[...]
    for t in range(own):
        total = jnp.zeros((lines, LANES), F32)
        for k in range(sunlit):
            food = nutrient_ref[k]
            limiter = food / (food + half_ref[t])
            grad = cot_ref[t, k] * wet_at(depth, k)
            total = total + limiter * uptake_ref[t, k].astype(F32) * grad
        term_ref[pl.ds(t, lines, stride=8), :] = total
    ids = lax.broadcasted_iota(jnp.int32, (provinces, LANES), 0)
    for s in range(lines):
        line = jnp.broadcast_to(region_ref[s : s + 1, :], (provinces, LANES))
        hot_ref[:, s * LANES : (s + 1) * LANES] = (line == ids).astype(F32).astype(BF16)
        term = term_ref[s * 8 : (s + 1) * 8, :]
        high = term.astype(BF16).astype(F32)
        both = jnp.concatenate([high, term - high], axis=0)
        parts_ref[:, s * LANES : (s + 1) * LANES] = both.astype(BF16)
    sums = lax.dot_general(hot_ref[...], parts_ref[...], (((1,), (1,)), ((), ())), preferred_element_type=F32)
    out_ref[...] = sums[:, 0:own] + sums[:, 8 : 8 + own]


def feed_kernel(matrix_ref, weighted_ref, out_ref, wide_ref, fed_ref):
    tracers, lines = weighted_ref.shape[0], weighted_ref.shape[1]
    matrix = matrix_ref[...].astype(F32).T.astype(BF16)
    for t in range(tracers):
        wide_ref[t * lines : (t + 1) * lines, :] = weighted_ref[t].astype(F32)
    for s in range(0, lines, 2):
        cells = [wide_ref[pl.ds(s + i, tracers, stride=lines), :].astype(BF16) for i in range(2)]
        fed = jnp.dot(matrix, jnp.concatenate(cells, axis=1), preferred_element_type=F32) * SCALE
        for i in range(2):
            fed_ref[pl.ds(s + i, tracers, stride=lines), :] = fed[:, i * LANES : (i + 1) * LANES]
    for t in range(tracers):
        out_ref[t] = fed_ref[t * lines : (t + 1) * lines, :]


def column_kernel(cot_ref, fed_ref, depth_ref, sinking_ref, col_ref, halo_ref):
    own, levels = cot_ref.shape[0], cot_ref.shape[1]
    sunlit = fed_ref.shape[0]
    blocks = depth_ref.shape[0] // ROWS
    depth = [row(depth_ref, r) for r in range(ROWS)]
    halo_ref[own * levels] = jnp.concatenate(depth, axis=0).astype(F32).astype(BF16)

    def middle(t, k, r):
        wet = wet_at(depth[r], k)
        grad = row(cot_ref, t, k, r) * wet
        if k < sunlit:
            grad = grad + wet * (fed_ref[k, t, r * blocks : (r + 1) * blocks, :] * (1.0 / SCALE))
        return grad

    for t in range(own):
        sink = sinking_ref[t]
        below = [middle(t, levels - 1, r) for r in range(ROWS)]
        for k in range(levels - 1, -1, -1):
            rows = []
            if k == levels - 1:
                rows = below
            else:
                here = [middle(t, k, r) for r in range(ROWS)]
                for r in range(ROWS):
                    coupling = sink * wet_at(depth[r], k + 1)
                    rows.append(here[r] + coupling * (below[r] - here[r]))
                below = here
            both = jnp.concatenate(rows, axis=0)
            col_ref[t, k] = both
            halo_ref[t * levels + k] = both.astype(BF16)


def mixing_kernel(col_ref, south_ref, north_ref, depth_ref, mixing_ref, out_ref):
    own, levels = col_ref.shape[0], col_ref.shape[1]
    blocks = col_ref.shape[2] // ROWS
    lane_ids = lax.broadcasted_iota(jnp.int32, (blocks, LANES), 1)
    last_lane, first_lane = lane_ids == LANES - 1, lane_ids == 0

    def east(v):
        turned = pltpu.roll(v, LANES - 1, 1)
        return jnp.where(last_lane, pltpu.roll(turned, blocks - 1, 0), turned)

    def west(v):
        turned = pltpu.roll(v, 1, 1)
        return jnp.where(first_lane, pltpu.roll(turned, 1, 0), turned)

    def split(v):
        wide = v.astype(F32)
        return [wide[r * blocks : (r + 1) * blocks] for r in range(ROWS)]

    def laplacian(rows, edges_y, edges_x, lo, hi):
        flux = [edges_y[i] * (rows[i + 1] - rows[i]) for i in range(lo - 1, hi)]
        out = []
        for n, i in enumerate(range(lo, hi)):
            zonal = edges_x[i] * (east(rows[i]) - rows[i])
            out.append((flux[n + 1] - flux[n]) + (zonal - west(zonal)))
        return out

    own_depth = [row(depth_ref, r).astype(F32) for r in range(ROWS)]
    depths = split(south_ref[own * levels]) + own_depth + split(north_ref[own * levels])

    @pl.loop(0, levels)
    def _(k):
        at = lax.convert_element_type(k, F32)
        wet = [wet_at(d, at) for d in depths]
        edges_y = [wet[i] * wet[i + 1] for i in range(5)]
        edges_x = [None] + [wet[i] * east(wet[i]) for i in range(1, 5)]
        for t in range(own):
            here = split(col_ref[t, k])
            rows = split(south_ref[t * levels + k]) + here + split(north_ref[t * levels + k])
            once = laplacian(rows, edges_y, edges_x, 1, 5)
            twice = laplacian([None] + once, edges_y, edges_x, 2, 4)
            for r in range(ROWS):
                out_ref[t, k, pl.ds(r, blocks, stride=ROWS), :] = here[r] - mixing_ref[t] * twice[r]


def dense(band):
    *lead, rows, zonal = band.shape
    cut = band.reshape(*lead, rows, zonal // LANES, LANES)
    return jnp.swapaxes(cut, -3, -2).reshape(*lead, rows * zonal // LANES, LANES)


def undense(lines, rows):
    *lead, count, _ = lines.shape
    cut = lines.reshape(*lead, count // rows, rows, LANES)
    return jnp.swapaxes(cut, -3, -2).reshape(*lead, rows, count * LANES // rows)


def call(kernel, shapes, specs, scratch=()):
    return pl.pallas_call(
        kernel,
        out_shape=shapes,
        in_specs=specs,
        out_specs=jax.tree.map(lambda _: VMEM, shapes),
        scratch_shapes=scratch,
        compiler_params=PARAMS,
    )


def body(
    cotangent,
    uptake_rate,
    nutrient,
    depth_levels,
    region_ids,
    uptake_matrix,
    province_rates,
    half_saturation,
    biharmonic,
    sinking,
):
    own, levels, band_rows, zonal = cotangent.shape
    sunlit = uptake_rate.shape[1]
    columns = band_rows * zonal
    lines = columns // LANES
    provinces = province_rates.shape[0]
    tracers = uptake_matrix.shape[0]
    tiles = lax.axis_size("tile")
    up = [(i, i + 1) for i in range(tiles - 1)]
    down = [(i + 1, i) for i in range(tiles - 1)]
    shape = jax.ShapeDtypeStruct
    cot, uptake, nutrient = dense(cotangent), dense(uptake_rate), dense(nutrient)
    depth, region = dense(depth_levels), dense(region_ids)

    weighted = call(
        weighted_kernel,
        shape((sunlit, own, lines, LANES), BF16),
        [VMEM, VMEM, VMEM, VMEM, VMEM, SMEM],
        [pltpu.VMEM((8, LANES), F32)],
    )(cot, nutrient, depth, region, province_rates.T, half_saturation)
    all_tracers = lax.all_to_all(weighted, "trc", 0, 0, tiled=True).reshape(tracers, lines, LANES)
    province_part = call(
        province_kernel,
        shape((provinces, own), F32),
        [VMEM, VMEM, VMEM, VMEM, VMEM, SMEM],
        [
            pltpu.VMEM((provinces, columns), BF16),
            pltpu.VMEM((lines * 8, LANES), F32),
            pltpu.VMEM((16, columns), BF16),
        ],
    )(cot, uptake, nutrient, depth, region, half_saturation)
    own_parts = lax.all_to_all(province_part, "tile", 0, 0, tiled=True)
    rate_grad = jnp.sum(own_parts, axis=0, keepdims=True) * (1.0 / (sunlit * columns))
    fed = call(
        feed_kernel,
        shape((tracers, lines, LANES), F32),
        [VMEM, VMEM],
        [pltpu.VMEM((tracers * lines, LANES), F32), pltpu.VMEM((tracers * lines, LANES), F32)],
    )(uptake_matrix, all_tracers)
    fed = fed.astype(jnp.float16).reshape(sunlit, own, lines, LANES)
    fed = lax.all_to_all(fed, "trc", 0, 0, tiled=True).astype(F32)
    col, halo = call(
        column_kernel,
        (shape((own, levels, lines, LANES), F32), shape((own * levels + 1, lines, LANES), BF16)),
        [VMEM, VMEM, VMEM, SMEM],
    )(cot, fed, depth, sinking)
    south = lax.ppermute(halo, "tile", up)
    north = lax.ppermute(halo, "tile", down)
    tracer_grad = call(
        mixing_kernel,
        shape((own, levels, lines, LANES), F32),
        [VMEM, VMEM, VMEM, VMEM, SMEM],
    )(col, south, north, depth, biharmonic)
    return (undense(tracer_grad, band_rows), rate_grad)


def solution(mesh):
    return jax.shard_map(
        body,
        mesh=mesh,
        in_specs=(
            P("trc", None, "tile", None),
            P("trc", None, "tile", None),
            P(None, "tile", None),
            P("tile", None),
            P("tile", None),
            P(),
            P(None, "trc"),
            P("trc"),
            P("trc"),
            P("trc"),
        ),
        out_specs=(P("trc", None, "tile", None), P("tile", "trc")),
        check_vma=False,
    )
```

time: 103 us -> 77.8 us (0.76)
  the two profiles are of different devices: /device:TPU:2 before, /device:TPU:1 now
where the time goes in v2:
time: 77.8 us; the launch traced here: 77.3 us
  blocking collectives  51.4 us (66%)
  starting transfers between devices  10 us (13%)
  Pallas kernels  9.13 us (12%)
  local copies, waits for them, and re-layouts  5.36 us (7%)
    all_to_all x1, blocking collectives, body(): own_parts = lax.all_to_all(province_part, 'tile', 0, 0, tiled=True)  23.4 us
    all_to_all x1, blocking collectives, body(): lax.all_to_all(weighted, 'trc', 0, 0, tiled=True)  16.3 us
    all_to_all x1, blocking collectives, body(): fed = lax.all_to_all(fed, 'trc', 0, 0, tiled=True).astype(F32)  11.7 us
    ppermute x1, starting transfers between devices, body(): south = lax.ppermute(halo, 'tile', up)  8.12 us
    pallas_call x1, Pallas kernels, body(): call(mixing_kernel, shape((own, levels, lines, LANES), F32), [VMEM, VMEM,...  6.37 us
    unnamed x26, local copies, waits for them, and re-layouts  5.36 us
    ppermute x1, starting transfers between devices, body(): north = lax.ppermute(halo, 'tile', down)  1.92 us
  transfers between devices with their start and end apart: 2, of which 0 were waited for; matrix products, arithmetic and copies ran while one was open for 1% of the time, Pallas kernels for 1%

profile of v2, /device:TPU:1, one launch (start us, length us, event | category | flops | bytes accessed | tf_op | source)
XLA Modules:
  0.0 77.3 jit_solution(10648181569703892710)
XLA Ops:
  0.7 0.7 copy-done.5
  1.3 1.2 %copy-done = f32[7,16,2,1024]{3,2,1,0:T(2,128)S(1)} copy-done((f32[7,16,2,1024]{3,2,1,0:T(2,128)S(1)}, f32[7,16,2,1024]{3,2,1,0:T(2,128)}, u32[]{:S(2)}) %copy-start) | copy-done | bytes 917528
  2.5 0.8 %copy-done.2 = f32[8,2,1024]{2,1,0:T(2,128)S(1)} copy-done((f32[8,2,1024]{2,1,0:T(2,128)S(1)}, f32[8,2,1024]{2,1,0:T(2,128)}, u32[]{:S(2)}) %copy-start.2) | copy-done | bytes 65560
  3.4 0.7 copy-done.6
  4.1 0.7 copy-done.9
  4.7 0.7 shard_map.113
  5.4 0.0 copy-start.8
  5.4 16.3 %all_to_all.19 = bf16[8,7,16,128]{3,2,1,0:T(8,128)(2,1)S(1)} all-to-all(bf16[8,7,16,128]{3,2,1,0:T(8,128)(2,1)S(1)} %shard_map.113), channel_id=1, replica_groups=mesh['tile'=64,'trc'=8] {'trc'}, dimensions={0} | all-to-all | bytes 458752 | tf_op jit(solution)/shard_map/all_to_all | solution.py:219
  21.8 0.4 shard_map.114
  22.1 0.0 copy-start.1
  22.2 11.7 %all_to_all.20 = f16[8,7,16,128]{3,2,1,0:T(8,128)(2,1)S(1)} all-to-all(f16[8,7,16,128]{3,2,1,0:T(8,128)(2,1)S(1)} %bitcast.54), channel_id=1, replica_groups=mesh['tile'=64,'trc'=8] {'trc'}, dimensions={0} | all-to-all | bytes 458752 | tf_op jit(solution)/shard_map/all_to_all | solution.py:239
  33.9 0.6 copy-done.11
  34.5 0.8 shard_map.115
  35.3 8.1 %collective-permute-start = (bf16[113,16,128]{2,1,0:T(8,128)(2,1)S(1)}, bf16[113,16,128]{2,1,0:T(8,128)(2,1)S(1)}, u32[]{:S(2)}, u32[]{:S(2)}) collective-permute-start(bf16[113,16,128]{2,1,0:T(8,128)(2,1)S(1)} %get-tuple-element.5), channel_id=1, source_target_pairs={{0,8},{8,16},{16,24},{24,32},{32,40},{40,48},{48,56},{56,64},{64,7... | collective-permute-start | bytes 1388552 | tf_op jit(solution)/shard_map/ppermute | solution.py:245
  43.4 1.9 %collective-permute-start.1 = (bf16[113,16,128]{2,1,0:T(8,128)(2,1)S(1)}, bf16[113,16,128]{2,1,0:T(8,128)(2,1)S(1)}, u32[]{:S(2)}, u32[]{:S(2)}) collective-permute-start(bf16[113,16,128]{2,1,0:T(8,128)(2,1)S(1)} %get-tuple-element.5), channel_id=1, source_target_pairs={{8,0},{16,8},{24,16},{32,24},{40,32},{48,40},{56,48},{64,56},{72,6... | collective-permute-start | bytes 1388552 | tf_op jit(solution)/shard_map/ppermute | solution.py:246
  45.3 0.0 copy-done.3
  45.4 1.0 %shard_map.117 = f32[64,7]{1,0:T(8,128)S(1)} custom-call(f32[7,16,16,128]{3,2,1,0:T(8,128)S(1)} %bitcast.40, bf16[7,8,16,128]{3,2,1,0:T(8,128)(2,1)S(1)} %bitcast.44, f32[8,16,128]{2,1,0:T(8,128)S(1)} %bitcast.43, s32[16,128]{1,0:T(8,128)S(1)} %bitcast.47, s32[16,128]{1,0:T(8,128)S(1)} %bitcast.51, f32[7]{0:T(128)S(1)} %copy-done.10), custom_call_target="tpu_custom_call" | custom-call | tf_op jit(solution)/shard_map/pallas_call | solution.py:220
  46.4 23.4 %all_to_all.21 = f32[64,1,7]{2,1,0:T(1,128)S(1)} all-to-all(f32[64,1,7]{2,1,0:T(1,128)S(1)} %bitcast.49), channel_id=1, replica_groups=mesh['tile'=64,'trc'=8] {'tile'}, dimensions={0} | all-to-all | bytes 3584 | tf_op jit(solution)/shard_map/all_to_all | solution.py:230
  69.7 0.1 reduce_sum.9
  69.8 0.5 multiply_bitcast_fusion
  70.3 0.0 collective-permute-done.south_ref
  70.3 0.0 collective-permute-done.1.north_ref
  70.3 0.6 copy-done.12
  71.0 6.4 %shard_map.116 = f32[7,16,16,128]{3,2,1,0:T(8,128)} custom-call(f32[7,16,16,128]{3,2,1,0:T(8,128)S(1)} %get-tuple-element.4.col_ref, bf16[113,16,128]{2,1,0:T(8,128)(2,1)S(1)} %collective-permute-done.south_ref, bf16[113,16,128]{2,1,0:T(8,128)(2,1)S(1)} %collective-permute-done.1.north_ref, s32[16,128]{1,0:T(8,128)S(1)} %bitcast.48, f32[7]{0:T(128)S(1)} %copy-done.12), custom_call_target="tpu_custom_call" | custom-call | tf_op jit(solution)/shard_map/pallas_call | solution.py:247
  (18 shorter events, 0.1 us)
Async XLA Ops:
  0.6 0.7 copy-start.5
  0.6 0.7 copy-start.10
  1.3 1.2 %copy-start = (f32[7,16,2,1024]{3,2,1,0:T(2,128)S(1)}, f32[7,16,2,1024]{3,2,1,0:T(2,128)}, u32[]{:S(2)}) copy-start(f32[7,16,2,1024]{3,2,1,0:T(2,128)} %param.10) | copy-start | bytes 2752516
  2.5 0.8 %copy-start.2 = (f32[8,2,1024]{2,1,0:T(2,128)S(1)}, f32[8,2,1024]{2,1,0:T(2,128)}, u32[]{:S(2)}) copy-start(f32[8,2,1024]{2,1,0:T(2,128)} %param.12) | copy-start | bytes 196612
  3.4 0.7 copy-start.6
  4.0 0.7 copy-start.9
  5.4 16.3 %copy-start.8 = (bf16[56,56]{1,0:T(8,128)(2,1)S(1)}, bf16[56,56]{1,0:T(8,128)(2,1)}, u32[]{:S(2)}) copy-start(bf16[56,56]{1,0:T(8,128)(2,1)} %matrix_ref.1) | copy-start | bytes 18820
  22.1 11.8 %copy-start.1 = (f32[7,16,2,1024]{3,2,1,0:T(2,128)S(1)}, f32[7,16,2,1024]{3,2,1,0:T(2,128)}, u32[]{:S(2)}) copy-start(f32[7,16,2,1024]{3,2,1,0:T(2,128)} %param.10) | copy-start | bytes 2752516
  33.9 0.7 copy-start.11
  34.5 10.8 %copy-start.3 = (f32[8,2,1024]{2,1,0:T(2,128)S(1)}, f32[8,2,1024]{2,1,0:T(2,128)}, u32[]{:S(2)}) copy-start(f32[8,2,1024]{2,1,0:T(2,128)} %param.12) | copy-start | bytes 196612
  34.5 10.8 %copy-start.4 = (bf16[7,8,2,1024]{3,2,1,0:T(2,128)(2,1)S(1)}, bf16[7,8,2,1024]{3,2,1,0:T(2,128)(2,1)}, u32[]{:S(2)}) copy-start(bf16[7,8,2,1024]{3,2,1,0:T(2,128)(2,1)} %param.11) | copy-start | bytes 688132
  34.5 10.9 %copy-start.7 = (s32[2,1024]{1,0:T(2,128)S(1)}, s32[2,1024]{1,0:T(2,128)}, u32[]{:S(2)}) copy-start(s32[2,1024]{1,0:T(2,128)} %param.14) | copy-start | bytes 24580
  35.3 35.0 %collective-permute-start = (bf16[113,16,128]{2,1,0:T(8,128)(2,1)S(1)}, bf16[113,16,128]{2,1,0:T(8,128)(2,1)S(1)}, u32[]{:S(2)}, u32[]{:S(2)}) collective-permute-start(bf16[113,16,128]{2,1,0:T(8,128)(2,1)S(1)} %get-tuple-element.5), channel_id=1, source_target_pairs={{0,8},{8,16},{16,24},{24,32},{32,40},{40,48},{48,56},{56,64},{64,7... | collective-permute-start | bytes 1388552 | tf_op jit(solution)/shard_map/ppermute | solution.py:245
  43.4 26.9 %collective-permute-start.1 = (bf16[113,16,128]{2,1,0:T(8,128)(2,1)S(1)}, bf16[113,16,128]{2,1,0:T(8,128)(2,1)S(1)}, u32[]{:S(2)}, u32[]{:S(2)}) collective-permute-start(bf16[113,16,128]{2,1,0:T(8,128)(2,1)S(1)} %get-tuple-element.5), channel_id=1, source_target_pairs={{8,0},{16,8},{24,16},{32,24},{40,32},{48,40},{56,48},{64,56},{72,6... | collective-permute-start | bytes 1388552 | tf_op jit(solution)/shard_map/ppermute | solution.py:246
  70.3 0.7 copy-start.12

commit v3 on v2

v3 whole, which is shorter than its diff:
```python
import jax
import jax.numpy as jnp
from jax import lax
from jax.experimental import pallas as pl
from jax.experimental.pallas import tpu as pltpu
from jax.sharding import PartitionSpec as P

SCALE = 256.0
LANES = 128
ROWS = 2
SUB = 8
BF16 = jnp.bfloat16
F32 = jnp.float32
VMEM = pl.BlockSpec(memory_space=pltpu.VMEM)
HBM = pl.BlockSpec(memory_space=pltpu.HBM)
PARAMS = pltpu.CompilerParams(vmem_limit_bytes=40 * 1024 * 1024)


def row(ref, *at):
    *lead, r = at
    blocks = ref.shape[-2] // ROWS
    return ref[(*lead, pl.ds(r, blocks, stride=ROWS), slice(None))]


def wet_at(depth, level):
    return (depth > level).astype(F32)


def weighted_kernel(
    cot_hbm, nutrient_hbm, depth_hbm, region_hbm, rates_hbm, half_hbm, sinking_hbm, mixing_hbm,
    out_ref, params_ref,
    cot_ref, nutrient_ref, depth_ref, region_ref, rates_ref, half_ref, sinking_ref, mixing_ref, sems,
):
    own, sunlit = out_ref.shape[1], out_ref.shape[0]
    blocks = cot_ref.shape[2] // ROWS
    pairs = [
        (depth_hbm, depth_ref), (region_hbm, region_ref), (rates_hbm, rates_ref), (nutrient_hbm, nutrient_ref),
        (half_hbm, half_ref), (sinking_hbm, sinking_ref), (mixing_hbm, mixing_ref),
    ]
    pairs += [(cot_hbm.at[t, 0:sunlit], cot_ref.at[t]) for t in range(own)]
    copies = [pltpu.make_async_copy(here, there, sems.at[n]) for n, (here, there) in enumerate(pairs)]
    for copy in copies:
        copy.start()
    for copy in copies[: len(pairs) - own]:
        copy.wait()
    depth = [row(depth_ref, r) for r in range(ROWS)]
    region = [row(region_ref, r) for r in range(ROWS)]
    rest = jnp.zeros((1, LANES - rates_ref.shape[1]), F32)
    for t in range(own):
        line = jnp.concatenate([rates_ref[t : t + 1, :], rest], axis=1)
        line = jnp.broadcast_to(line, (blocks, LANES))
        rates = [jnp.take_along_axis(line, region[r], axis=1) for r in range(ROWS)]
        half = half_ref[t]
        for n, ref in enumerate((half_ref, sinking_ref, mixing_ref)):
            params_ref[n * SUB + t : n * SUB + t + 1, :] = jnp.full((1, LANES), ref[t], F32)
        copies[len(pairs) - own + t].wait()
        for k in range(sunlit):
            rows = []
            for r in range(ROWS):
                food = row(nutrient_ref, k, r)
                limiter = food / (food + half)
                grad = row(cot_ref, t, k, r) * wet_at(depth[r], k)
                rows.append(rates[r] * limiter * grad)
            out_ref[k, t] = jnp.concatenate(rows, axis=0).astype(BF16)


def province_kernel(cot_ref, uptake_ref, nutrient_ref, depth_ref, region_ref, params_ref, out_ref, hot_ref, term_ref, parts_ref):
    provinces, own = out_ref.shape
    sunlit = nutrient_ref.shape[0]
    lines = depth_ref.shape[0]
    depth = depth_ref[...]
    term_ref[...] = jnp.zeros(term_ref.shape, F32)
    for t in range(own):
        half = jnp.broadcast_to(params_ref[t : t + 1, :], (lines, LANES))
        total = jnp.zeros((lines, LANES), F32)
        for k in range(sunlit):
            food = nutrient_ref[k]
            limiter = food / (food + half)
            grad = cot_ref[t, k] * wet_at(depth, k)
            total = total + limiter * uptake_ref[t, k].astype(F32) * grad
        term_ref[pl.ds(t, lines, stride=8), :] = total
    ids = lax.broadcasted_iota(jnp.int32, (provinces, LANES), 0)
    for s in range(lines):
        line = jnp.broadcast_to(region_ref[s : s + 1, :], (provinces, LANES))
        hot_ref[:, s * LANES : (s + 1) * LANES] = (line == ids).astype(F32).astype(BF16)
        term = term_ref[s * 8 : (s + 1) * 8, :]
        high = term.astype(BF16).astype(F32)
        both = jnp.concatenate([high, term - high], axis=0)
        parts_ref[:, s * LANES : (s + 1) * LANES] = both.astype(BF16)
    sums = lax.dot_general(hot_ref[...], parts_ref[...], (((1,), (1,)), ((), ())), preferred_element_type=F32)
    out_ref[...] = sums[:, 0:own] + sums[:, 8 : 8 + own]


def feed_kernel(matrix_ref, weighted_ref, out_ref, wide_ref, fed_ref):
    tracers, lines = weighted_ref.shape[0], weighted_ref.shape[1]
    matrix = matrix_ref[...].astype(F32).T.astype(BF16)
    for t in range(tracers):
        wide_ref[t * lines : (t + 1) * lines, :] = weighted_ref[t].astype(F32)
    for s in range(0, lines, 2):
        cells = [wide_ref[pl.ds(s + i, tracers, stride=lines), :].astype(BF16) for i in range(2)]
        fed = jnp.dot(matrix, jnp.concatenate(cells, axis=1), preferred_element_type=F32) * SCALE
        for i in range(2):
            fed_ref[pl.ds(s + i, tracers, stride=lines), :] = fed[:, i * LANES : (i + 1) * LANES]
    for t in range(tracers):
        out_ref[t] = fed_ref[t * lines : (t + 1) * lines, :]


def column_kernel(cot_ref, fed_ref, depth_ref, params_ref, col_ref, halo_ref):
    lines = depth_ref.shape[0]
    blocks = lines // ROWS
    own = col_ref.shape[0] // lines
    levels = col_ref.shape[1]
    blocks_of = [depth_ref[b * ROWS + r : b * ROWS + r + 1, :] for r in range(ROWS) for b in range(blocks)]
    halo_ref[own * lines] = jnp.concatenate(blocks_of, axis=0).astype(F32).astype(BF16)
    ids = lax.broadcasted_iota(jnp.int32, (SUB, LANES), 0)
    bottom = ids == SUB - 1
    for n in range(lines):
        r, b = n // blocks, n % blocks
        depth = jnp.broadcast_to(blocks_of[n], (SUB, LANES))
        top_wet, low_wet = (depth > ids).astype(F32), (depth > ids + SUB).astype(F32)
        top_next = (depth > ids + 1).astype(F32)
        low_next = jnp.where(bottom, 0.0, (depth > ids + SUB + 1).astype(F32))

        for t in range(own):
            base = (t * levels) * lines + b * ROWS + r
            top = cot_ref[pl.ds(base, SUB, stride=lines), :] * top_wet
            low = cot_ref[pl.ds(base + SUB * lines, SUB, stride=lines), :] * low_wet
            fed = fed_ref[pl.ds(t * lines + n, SUB, stride=own * lines), :] * (1.0 / SCALE)
            top = top + top_wet * fed
            low_up = pltpu.roll(low, SUB - 1, 0)
            top_up = jnp.where(bottom, low_up, pltpu.roll(top, SUB - 1, 0))
            sink = params_ref[SUB + t : SUB + t + 1, :]
            col_top = top + sink * top_next * (top_up - top)
            col_low = low + sink * low_next * (low_up - low)
            both = jnp.concatenate([col_top, col_low], axis=0)
            col_ref[t * lines + n] = both
            halo_ref[t * lines + n] = both.astype(BF16)


def mixing_kernel(col_ref, south_ref, north_ref, depth_ref, params_ref, out_hbm, edges_y_ref, edges_x_ref, out_ref, sems):
    lines = depth_ref.shape[0]
    own = col_ref.shape[0] // lines
    blocks = lines // ROWS
    levels = col_ref.shape[1]
    halves = levels // SUB
    ids = lax.broadcasted_iota(jnp.int32, (SUB, LANES), 0)
    lane_ids = lax.broadcasted_iota(jnp.int32, (SUB, LANES), 1)
    last_lane, first_lane = lane_ids == LANES - 1, lane_ids == 0

    def east(v):
        turned = [pltpu.roll(x, LANES - 1, 1) for x in v]
        return [jnp.where(last_lane, turned[(b + 1) % blocks], turned[b]) for b in range(blocks)]

    def west(v):
        turned = [pltpu.roll(x, 1, 1) for x in v]
        return [jnp.where(first_lane, turned[(b - 1) % blocks], turned[b]) for b in range(blocks)]

    def own_depth(n):
        r, b = n // blocks, n % blocks
        return jnp.broadcast_to(depth_ref[b * ROWS + r : b * ROWS + r + 1, :], (SUB, LANES)).astype(F32)

    def field(which, at, h):
        ref = (south_ref, col_ref, north_ref)[at // ROWS]
        return [ref[which * lines + (at % ROWS) * blocks + b, h * SUB : (h + 1) * SUB, :].astype(F32) for b in range(blocks)]

    far = [ref[own * lines].astype(F32) for ref in (south_ref, north_ref)]
    for h in range(halves):
        at = (ids + h * SUB).astype(F32)
        wet = []
        for i in range(3 * ROWS):
            if i // ROWS == 1:
                depths = [own_depth((i % ROWS) * blocks + b) for b in range(blocks)]
            else:
                band, first = far[i // (2 * ROWS)], (i % ROWS) * blocks
                depths = [jnp.broadcast_to(band[first + b : first + b + 1], (SUB, LANES)) for b in range(blocks)]
            wet.append([(d > at).astype(F32) for d in depths])
        for i in range(3 * ROWS - 1):
            for b in range(blocks):
                edges_y_ref[h, i, b] = wet[i][b] * wet[i + 1][b]
        for i in range(1, 3 * ROWS - 1):
            ahead = east(wet[i])
            for b in range(blocks):
                edges_x_ref[h, i - 1, b] = wet[i][b] * ahead[b]

    def laplacian(rows, h, lo, hi):
        flux = [[edges_y_ref[h, i, b] * (rows[i + 1][b] - rows[i][b]) for b in range(blocks)] for i in range(lo - 1, hi)]
        out = []
        for n, i in enumerate(range(lo, hi)):
            ahead = east(rows[i])
            zonal = [edges_x_ref[h, i - 1, b] * (ahead[b] - rows[i][b]) for b in range(blocks)]
            behind = west(zonal)
            out.append([(flux[n + 1][b] - flux[n][b]) + (zonal[b] - behind[b]) for b in range(blocks)])
        return out

    def copy_out(t):
        part = pl.ds(t * levels * lines, levels * lines)
        return pltpu.make_async_copy(out_ref.at[part], out_hbm.at[part], sems.at[t])

    @pl.loop(0, own)
    def _(t):
        mixing = jnp.broadcast_to(params_ref[pl.ds(2 * SUB + t, 1), :], (SUB, LANES))
        for h in range(halves):
            rows = [field(t, i, h) for i in range(3 * ROWS)]
            once = laplacian(rows, h, 1, 5)
            twice = laplacian([None] + once, h, 2, 4)
            for r in range(ROWS):
                for b in range(blocks):
                    value = rows[ROWS + r][b] - mixing * twice[r][b]
                    out_ref[pl.ds((t * levels + h * SUB) * lines + b * ROWS + r, SUB, stride=lines), :] = value
        copy_out(t).start()

    for t in range(own):
        copy_out(t).wait()


def dense(band):
    *lead, rows, zonal = band.shape
    cut = band.reshape(*lead, rows, zonal // LANES, LANES)
    return jnp.swapaxes(cut, -3, -2).reshape(*lead, rows * zonal // LANES, LANES)


def undense(lines, rows):
    *lead, count, _ = lines.shape
    cut = lines.reshape(*lead, count // rows, rows, LANES)
    return jnp.swapaxes(cut, -3, -2).reshape(*lead, rows, count * LANES // rows)


def call(kernel, shapes, ins, outs, scratch=(), cost=None):
    return pl.pallas_call(
        kernel,
        out_shape=shapes,
        in_specs=ins,
        out_specs=outs,
        scratch_shapes=scratch,
        cost_estimate=cost,
        compiler_params=PARAMS,
    )


def body(
    cotangent,
    uptake_rate,
    nutrient,
    depth_levels,
    region_ids,
    uptake_matrix,
    province_rates,
    half_saturation,
    biharmonic,
    sinking,
):
    own, levels, band_rows, zonal = cotangent.shape
    sunlit = uptake_rate.shape[1]
    columns = band_rows * zonal
    lines = columns // LANES
    provinces = province_rates.shape[0]
    tracers = uptake_matrix.shape[0]
    tiles = lax.axis_size("tile")
    up = [(i, i + 1) for i in range(tiles - 1)]
    down = [(i + 1, i) for i in range(tiles - 1)]
    shape = jax.ShapeDtypeStruct
    cot, uptake, nutrient = dense(cotangent), dense(uptake_rate), dense(nutrient)
    depth, region = dense(depth_levels), dense(region_ids)

    inputs = (cot, nutrient, depth, region, province_rates.T, half_saturation, sinking, biharmonic)
    weighted, params = call(
        weighted_kernel,
        (shape((sunlit, own, lines, LANES), BF16), shape((3 * SUB, LANES), F32)),
        [HBM] * 8,
        (VMEM, VMEM),
        [
            pltpu.VMEM((own, sunlit, lines, LANES), F32),
            pltpu.VMEM((sunlit, lines, LANES), F32),
            pltpu.VMEM((lines, LANES), jnp.int32),
            pltpu.VMEM((lines, LANES), jnp.int32),
            pltpu.VMEM((own, provinces), F32),
            pltpu.SMEM((own,), F32),
            pltpu.SMEM((own,), F32),
            pltpu.SMEM((own,), F32),
            pltpu.SemaphoreType.DMA((own + 7,)),
        ],
        None,
    )(*(pltpu.with_memory_space_constraint(a, pltpu.HBM) for a in inputs))
    all_tracers = lax.all_to_all(weighted, "trc", 0, 0, tiled=True).reshape(tracers, lines, LANES)
    province_part = call(
        province_kernel,
        shape((provinces, own), F32),
        [VMEM] * 6,
        VMEM,
        [
            pltpu.VMEM((provinces, columns), BF16),
            pltpu.VMEM((lines * SUB, LANES), F32),
            pltpu.VMEM((2 * SUB, columns), BF16),
        ],
    )(cot, uptake, nutrient, depth, region, params)
    fed = call(
        feed_kernel,
        shape((tracers, lines, LANES), F32),
        [VMEM, VMEM],
        VMEM,
        [pltpu.VMEM((tracers * lines, LANES), F32), pltpu.VMEM((tracers * lines, LANES), F32)],
    )(uptake_matrix, all_tracers)
    fed = fed.astype(jnp.float16).reshape(sunlit, own, lines, LANES)
    fed = lax.all_to_all(fed, "trc", 0, 0, tiled=True).astype(F32)
    col, halo = call(
        column_kernel,
        (shape((own * lines, levels, LANES), F32), shape((own * lines + 1, levels, LANES), BF16)),
        [VMEM] * 4,
        (VMEM, VMEM),
    )(cot.reshape(-1, LANES), fed.reshape(-1, LANES), depth, params)
    south = lax.ppermute(halo, "tile", up)
    north = lax.ppermute(halo, "tile", down)
    province_part, south, north = lax.optimization_barrier((province_part, south, north))
    own_parts = lax.all_to_all(province_part, "tile", 0, 0, tiled=True)
    tracer_grad = call(
        mixing_kernel,
        shape((own * levels * lines, LANES), F32),
        [VMEM] * 5,
        HBM,
        [
            pltpu.VMEM((levels // SUB, 5, lines // ROWS, SUB, LANES), F32),
            pltpu.VMEM((levels // SUB, 4, lines // ROWS, SUB, LANES), F32),
            pltpu.VMEM((own * levels * lines, LANES), F32),
            pltpu.SemaphoreType.DMA((own,)),
        ],
        pl.CostEstimate(flops=20_000_000, bytes_accessed=100_000_000, transcendentals=0),
    )(col, south, north, depth, params)
    own_parts, tracer_grad = lax.optimization_barrier((own_parts, tracer_grad))
    rate_grad = jnp.sum(own_parts, axis=0, keepdims=True) * (1.0 / (sunlit * columns))
    tracer_grad = tracer_grad.reshape(own, levels, lines, LANES)
    return (undense(tracer_grad, band_rows), rate_grad)


def solution(mesh):
    return jax.shard_map(
        body,
        mesh=mesh,
        in_specs=(
            P("trc", None, "tile", None),
            P("trc", None, "tile", None),
            P(None, "tile", None),
            P("tile", None),
            P("tile", None),
            P(),
            P(None, "trc"),
            P("trc"),
            P("trc"),
            P("trc"),
        ),
        out_specs=(P("trc", None, "tile", None), P("tile", "trc")),
        check_vma=False,
    )
```

time: 77.8 us -> 72.9 us (0.937)
  blocking collectives: 51.4 us -> 28 us
  starting transfers between devices: 10 us -> 22.9 us
  waiting for transfers between devices: 0.01 us -> 12.3 us
  local copies, waits for them, and re-layouts: 5.36 us -> 0.66 us
  Pallas kernels: 9.13 us -> 7.32 us
    all_to_all x1 -> x0, blocking collectives: 23.4 us -> none  [body(): own_parts = lax.all_to_all(province_part, 'tile', 0, 0, tiled=True)]
    all_to_all x0 -> x1, starting transfers between devices: none -> 12.8 us  [body(): own_parts = lax.all_to_all(province_part, 'tile', 0, 0, tiled=True)]
    all_to_all x0 -> x1, waiting for transfers between devices: none -> 5.49 us  [body(): own_parts = lax.all_to_all(province_part, 'tile', 0, 0, tiled=True)]
    unnamed x26 -> x12, local copies, waits for them, and re-layouts: 5.36 us -> 0.66 us
    ppermute x1, waiting for transfers between devices: 0.01 us -> 4.4 us  [body(): north = lax.ppermute(halo, 'tile', down)]
    ppermute x1, waiting for transfers between devices: 0.01 us -> 2.43 us  [body(): south = lax.ppermute(halo, 'tile', up)]
    pallas_call x5, Pallas kernels: 9.13 us -> 7.32 us  [the longest x1 3.76 us: body(): call(mixing_kernel, shape((own * levels * lines, LANES), F32), [VMEM] * 5...]
  transfers between devices with their start and end apart: 2 -> 3, of which waited for: 0 -> 3; matrix products, arithmetic and copies ran while one was open for 1% -> 0% of each run, Pallas kernels for 1% -> 7%
where the time goes in v3:
time: 72.9 us; the launch traced here: 72.5 us
  blocking collectives  28 us (38%)
  starting transfers between devices  22.9 us (31%)
  waiting for transfers between devices  12.3 us (17%)
  Pallas kernels  7.32 us (10%)
  between operations  0.74 us (1%)
    all_to_all x1, blocking collectives, body(): lax.all_to_all(weighted, 'trc', 0, 0, tiled=True)  16.3 us
    all_to_all x1, starting transfers between devices, body(): own_parts = lax.all_to_all(province_part, 'tile', 0, 0, tiled=True)  12.8 us
    all_to_all x1, blocking collectives, body(): fed = lax.all_to_all(fed, 'trc', 0, 0, tiled=True).astype(F32)  11.7 us
    ppermute x1, starting transfers between devices, body(): south = lax.ppermute(halo, 'tile', up)  8.12 us
    all_to_all x1, waiting for transfers between devices, body(): own_parts = lax.all_to_all(province_part, 'tile', 0, 0, tiled=True)  5.49 us
    ppermute x1, waiting for transfers between devices, body(): north = lax.ppermute(halo, 'tile', down)  4.4 us
    pallas_call x1, Pallas kernels, body(): call(mixing_kernel, shape((own * levels * lines, LANES), F32), [VMEM] * 5...  3.76 us
    ppermute x1, waiting for transfers between devices, body(): south = lax.ppermute(halo, 'tile', up)  2.43 us
  transfers between devices with their start and end apart: 3, of which 3 were waited for; matrix products, arithmetic and copies ran while one was open for 0% of the time, Pallas kernels for 7%

profile of v3, /device:TPU:1, one launch (start us, length us, event | category | flops | bytes accessed | tf_op | source)
XLA Modules:
  0.0 72.5 jit_solution(5852377201655541546)
XLA Ops:
  0.6 1.6 %shard_map.113 = (bf16[8,7,16,128]{3,2,1,0:T(8,128)(2,1)S(1)}, f32[24,128]{1,0:T(8,128)S(1)}) custom-call(f32[7,16,16,128]{3,2,1,0:T(8,128)} %bitcast.44, f32[8,16,128]{2,1,0:T(8,128)} %bitcast.48, s32[16,128]{1,0:T(8,128)} %bitcast.51, s32[16,128]{1,0:T(8,128)} %bitcast.55, f32[7,64]{1,0:T(8,128)} %bitcast.60, f32[7]{0:T(128)} %half_hbm.1, f32[7]{0:T(128)} %sinking_hbm.1, ...), custom_call_target="tpu_custom_call" | custom-call | tf_op jit(solution)/shard_map/pallas_call | solution.py:266
  2.3 0.0 copy-start.5
  2.3 16.3 %all_to_all.22 = bf16[8,7,16,128]{3,2,1,0:T(8,128)(2,1)S(1)} all-to-all(bf16[8,7,16,128]{3,2,1,0:T(8,128)(2,1)S(1)} %get-tuple-element.12), channel_id=1, replica_groups=mesh['tile'=64,'trc'=8] {'trc'}, dimensions={0} | all-to-all | bytes 458752 | tf_op jit(solution)/shard_map/all_to_all | solution.py:284
  18.6 0.0 copy-done.5
  18.6 0.4 shard_map.115
  19.0 0.0 copy-start
  19.0 11.7 %all_to_all.23 = f16[8,7,16,128]{3,2,1,0:T(8,128)(2,1)S(1)} all-to-all(f16[8,7,16,128]{3,2,1,0:T(8,128)(2,1)S(1)} %bitcast.57), channel_id=1, replica_groups=mesh['tile'=64,'trc'=8] {'trc'}, dimensions={0} | all-to-all | bytes 458752 | tf_op jit(solution)/shard_map/all_to_all | solution.py:304
  30.7 0.0 copy-start.3
  30.8 0.0 copy-done
  30.8 0.6 copy-done.3
  31.4 0.0 copy-start.1
  31.4 0.5 shard_map.116
  31.9 8.1 %collective-permute-start = (bf16[113,16,128]{2,1,0:T(8,128)(2,1)S(1)}, bf16[113,16,128]{2,1,0:T(8,128)(2,1)S(1)}, u32[]{:S(2)}, u32[]{:S(2)}) collective-permute-start(bf16[113,16,128]{2,1,0:T(8,128)(2,1)S(1)} %get-tuple-element.13), channel_id=1, source_target_pairs={{0,8},{8,16},{16,24},{24,32},{32,40},{40,48},{48,56},{56,64},{64,7... | collective-permute-start | bytes 1388552 | tf_op jit(solution)/shard_map/ppermute | solution.py:311
  40.1 1.9 %collective-permute-start.1 = (bf16[113,16,128]{2,1,0:T(8,128)(2,1)S(1)}, bf16[113,16,128]{2,1,0:T(8,128)(2,1)S(1)}, u32[]{:S(2)}, u32[]{:S(2)}) collective-permute-start(bf16[113,16,128]{2,1,0:T(8,128)(2,1)S(1)} %get-tuple-element.13), channel_id=1, source_target_pairs={{8,0},{16,8},{24,16},{32,24},{40,32},{48,40},{56,48},{64,56},{72,6... | collective-permute-start | bytes 1388552 | tf_op jit(solution)/shard_map/ppermute | solution.py:312
  42.0 0.0 copy-done.1
  42.0 0.0 copy-done.2
  42.0 0.0 copy-done.4
  42.0 1.1 %shard_map.114 = f32[64,7]{1,0:T(8,128)} custom-call(f32[7,16,16,128]{3,2,1,0:T(8,128)S(1)} %bitcast.46, bf16[7,8,16,128]{3,2,1,0:T(8,128)(2,1)S(1)} %bitcast.50, f32[8,16,128]{2,1,0:T(8,128)S(1)} %bitcast.49, s32[16,128]{1,0:T(8,128)S(1)} %bitcast.53, s32[16,128]{1,0:T(8,128)S(1)} %bitcast.56, f32[24,128]{1,0:T(8,128)S(1)} %get-tuple-element.11.params_ref), custom_call_target="tpu_custom_call" | custom-call | tf_op jit(solution)/shard_map/pallas_call | solution.py:285
  43.1 2.4 %collective-permute-done.south_ref = bf16[113,16,128]{2,1,0:T(8,128)(2,1)S(1)} collective-permute-done((bf16[113,16,128]{2,1,0:T(8,128)(2,1)S(1)}, bf16[113,16,128]{2,1,0:T(8,128)(2,1)S(1)}, u32[]{:S(2)}, u32[]{:S(2)}) %collective-permute-start) | collective-permute-done | bytes 462880 | tf_op jit(solution)/shard_map/ppermute | solution.py:311
  45.5 4.4 %collective-permute-done.1.north_ref = bf16[113,16,128]{2,1,0:T(8,128)(2,1)S(1)} collective-permute-done((bf16[113,16,128]{2,1,0:T(8,128)(2,1)S(1)}, bf16[113,16,128]{2,1,0:T(8,128)(2,1)S(1)}, u32[]{:S(2)}, u32[]{:S(2)}) %collective-permute-start.1) | collective-permute-done | bytes 462880 | tf_op jit(solution)/shard_map/ppermute | solution.py:312
  49.9 12.8 %all-to-all-start.2 = ((f32[64,1,7]{2,1,0:T(1,128)}), f32[64,1,7]{2,1,0:T(1,128)S(1)}, u32[]{:S(2)}, u32[]{:S(2)}) async-start(f32[64,1,7]{2,1,0:T(1,128)} %bitcast.29), calls=%async_computation.2 | async-start | bytes 65536 | tf_op jit(solution)/shard_map/all_to_all | solution.py:314
  62.7 3.8 %shard_map.117 = f32[1792,128]{1,0:T(8,128)} custom-call(f32[112,16,128]{2,1,0:T(8,128)S(1)} %get-tuple-element.15.col_ref, bf16[113,16,128]{2,1,0:T(8,128)(2,1)S(1)} %collective-permute-done.south_ref, bf16[113,16,128]{2,1,0:T(8,128)(2,1)S(1)} %collective-permute-done.1.north_ref, s32[16,128]{1,0:T(8,128)S(1)} %bitcast.54, ...), custom_call_target="tpu_custom_call" | custom-call | flops 20000000 | bytes 100000000 | tf_op jit(solution)/shard_map/pallas_call | solution.py:315
  66.5 5.5 %all-to-all-done.2 = f32[64,1,7]{2,1,0:T(1,128)S(1)} async-done(((f32[64,1,7]{2,1,0:T(1,128)}), f32[64,1,7]{2,1,0:T(1,128)S(1)}, u32[]{:S(2)}, u32[]{:S(2)}) %all-to-all-start.2) | async-done | bytes 1824 | tf_op jit(solution)/shard_map/all_to_all | solution.py:314
  72.0 0.5 multiply_bitcast_fusion
  (5 shorter events, 0.1 us)
Async XLA Ops:
  2.3 16.3 %copy-start.5 = (bf16[56,56]{1,0:T(8,128)(2,1)S(1)}, bf16[56,56]{1,0:T(8,128)(2,1)}, u32[]{:S(2)}) copy-start(bf16[56,56]{1,0:T(8,128)(2,1)} %matrix_ref.1) | copy-start | bytes 18820
  19.0 11.8 %copy-start = (f32[7,16,2,1024]{3,2,1,0:T(2,128)S(1)}, f32[7,16,2,1024]{3,2,1,0:T(2,128)}, u32[]{:S(2)}) copy-start(f32[7,16,2,1024]{3,2,1,0:T(2,128)} %param.10) | copy-start | bytes 2752516
  30.7 0.7 copy-start.3
  31.4 10.6 %copy-start.1 = (f32[8,2,1024]{2,1,0:T(2,128)S(1)}, f32[8,2,1024]{2,1,0:T(2,128)}, u32[]{:S(2)}) copy-start(f32[8,2,1024]{2,1,0:T(2,128)} %param.12) | copy-start | bytes 196612
  31.4 10.6 %copy-start.2 = (bf16[7,8,2,1024]{3,2,1,0:T(2,128)(2,1)S(1)}, bf16[7,8,2,1024]{3,2,1,0:T(2,128)(2,1)}, u32[]{:S(2)}) copy-start(bf16[7,8,2,1024]{3,2,1,0:T(2,128)(2,1)} %param.11) | copy-start | bytes 688132
  31.4 10.6 %copy-start.4 = (s32[2,1024]{1,0:T(2,128)S(1)}, s32[2,1024]{1,0:T(2,128)}, u32[]{:S(2)}) copy-start(s32[2,1024]{1,0:T(2,128)} %param.14) | copy-start | bytes 24580
  31.9 13.6 %collective-permute-start = (bf16[113,16,128]{2,1,0:T(8,128)(2,1)S(1)}, bf16[113,16,128]{2,1,0:T(8,128)(2,1)S(1)}, u32[]{:S(2)}, u32[]{:S(2)}) collective-permute-start(bf16[113,16,128]{2,1,0:T(8,128)(2,1)S(1)} %get-tuple-element.13), channel_id=1, source_target_pairs={{0,8},{8,16},{16,24},{24,32},{32,40},{40,48},{48,56},{56,64},{64,7... | collective-permute-start | bytes 1388552 | tf_op jit(solution)/shard_map/ppermute | solution.py:311
  40.1 9.8 %collective-permute-start.1 = (bf16[113,16,128]{2,1,0:T(8,128)(2,1)S(1)}, bf16[113,16,128]{2,1,0:T(8,128)(2,1)S(1)}, u32[]{:S(2)}, u32[]{:S(2)}) collective-permute-start(bf16[113,16,128]{2,1,0:T(8,128)(2,1)S(1)} %get-tuple-element.13), channel_id=1, source_target_pairs={{8,0},{16,8},{24,16},{32,24},{40,32},{48,40},{56,48},{64,56},{72,6... | collective-permute-start | bytes 1388552 | tf_op jit(solution)/shard_map/ppermute | solution.py:312
  49.9 22.1 %all-to-all-start.2 = ((f32[64,1,7]{2,1,0:T(1,128)}), f32[64,1,7]{2,1,0:T(1,128)S(1)}, u32[]{:S(2)}, u32[]{:S(2)}) async-start(f32[64,1,7]{2,1,0:T(1,128)} %bitcast.29), calls=%async_computation.2 | async-start | bytes 65536 | tf_op jit(solution)/shard_map/all_to_all | solution.py:314

commit v4 on v3

--- a/solution.py
+++ b/solution.py
@@ -28,8 +28,8 @@
 
 def weighted_kernel(
     cot_hbm, nutrient_hbm, depth_hbm, region_hbm, rates_hbm, half_hbm, sinking_hbm, mixing_hbm,
-    out_ref, params_ref,
-    cot_ref, nutrient_ref, depth_ref, region_ref, rates_ref, half_ref, sinking_ref, mixing_ref, sems,
+    out_ref, params_ref, nutrient_ref, depth_ref, region_ref,
+    cot_ref, rates_ref, half_ref, sinking_ref, mixing_ref, sems,
 ):
     own, sunlit = out_ref.shape[1], out_ref.shape[0]
     blocks = cot_ref.shape[2] // ROWS
@@ -263,16 +263,19 @@
     depth, region = dense(depth_levels), dense(region_ids)
 
     inputs = (cot, nutrient, depth, region, province_rates.T, half_saturation, sinking, biharmonic)
-    weighted, params = call(
+    weighted, params, nutrient, depth, region = call(
         weighted_kernel,
-        (shape((sunlit, own, lines, LANES), BF16), shape((3 * SUB, LANES), F32)),
+        (
+            shape((sunlit, own, lines, LANES), BF16),
+            shape((3 * SUB, LANES), F32),
+            shape(nutrient.shape, F32),
+            shape(depth.shape, jnp.int32),
+            shape(region.shape, jnp.int32),
+        ),
         [HBM] * 8,
-        (VMEM, VMEM),
+        (VMEM,) * 5,
         [
             pltpu.VMEM((own, sunlit, lines, LANES), F32),
-            pltpu.VMEM((sunlit, lines, LANES), F32),
-            pltpu.VMEM((lines, LANES), jnp.int32),
-            pltpu.VMEM((lines, LANES), jnp.int32),
             pltpu.VMEM((own, provinces), F32),
             pltpu.SMEM((own,), F32),
             pltpu.SMEM((own,), F32),
@@ -301,7 +304,9 @@
         [pltpu.VMEM((tracers * lines, LANES), F32), pltpu.VMEM((tracers * lines, LANES), F32)],
     )(uptake_matrix, all_tracers)
     fed = fed.astype(jnp.float16).reshape(sunlit, own, lines, LANES)
-    fed = lax.all_to_all(fed, "trc", 0, 0, tiled=True).astype(F32)
+    fed = lax.all_to_all(fed, "trc", 0, 0, tiled=True)
+    fed, province_part = lax.optimization_barrier((fed, province_part))
+    fed = fed.astype(F32)
     col, halo = call(
         column_kernel,
         (shape((own * lines, levels, LANES), F32), shape((own * lines + 1, levels, LANES), BF16)),
@@ -310,7 +315,6 @@
     )(cot.reshape(-1, LANES), fed.reshape(-1, LANES), depth, params)
     south = lax.ppermute(halo, "tile", up)
     north = lax.ppermute(halo, "tile", down)
-    province_part, south, north = lax.optimization_barrier((province_part, south, north))
     own_parts = lax.all_to_all(province_part, "tile", 0, 0, tiled=True)
     tracer_grad = call(
         mixing_kernel,

time: 72.9 us -> 65.7 us (0.901)
  blocking collectives: 28 us -> 16.3 us
  starting transfers between devices: 22.9 us -> 26.1 us
  waiting for transfers between devices: 12.3 us -> 13.5 us
    all_to_all x1 -> x0, blocking collectives: 11.7 us -> none  [body(): fed = lax.all_to_all(fed, 'trc', 0, 0, tiled=True).astype(F32)]
    all_to_all x0 -> x1, waiting for transfers between devices: none -> 8 us  [body(): fed = lax.all_to_all(fed, 'trc', 0, 0, tiled=True)]
    ppermute x1, waiting for transfers between devices: 4.4 us -> 0.01 us  [body(): north = lax.ppermute(halo, 'tile', down)]
    ppermute x1, starting transfers between devices: 8.12 us -> 3.88 us  [body(): south = lax.ppermute(halo, 'tile', up)]
    ppermute x1, starting transfers between devices: 1.92 us -> 6.16 us  [body(): north = lax.ppermute(halo, 'tile', down)]
    all_to_all x0 -> x1, starting transfers between devices: none -> 3.53 us  [body(): fed = lax.all_to_all(fed, 'trc', 0, 0, tiled=True)]
    ppermute x1, waiting for transfers between devices: 2.43 us -> 0.01 us  [body(): south = lax.ppermute(halo, 'tile', up)]
  transfers between devices with their start and end apart: 3 -> 4, of which waited for: 3 -> 2; matrix products, arithmetic and copies ran while one was open for 0% -> 0% of each run, Pallas kernels for 7% -> 7%
where the time goes in v4:
time: 65.7 us; the launch traced here: 65.3 us
  starting transfers between devices  26.1 us (40%)
  blocking collectives  16.3 us (25%)
  waiting for transfers between devices  13.5 us (21%)
  Pallas kernels  7.29 us (11%)
  other arithmetic  1.31 us (2%)
  between operations  0.74 us (1%)
    all_to_all x1, blocking collectives, body(): lax.all_to_all(weighted, 'trc', 0, 0, tiled=True)  16.3 us
    all_to_all x1, starting transfers between devices, body(): own_parts = lax.all_to_all(province_part, 'tile', 0, 0, tiled=True)  12.5 us
    all_to_all x1, waiting for transfers between devices, body(): fed = lax.all_to_all(fed, 'trc', 0, 0, tiled=True)  8 us
    ppermute x1, starting transfers between devices, body(): north = lax.ppermute(halo, 'tile', down)  6.16 us
    all_to_all x1, waiting for transfers between devices, body(): own_parts = lax.all_to_all(province_part, 'tile', 0, 0, tiled=True)  5.51 us
    ppermute x1, starting transfers between devices, body(): south = lax.ppermute(halo, 'tile', up)  3.88 us
    pallas_call x1, Pallas kernels, body(): call(mixing_kernel, shape((own * levels * lines, LANES), F32), [VMEM] * 5...  3.75 us
    all_to_all x1, starting transfers between devices, body(): fed = lax.all_to_all(fed, 'trc', 0, 0, tiled=True)  3.53 us
  transfers between devices with their start and end apart: 4, of which 2 were waited for; matrix products, arithmetic and copies ran while one was open for 0% of the time, Pallas kernels for 7%

profile of v4, /device:TPU:1, one launch (start us, length us, event | category | flops | bytes accessed | tf_op | source)
XLA Modules:
  0.0 65.3 jit_solution(4398690611616074983)
XLA Ops:
  0.6 1.6 %shard_map.113 = (bf16[8,7,16,128]{3,2,1,0:T(8,128)(2,1)S(1)}, f32[24,128]{1,0:T(8,128)S(1)}, f32[8,16,128]{2,1,0:T(8,128)S(1)}, s32[16,128]{1,0:T(8,128)S(1)}, s32[16,128]{1,0:T(8,128)S(1)}) custom-call(f32[7,16,16,128]{3,2,1,0:T(8,128)} %bitcast.44, f32[8,16,128]{2,1,0:T(8,128)} %bitcast.51, s32[16,128]{1,0:T(8,128)} %bitcast.52, s32[16,128]{1,0:T(8,128)} %bitcast.53, ...), custom_call_target="tpu_custom_call" | custom-call | tf_op jit(solution)/shard_map/pallas_call | solution.py:266
  2.3 0.0 copy-start.2
  2.3 16.3 %all_to_all.22 = bf16[8,7,16,128]{3,2,1,0:T(8,128)(2,1)S(1)} all-to-all(bf16[8,7,16,128]{3,2,1,0:T(8,128)(2,1)S(1)} %get-tuple-element.13), channel_id=1, replica_groups=mesh['tile'=64,'trc'=8] {'trc'}, dimensions={0} | all-to-all | bytes 458752 | tf_op jit(solution)/shard_map/all_to_all | solution.py:287
  18.6 0.0 copy-done.2
  18.6 0.0 copy-start
  18.6 0.4 shard_map.114
  19.0 0.7 %convert_element_type.4 = f16[56,16,128]{2,1,0:T(8,128)(2,1)} convert(f32[56,16,128]{2,1,0:T(8,128)S(1)} %shard_map.114) | non-fusion elementwise | flops 114688 | bytes 688128 | tf_op jit(solution)/shard_map/convert_element_type | solution.py:306
  19.7 0.0 copy-start.1
  19.7 3.5 %all-to-all-start.1 = ((f16[8,7,16,128]{3,2,1,0:T(8,128)(2,1)}), f16[8,7,16,128]{3,2,1,0:T(8,128)(2,1)S(1)}, u32[]{:S(2)}, u32[]{:S(2)}) async-start(f16[8,7,16,128]{3,2,1,0:T(8,128)(2,1)} %bitcast.14), calls=%async_computation.1 | async-start | bytes 458752 | tf_op jit(solution)/shard_map/all_to_all | solution.py:307
  23.2 0.0 copy-done
  23.3 0.0 copy-done.1
  23.3 1.0 %shard_map.115 = f32[64,7]{1,0:T(8,128)} custom-call(f32[7,16,16,128]{3,2,1,0:T(8,128)S(1)} %bitcast.45, bf16[7,8,16,128]{3,2,1,0:T(8,128)(2,1)S(1)} %bitcast.48, f32[8,16,128]{2,1,0:T(8,128)S(1)} %get-tuple-element.14.nutrient_ref, s32[16,128]{1,0:T(8,128)S(1)} %get-tuple-element.15.depth_ref, s32[16,128]{1,0:T(8,128)S(1)} %get-tuple-element.16.region_ref, ...), custom_call_target="tpu_custom_call" | custom-call | tf_op jit(solution)/shard_map/pallas_call | solution.py:288
  24.3 8.0 %all-to-all-done.1 = f16[8,7,16,128]{3,2,1,0:T(8,128)(2,1)S(1)} async-done(((f16[8,7,16,128]{3,2,1,0:T(8,128)(2,1)}), f16[8,7,16,128]{3,2,1,0:T(8,128)(2,1)S(1)}, u32[]{:S(2)}, u32[]{:S(2)}) %all-to-all-start.1) | async-done | bytes 229408 | tf_op jit(solution)/shard_map/all_to_all | solution.py:307
  32.4 0.5 shard_map.116
  32.9 6.2 %collective-permute-start.1 = (bf16[113,16,128]{2,1,0:T(8,128)(2,1)S(1)}, bf16[113,16,128]{2,1,0:T(8,128)(2,1)S(1)}, u32[]{:S(2)}, u32[]{:S(2)}) collective-permute-start(bf16[113,16,128]{2,1,0:T(8,128)(2,1)S(1)} %get-tuple-element.21), channel_id=1, source_target_pairs={{8,0},{16,8},{24,16},{32,24},{40,32},{48,40},{56,48},{64,56},{72,6... | collective-permute-start | bytes 1388552 | tf_op jit(solution)/shard_map/ppermute | solution.py:317
  39.0 3.9 %collective-permute-start = (bf16[113,16,128]{2,1,0:T(8,128)(2,1)S(1)}, bf16[113,16,128]{2,1,0:T(8,128)(2,1)S(1)}, u32[]{:S(2)}, u32[]{:S(2)}) collective-permute-start(bf16[113,16,128]{2,1,0:T(8,128)(2,1)S(1)} %get-tuple-element.21), channel_id=1, source_target_pairs={{0,8},{8,16},{16,24},{24,32},{32,40},{40,48},{48,56},{56,64},{64,7... | collective-permute-start | bytes 1388552 | tf_op jit(solution)/shard_map/ppermute | solution.py:316
  42.9 12.5 %all-to-all-start.2 = ((f32[64,1,7]{2,1,0:T(1,128)}), f32[64,1,7]{2,1,0:T(1,128)S(1)}, u32[]{:S(2)}, u32[]{:S(2)}) async-start(f32[64,1,7]{2,1,0:T(1,128)} %bitcast.21), calls=%async_computation.2 | async-start | bytes 65536 | tf_op jit(solution)/shard_map/all_to_all | solution.py:318
  55.5 0.0 collective-permute-done.1.north_ref
  55.5 0.0 collective-permute-done.south_ref
  55.5 3.7 %shard_map.117 = f32[1792,128]{1,0:T(8,128)} custom-call(f32[112,16,128]{2,1,0:T(8,128)S(1)} %get-tuple-element.20.col_ref, bf16[113,16,128]{2,1,0:T(8,128)(2,1)S(1)} %collective-permute-done.south_ref, bf16[113,16,128]{2,1,0:T(8,128)(2,1)S(1)} %collective-permute-done.1.north_ref, s32[16,128]{1,0:T(8,128)S(1)} %get-tuple-element.15.depth_ref, ...), custom_call_target="tpu_custom_call" | custom-call | flops 20000000 | bytes 100000000 | tf_op jit(solution)/shard_map/pallas_call | solution.py:319
  59.3 5.5 %all-to-all-done.2 = f32[64,1,7]{2,1,0:T(1,128)S(1)} async-done(((f32[64,1,7]{2,1,0:T(1,128)}), f32[64,1,7]{2,1,0:T(1,128)S(1)}, u32[]{:S(2)}, u32[]{:S(2)}) %all-to-all-start.2) | async-done | bytes 1824 | tf_op jit(solution)/shard_map/all_to_all | solution.py:318
  64.8 0.5 multiply_bitcast_fusion
  (2 shorter events, 0.1 us)
Async XLA Ops:
  2.3 16.3 %copy-start.2 = (bf16[56,56]{1,0:T(8,128)(2,1)S(1)}, bf16[56,56]{1,0:T(8,128)(2,1)}, u32[]{:S(2)}) copy-start(bf16[56,56]{1,0:T(8,128)(2,1)} %matrix_ref.1) | copy-start | bytes 18820
  18.6 4.6 %copy-start = (f32[7,16,2,1024]{3,2,1,0:T(2,128)S(1)}, f32[7,16,2,1024]{3,2,1,0:T(2,128)}, u32[]{:S(2)}) copy-start(f32[7,16,2,1024]{3,2,1,0:T(2,128)} %param.10) | copy-start | bytes 2752516
  19.7 3.6 %copy-start.1 = (bf16[7,8,2,1024]{3,2,1,0:T(2,128)(2,1)S(1)}, bf16[7,8,2,1024]{3,2,1,0:T(2,128)(2,1)}, u32[]{:S(2)}) copy-start(bf16[7,8,2,1024]{3,2,1,0:T(2,128)(2,1)} %param.11) | copy-start | bytes 688132
  19.7 12.6 %all-to-all-start.1 = ((f16[8,7,16,128]{3,2,1,0:T(8,128)(2,1)}), f16[8,7,16,128]{3,2,1,0:T(8,128)(2,1)S(1)}, u32[]{:S(2)}, u32[]{:S(2)}) async-start(f16[8,7,16,128]{3,2,1,0:T(8,128)(2,1)} %bitcast.14), calls=%async_computation.1 | async-start | bytes 458752 | tf_op jit(solution)/shard_map/all_to_all | solution.py:307
  32.9 22.6 %collective-permute-start.1 = (bf16[113,16,128]{2,1,0:T(8,128)(2,1)S(1)}, bf16[113,16,128]{2,1,0:T(8,128)(2,1)S(1)}, u32[]{:S(2)}, u32[]{:S(2)}) collective-permute-start(bf16[113,16,128]{2,1,0:T(8,128)(2,1)S(1)} %get-tuple-element.21), channel_id=1, source_target_pairs={{8,0},{16,8},{24,16},{32,24},{40,32},{48,40},{56,48},{64,56},{72,6... | collective-permute-start | bytes 1388552 | tf_op jit(solution)/shard_map/ppermute | solution.py:317
  39.0 16.5 %collective-permute-start = (bf16[113,16,128]{2,1,0:T(8,128)(2,1)S(1)}, bf16[113,16,128]{2,1,0:T(8,128)(2,1)S(1)}, u32[]{:S(2)}, u32[]{:S(2)}) collective-permute-start(bf16[113,16,128]{2,1,0:T(8,128)(2,1)S(1)} %get-tuple-element.21), channel_id=1, source_target_pairs={{0,8},{8,16},{16,24},{24,32},{32,40},{40,48},{48,56},{56,64},{64,7... | collective-permute-start | bytes 1388552 | tf_op jit(solution)/shard_map/ppermute | solution.py:316
  42.9 21.8 %all-to-all-start.2 = ((f32[64,1,7]{2,1,0:T(1,128)}), f32[64,1,7]{2,1,0:T(1,128)S(1)}, u32[]{:S(2)}, u32[]{:S(2)}) async-start(f32[64,1,7]{2,1,0:T(1,128)} %bitcast.21), calls=%async_computation.2 | async-start | bytes 65536 | tf_op jit(solution)/shard_map/all_to_all | solution.py:318

commit v5 on v4

--- a/solution.py
+++ b/solution.py
@@ -88,7 +88,8 @@
         both = jnp.concatenate([high, term - high], axis=0)
         parts_ref[:, s * LANES : (s + 1) * LANES] = both.astype(BF16)
     sums = lax.dot_general(hot_ref[...], parts_ref[...], (((1,), (1,)), ((), ())), preferred_element_type=F32)
-    out_ref[...] = sums[:, 0:own] + sums[:, 8 : 8 + own]
+    scale = 1.0 / (sunlit * lines * LANES)
+    out_ref[...] = (sums[:, 0:own] + sums[:, SUB : SUB + own]) * scale
 
 
 def feed_kernel(matrix_ref, weighted_ref, out_ref, wide_ref, fed_ref):
@@ -105,7 +106,8 @@
         out_ref[t] = fed_ref[t * lines : (t + 1) * lines, :]
 
 
-def column_kernel(cot_ref, fed_ref, depth_ref, params_ref, col_ref, halo_ref):
+def column_kernel(cot_ref, fed_ref, depth_ref, params_ref, part_ref, other_ref, col_ref, halo_ref, pair_ref):
+    pair_ref[...] = part_ref[...] + other_ref[...]
     lines = depth_ref.shape[0]
     blocks = lines // ROWS
     own = col_ref.shape[0] // lines
@@ -296,6 +298,8 @@
             pltpu.VMEM((2 * SUB, columns), BF16),
         ],
     )(cot, uptake, nutrient, depth, region, params)
+    all_tracers, province_part = lax.optimization_barrier((all_tracers, province_part))
+    other_part = lax.ppermute(province_part, "tile", [(i, i ^ 1) for i in range(tiles)])
     fed = call(
         feed_kernel,
         shape((tracers, lines, LANES), F32),
@@ -305,17 +309,21 @@
     )(uptake_matrix, all_tracers)
     fed = fed.astype(jnp.float16).reshape(sunlit, own, lines, LANES)
     fed = lax.all_to_all(fed, "trc", 0, 0, tiled=True)
-    fed, province_part = lax.optimization_barrier((fed, province_part))
     fed = fed.astype(F32)
-    col, halo = call(
+    col, halo, pair_part = call(
         column_kernel,
-        (shape((own * lines, levels, LANES), F32), shape((own * lines + 1, levels, LANES), BF16)),
-        [VMEM] * 4,
-        (VMEM, VMEM),
-    )(cot.reshape(-1, LANES), fed.reshape(-1, LANES), depth, params)
+        (
+            shape((own * lines, levels, LANES), F32),
+            shape((own * lines + 1, levels, LANES), BF16),
+            shape(province_part.shape, F32),
+        ),
+        [VMEM] * 6,
+        (VMEM,) * 3,
+    )(cot.reshape(-1, LANES), fed.reshape(-1, LANES), depth, params, province_part, other_part)
     south = lax.ppermute(halo, "tile", up)
     north = lax.ppermute(halo, "tile", down)
-    own_parts = lax.all_to_all(province_part, "tile", 0, 0, tiled=True)
+    groups = [list(range(core, tiles, 2)) for core in range(2)]
+    own_parts = lax.all_to_all(pair_part, "tile", 0, 0, axis_index_groups=groups, tiled=True)
     tracer_grad = call(
         mixing_kernel,
         shape((own * levels * lines, LANES), F32),
@@ -327,10 +335,11 @@
             pltpu.VMEM((own * levels * lines, LANES), F32),
             pltpu.SemaphoreType.DMA((own,)),
         ],
-        pl.CostEstimate(flops=20_000_000, bytes_accessed=100_000_000, transcendentals=0),
+        pl.CostEstimate(flops=1_000_000, bytes_accessed=2_000_000, transcendentals=0),
     )(col, south, north, depth, params)
     own_parts, tracer_grad = lax.optimization_barrier((own_parts, tracer_grad))
-    rate_grad = jnp.sum(own_parts, axis=0, keepdims=True) * (1.0 / (sunlit * columns))
+    both = jnp.sum(own_parts.reshape(tiles // 2, 2, own), axis=0)
+    rate_grad = jnp.where((lax.axis_index("tile") & 1) == 0, both[0:1], both[1:2])
     tracer_grad = tracer_grad.reshape(own, levels, lines, LANES)
     return (undense(tracer_grad, band_rows), rate_grad)
 

time: 65.7 us -> 67.1 us (1.021); the launches traced: 65.3 us -> 65.8 us
  blocking collectives: 16.3 us -> 0 us
  starting transfers between devices: 26.1 us -> 38.8 us
  waiting for transfers between devices: 13.5 us -> 16.9 us
  Pallas kernels: 7.29 us -> 8.04 us
    all_to_all x1 -> x0, blocking collectives: 16.3 us -> none  [body(): lax.all_to_all(weighted, 'trc', 0, 0, tiled=True)]
    all_to_all x1 -> x2, waiting for transfers between devices: 5.51 us -> 13.5 us  [the longest x1 8.56 us: body(): lax.all_to_all(weighted, 'trc', 0, 0, tiled=True)]
    all_to_all x1 -> x2, starting transfers between devices: 12.5 us -> 19.8 us  [the longest x1 12 us: body(): lax.all_to_all(pair_part, 'tile', 0, 0, axis_index_groups=groups, tiled=T...]
    ppermute x0 -> x1, starting transfers between devices: none -> 5.57 us  [body(): lax.ppermute(province_part, 'tile', [(i, i ^ 1) for i in range(tiles)])]
    all_to_all x1, waiting for transfers between devices: 8 us -> 3.35 us  [body(): fed = lax.all_to_all(fed, 'trc', 0, 0, tiled=True)]
    ppermute x1, starting transfers between devices: 6.16 us -> 1.92 us  [body(): north = lax.ppermute(halo, 'tile', down)]
    ppermute x1, starting transfers between devices: 3.88 us -> 8.09 us  [body(): south = lax.ppermute(halo, 'tile', up)]
    pallas_call x1, Pallas kernels: 1.62 us -> 2.38 us  [body(): call(weighted_kernel, (shape((sunlit, own, lines, LANES), BF16), shape((3...]
  transfers between devices with their start and end apart: 4 -> 6, of which waited for: 2 -> 3; matrix products, arithmetic and copies ran while one was open for 0% -> 0% of each run, Pallas kernels for 7% -> 6%
where the time goes in v5:
time: 67.1 us; the launch traced here: 65.8 us
  starting transfers between devices  38.8 us (58%)
  waiting for transfers between devices  16.9 us (25%)
  Pallas kernels  8.04 us (12%)
  other arithmetic  1.33 us (2%)
  between operations  0.78 us (1%)
    all_to_all x1, starting transfers between devices, body(): lax.all_to_all(pair_part, 'tile', 0, 0, axis_index_groups=groups, tiled=T...  12 us
    all_to_all x1, waiting for transfers between devices, body(): lax.all_to_all(weighted, 'trc', 0, 0, tiled=True)  8.56 us
    ppermute x1, starting transfers between devices, body(): south = lax.ppermute(halo, 'tile', up)  8.09 us
    all_to_all x1, starting transfers between devices, body(): lax.all_to_all(weighted, 'trc', 0, 0, tiled=True)  7.79 us
    ppermute x1, starting transfers between devices, body(): lax.ppermute(province_part, 'tile', [(i, i ^ 1) for i in range(tiles)])  5.57 us
    all_to_all x1, waiting for transfers between devices, body(): lax.all_to_all(pair_part, 'tile', 0, 0, axis_index_groups=groups, tiled=T...  4.98 us
    pallas_call x1, Pallas kernels, body(): call(mixing_kernel, shape((own * levels * lines, LANES), F32), [VMEM] * 5...  3.75 us
    all_to_all x1, starting transfers between devices, body(): fed = lax.all_to_all(fed, 'trc', 0, 0, tiled=True)  3.4 us
  transfers between devices with their start and end apart: 6, of which 3 were waited for; matrix products, arithmetic and copies ran while one was open for 0% of the time, Pallas kernels for 6%

profile of v5, /device:TPU:1, one launch (start us, length us, event | category | flops | bytes accessed | tf_op | source)
XLA Modules:
  0.0 65.8 jit_solution(3335027862622215901)
XLA Ops:
  0.6 0.0 copy-start
  0.6 2.4 %shard_map.113 = (bf16[8,7,16,128]{3,2,1,0:T(8,128)(2,1)}, f32[24,128]{1,0:T(8,128)S(1)}, f32[8,16,128]{2,1,0:T(8,128)S(1)}, s32[16,128]{1,0:T(8,128)S(1)}, s32[16,128]{1,0:T(8,128)S(1)}) custom-call(f32[7,16,16,128]{3,2,1,0:T(8,128)} %bitcast.41, f32[8,16,128]{2,1,0:T(8,128)} %bitcast.47, s32[16,128]{1,0:T(8,128)} %bitcast.48, s32[16,128]{1,0:T(8,128)} %bitcast.49, ...), custom_call_target="tpu_custom_call" | custom-call | tf_op jit(solution)/shard_map/pallas_call | solution.py:268
  3.0 0.0 copy-start.1
  3.0 7.8 %all-to-all-start = ((bf16[8,7,16,128]{3,2,1,0:T(8,128)(2,1)}), bf16[8,7,16,128]{3,2,1,0:T(8,128)(2,1)S(1)}, u32[]{:S(2)}, u32[]{:S(2)}) async-start(bf16[8,7,16,128]{3,2,1,0:T(8,128)(2,1)} %get-tuple-element.14), calls=%async_computation | async-start | bytes 458752 | tf_op jit(solution)/shard_map/all_to_all | solution.py:289
  10.8 0.0 copy-done
  10.8 0.0 copy-done.1
  10.9 0.0 copy-start.2
  10.9 0.4 shard_map.114.part_ref
  11.3 8.6 %all-to-all-done = bf16[8,7,16,128]{3,2,1,0:T(8,128)(2,1)S(1)} async-done(((bf16[8,7,16,128]{3,2,1,0:T(8,128)(2,1)}), bf16[8,7,16,128]{3,2,1,0:T(8,128)(2,1)S(1)}, u32[]{:S(2)}, u32[]{:S(2)}) %all-to-all-start) | async-done | bytes 229408 | tf_op jit(solution)/shard_map/all_to_all | solution.py:289
  19.9 0.4 shard_map.115
  20.2 0.7 %convert_element_type.4 = f16[56,16,128]{2,1,0:T(8,128)(2,1)} convert(f32[56,16,128]{2,1,0:T(8,128)S(1)} %shard_map.115) | non-fusion elementwise | flops 114688 | bytes 688128 | tf_op jit(solution)/shard_map/convert_element_type | solution.py:310
  21.0 3.4 %all-to-all-start.1 = ((f16[8,7,16,128]{3,2,1,0:T(8,128)(2,1)}), f16[8,7,16,128]{3,2,1,0:T(8,128)(2,1)S(1)}, u32[]{:S(2)}, u32[]{:S(2)}) async-start(f16[8,7,16,128]{3,2,1,0:T(8,128)(2,1)} %bitcast.20), calls=%async_computation.1 | async-start | bytes 458752 | tf_op jit(solution)/shard_map/all_to_all | solution.py:311
  24.4 5.6 %collective-permute-start = (f32[64,7]{1,0:T(8,128)S(1)}, f32[64,7]{1,0:T(8,128)S(1)}, u32[]{:S(2)}, u32[]{:S(2)}) collective-permute-start(f32[64,7]{1,0:T(8,128)S(1)} %shard_map.114.part_ref), channel_id=1, source_target_pairs={{0,8},{8,0},{16,24},{24,16},{32,40},{40,32},{48,56},{56,48},{64,72... | collective-permute-start | bytes 5384 | tf_op jit(solution)/shard_map/ppermute | solution.py:302
  29.9 3.4 %all-to-all-done.1 = f16[8,7,16,128]{3,2,1,0:T(8,128)(2,1)S(1)} async-done(((f16[8,7,16,128]{3,2,1,0:T(8,128)(2,1)}), f16[8,7,16,128]{3,2,1,0:T(8,128)(2,1)S(1)}, u32[]{:S(2)}, u32[]{:S(2)}) %all-to-all-start.1) | async-done | bytes 229408 | tf_op jit(solution)/shard_map/all_to_all | solution.py:311
  33.3 0.0 collective-permute-done.other_ref
  33.4 1.1 %shard_map.116 = (f32[112,16,128]{2,1,0:T(8,128)S(1)}, bf16[113,16,128]{2,1,0:T(8,128)(2,1)S(1)}, f32[64,7]{1,0:T(8,128)}) custom-call(f32[1792,128]{1,0:T(8,128)S(1)} %bitcast.43, f32[896,128]{1,0:T(8,128)S(1)} %bitcast_convert_fusion.fed_ref, s32[16,128]{1,0:T(8,128)S(1)} %get-tuple-element.16.depth_ref, f32[24,128]{1,0:T(8,128)S(1)} %get-tuple-element.18.params_ref, ...), custom_call_target="tpu_custom_call" | custom-call | tf_op jit(solution)/shard_map/pallas_call | solution.py:313
  34.5 8.1 %collective-permute-start.1 = (bf16[113,16,128]{2,1,0:T(8,128)(2,1)S(1)}, bf16[113,16,128]{2,1,0:T(8,128)(2,1)S(1)}, u32[]{:S(2)}, u32[]{:S(2)}) collective-permute-start(bf16[113,16,128]{2,1,0:T(8,128)(2,1)S(1)} %get-tuple-element.23), channel_id=1, source_target_pairs={{0,8},{8,16},{16,24},{24,32},{32,40},{40,48},{48,56},{56,64},{64,7... | collective-permute-start | bytes 1388552 | tf_op jit(solution)/shard_map/ppermute | solution.py:323
  42.6 1.9 %collective-permute-start.2 = (bf16[113,16,128]{2,1,0:T(8,128)(2,1)S(1)}, bf16[113,16,128]{2,1,0:T(8,128)(2,1)S(1)}, u32[]{:S(2)}, u32[]{:S(2)}) collective-permute-start(bf16[113,16,128]{2,1,0:T(8,128)(2,1)S(1)} %get-tuple-element.23), channel_id=1, source_target_pairs={{8,0},{16,8},{24,16},{32,24},{40,32},{48,40},{56,48},{64,56},{72,6... | collective-permute-start | bytes 1388552 | tf_op jit(solution)/shard_map/ppermute | solution.py:324
  44.5 12.0 %all-to-all-start.2 = ((f32[32,2,7]{2,1,0:T(2,128)}), f32[32,2,7]{2,1,0:T(2,128)S(1)}, u32[]{:S(2)}, u32[]{:S(2)}) async-start(f32[32,2,7]{2,1,0:T(2,128)} %bitcast.22), calls=%async_computation.2 | async-start | bytes 65536 | tf_op jit(solution)/shard_map/all_to_all | solution.py:326
  56.5 0.0 collective-permute-done.1.south_ref
  56.5 0.0 collective-permute-done.2.north_ref
  56.5 3.7 %shard_map.117 = f32[1792,128]{1,0:T(8,128)} custom-call(f32[112,16,128]{2,1,0:T(8,128)S(1)} %get-tuple-element.22.col_ref, bf16[113,16,128]{2,1,0:T(8,128)(2,1)S(1)} %collective-permute-done.1.south_ref, bf16[113,16,128]{2,1,0:T(8,128)(2,1)S(1)} %collective-permute-done.2.north_ref, s32[16,128]{1,0:T(8,128)S(1)} %get-tuple-element.16.depth_ref, ...), custom_call_target="tpu_custom_call" | custom-call | flops 1000000 | bytes 2000000 | tf_op jit(solution)/shard_map/pallas_call | solution.py:327
  60.3 5.0 %all-to-all-done.2 = f32[32,2,7]{2,1,0:T(2,128)S(1)} async-done(((f32[32,2,7]{2,1,0:T(2,128)}), f32[32,2,7]{2,1,0:T(2,128)S(1)}, u32[]{:S(2)}, u32[]{:S(2)}) %all-to-all-start.2) | async-done | bytes 1824 | tf_op jit(solution)/shard_map/all_to_all | solution.py:326
  65.3 0.5 broadcast_select_fusion
  (3 shorter events, 0.1 us)
Async XLA Ops:
  0.6 10.2 %copy-start = (f32[7,16,2,1024]{3,2,1,0:T(2,128)S(1)}, f32[7,16,2,1024]{3,2,1,0:T(2,128)}, u32[]{:S(2)}) copy-start(f32[7,16,2,1024]{3,2,1,0:T(2,128)} %param.10) | copy-start | bytes 2752516
  3.0 7.8 %copy-start.1 = (bf16[7,8,2,1024]{3,2,1,0:T(2,128)(2,1)S(1)}, bf16[7,8,2,1024]{3,2,1,0:T(2,128)(2,1)}, u32[]{:S(2)}) copy-start(bf16[7,8,2,1024]{3,2,1,0:T(2,128)(2,1)} %param.11) | copy-start | bytes 688132
  3.0 16.8 %all-to-all-start = ((bf16[8,7,16,128]{3,2,1,0:T(8,128)(2,1)}), bf16[8,7,16,128]{3,2,1,0:T(8,128)(2,1)S(1)}, u32[]{:S(2)}, u32[]{:S(2)}) async-start(bf16[8,7,16,128]{3,2,1,0:T(8,128)(2,1)} %get-tuple-element.14), calls=%async_computation | async-start | bytes 458752 | tf_op jit(solution)/shard_map/all_to_all | solution.py:289
  10.9 9.0 %copy-start.2 = (bf16[56,56]{1,0:T(8,128)(2,1)S(1)}, bf16[56,56]{1,0:T(8,128)(2,1)}, u32[]{:S(2)}) copy-start(bf16[56,56]{1,0:T(8,128)(2,1)} %matrix_ref.1) | copy-start | bytes 18820
  21.0 12.3 %all-to-all-start.1 = ((f16[8,7,16,128]{3,2,1,0:T(8,128)(2,1)}), f16[8,7,16,128]{3,2,1,0:T(8,128)(2,1)S(1)}, u32[]{:S(2)}, u32[]{:S(2)}) async-start(f16[8,7,16,128]{3,2,1,0:T(8,128)(2,1)} %bitcast.20), calls=%async_computation.1 | async-start | bytes 458752 | tf_op jit(solution)/shard_map/all_to_all | solution.py:311
  24.4 9.0 %collective-permute-start = (f32[64,7]{1,0:T(8,128)S(1)}, f32[64,7]{1,0:T(8,128)S(1)}, u32[]{:S(2)}, u32[]{:S(2)}) collective-permute-start(f32[64,7]{1,0:T(8,128)S(1)} %shard_map.114.part_ref), channel_id=1, source_target_pairs={{0,8},{8,0},{16,24},{24,16},{32,40},{40,32},{48,56},{56,48},{64,72... | collective-permute-start | bytes 5384 | tf_op jit(solution)/shard_map/ppermute | solution.py:302
  34.5 22.0 %collective-permute-start.1 = (bf16[113,16,128]{2,1,0:T(8,128)(2,1)S(1)}, bf16[113,16,128]{2,1,0:T(8,128)(2,1)S(1)}, u32[]{:S(2)}, u32[]{:S(2)}) collective-permute-start(bf16[113,16,128]{2,1,0:T(8,128)(2,1)S(1)} %get-tuple-element.23), channel_id=1, source_target_pairs={{0,8},{8,16},{16,24},{24,32},{32,40},{40,48},{48,56},{56,64},{64,7... | collective-permute-start | bytes 1388552 | tf_op jit(solution)/shard_map/ppermute | solution.py:323
  42.6 13.9 %collective-permute-start.2 = (bf16[113,16,128]{2,1,0:T(8,128)(2,1)S(1)}, bf16[113,16,128]{2,1,0:T(8,128)(2,1)S(1)}, u32[]{:S(2)}, u32[]{:S(2)}) collective-permute-start(bf16[113,16,128]{2,1,0:T(8,128)(2,1)S(1)} %get-tuple-element.23), channel_id=1, source_target_pairs={{8,0},{16,8},{24,16},{32,24},{40,32},{48,40},{56,48},{64,56},{72,6... | collective-permute-start | bytes 1388552 | tf_op jit(solution)/shard_map/ppermute | solution.py:324
  44.5 20.8 %all-to-all-start.2 = ((f32[32,2,7]{2,1,0:T(2,128)}), f32[32,2,7]{2,1,0:T(2,128)S(1)}, u32[]{:S(2)}, u32[]{:S(2)}) async-start(f32[32,2,7]{2,1,0:T(2,128)} %bitcast.22), calls=%async_computation.2 | async-start | bytes 65536 | tf_op jit(solution)/shard_map/all_to_all | solution.py:326

commit v6 on v4

--- a/solution.py
+++ b/solution.py
@@ -9,6 +9,7 @@
 LANES = 128
 ROWS = 2
 SUB = 8
+CHIPS_X, CHIPS_Z, CORES = 4, 8, 2
 BF16 = jnp.bfloat16
 F32 = jnp.float32
 VMEM = pl.BlockSpec(memory_space=pltpu.VMEM)
@@ -79,7 +80,9 @@
             grad = cot_ref[t, k] * wet_at(depth, k)
             total = total + limiter * uptake_ref[t, k].astype(F32) * grad
         term_ref[pl.ds(t, lines, stride=8), :] = total
-    ids = lax.broadcasted_iota(jnp.int32, (provinces, LANES), 0)
+    place = lax.broadcasted_iota(jnp.int32, (provinces, LANES), 0)
+    z, x, core = place // (CHIPS_X * CORES), (place // CORES) % CHIPS_X, place % CORES
+    ids = (x * CHIPS_Z + z) * CORES + core
     for s in range(lines):
         line = jnp.broadcast_to(region_ref[s : s + 1, :], (provinces, LANES))
         hot_ref[:, s * LANES : (s + 1) * LANES] = (line == ids).astype(F32).astype(BF16)
@@ -88,7 +91,8 @@
         both = jnp.concatenate([high, term - high], axis=0)
         parts_ref[:, s * LANES : (s + 1) * LANES] = both.astype(BF16)
     sums = lax.dot_general(hot_ref[...], parts_ref[...], (((1,), (1,)), ((), ())), preferred_element_type=F32)
-    out_ref[...] = sums[:, 0:own] + sums[:, 8 : 8 + own]
+    scale = 1.0 / (sunlit * lines * LANES)
+    out_ref[...] = (sums[:, 0:own] + sums[:, SUB : SUB + own]) * scale
 
 
 def feed_kernel(matrix_ref, weighted_ref, out_ref, wide_ref, fed_ref):
@@ -296,6 +300,13 @@
             pltpu.VMEM((2 * SUB, columns), BF16),
         ],
     )(cot, uptake, nutrient, depth, region, params)
+    def exchanged(part, step):
+        return part + lax.ppermute(part, "tile", [(i, i ^ step) for i in range(tiles)])
+
+    chip_sum = exchanged(province_part, 1)
+    half_sum = exchanged(chip_sum, CHIPS_Z * CORES)
+    all_tracers, _ = lax.optimization_barrier((all_tracers, half_sum))
+    line_sum = exchanged(half_sum, 2 * CHIPS_Z * CORES)
     fed = call(
         feed_kernel,
         shape((tracers, lines, LANES), F32),
@@ -305,7 +316,7 @@
     )(uptake_matrix, all_tracers)
     fed = fed.astype(jnp.float16).reshape(sunlit, own, lines, LANES)
     fed = lax.all_to_all(fed, "trc", 0, 0, tiled=True)
-    fed, province_part = lax.optimization_barrier((fed, province_part))
+    fed, _ = lax.optimization_barrier((fed, line_sum))
     fed = fed.astype(F32)
     col, halo = call(
         column_kernel,
@@ -315,7 +326,10 @@
     )(cot.reshape(-1, LANES), fed.reshape(-1, LANES), depth, params)
     south = lax.ppermute(halo, "tile", up)
     north = lax.ppermute(halo, "tile", down)
-    own_parts = lax.all_to_all(province_part, "tile", 0, 0, tiled=True)
+    groups = [
+        [(x * CHIPS_Z + z) * CORES + core for z in range(CHIPS_Z)] for x in range(CHIPS_X) for core in range(CORES)
+    ]
+    own_parts = lax.all_to_all(line_sum, "tile", 0, 0, axis_index_groups=groups, tiled=True)
     tracer_grad = call(
         mixing_kernel,
         shape((own * levels * lines, LANES), F32),
@@ -327,10 +341,14 @@
             pltpu.VMEM((own * levels * lines, LANES), F32),
             pltpu.SemaphoreType.DMA((own,)),
         ],
-        pl.CostEstimate(flops=20_000_000, bytes_accessed=100_000_000, transcendentals=0),
+        pl.CostEstimate(flops=1_000_000, bytes_accessed=2_000_000, transcendentals=0),
     )(col, south, north, depth, params)
     own_parts, tracer_grad = lax.optimization_barrier((own_parts, tracer_grad))
-    rate_grad = jnp.sum(own_parts, axis=0, keepdims=True) * (1.0 / (sunlit * columns))
+    tile = lax.axis_index("tile")
+    place = (tile // (CHIPS_Z * CORES)) * CORES + tile % CORES
+    own_parts = own_parts.reshape(CHIPS_Z, CHIPS_X * CORES, own)
+    mine = lax.broadcasted_iota(jnp.int32, own_parts.shape, 1) == place
+    rate_grad = jnp.sum(jnp.where(mine, own_parts, 0.0), axis=(0, 1))[None]
     tracer_grad = tracer_grad.reshape(own, levels, lines, LANES)
     return (undense(tracer_grad, band_rows), rate_grad)
 

time: 65.7 us -> 65.3 us (level)
  the two profiles are of different devices: /device:TPU:1 before, /device:TPU:6 now
where the time goes in v6:
time: 65.3 us; the launch traced here: 64.8 us
  starting transfers between devices  37.8 us (58%)
  waiting for transfers between devices  16.6 us (25%)
  Pallas kernels  7.46 us (11%)
  other arithmetic  2 us (3%)
  between operations  0.78 us (1%)
    ppermute x3, waiting for transfers between devices, exchanged(): lax.ppermute(part, 'tile', [(i, i ^ step) for i in range(tiles)])  8.11 us
    ppermute x3, starting transfers between devices, exchanged(): lax.ppermute(part, 'tile', [(i, i ^ step) for i in range(tiles)])  8.08 us
    ppermute x1, starting transfers between devices, body(): north = lax.ppermute(halo, 'tile', down)  8.07 us
    all_to_all x1, starting transfers between devices, body(): lax.all_to_all(weighted, 'trc', 0, 0, tiled=True)  7.24 us
    all_to_all x1, starting transfers between devices, body(): lax.all_to_all(line_sum, 'tile', 0, 0, axis_index_groups=groups, tiled=True)  7.08 us
    all_to_all x1, starting transfers between devices, body(): fed = lax.all_to_all(fed, 'trc', 0, 0, tiled=True)  5.43 us
    all_to_all x1, waiting for transfers between devices, body(): lax.all_to_all(line_sum, 'tile', 0, 0, axis_index_groups=groups, tiled=True)  4.15 us
    pallas_call x1, Pallas kernels, body(): call(mixing_kernel, shape((own * levels * lines, LANES), F32), [VMEM] * 5...  3.75 us
  transfers between devices with their start and end apart: 8, of which 6 were waited for; matrix products, arithmetic and copies ran while one was open for 1% of the time, Pallas kernels for 6%

profile of v6, /device:TPU:6, one launch (start us, length us, event | category | flops | bytes accessed | tf_op | source)
XLA Modules:
  0.0 64.8 jit_solution(3649668885604463567)
XLA Ops:
  0.6 2.4 %shard_map.113 = (bf16[8,7,16,128]{3,2,1,0:T(8,128)(2,1)}, f32[24,128]{1,0:T(8,128)S(1)}, f32[8,16,128]{2,1,0:T(8,128)S(1)}, s32[16,128]{1,0:T(8,128)S(1)}, s32[16,128]{1,0:T(8,128)S(1)}) custom-call(f32[7,16,16,128]{3,2,1,0:T(8,128)} %bitcast.41, f32[8,16,128]{2,1,0:T(8,128)} %bitcast.48, s32[16,128]{1,0:T(8,128)} %bitcast.49, s32[16,128]{1,0:T(8,128)} %bitcast.50, ...), custom_call_target="tpu_custom_call" | custom-call | tf_op jit(solution)/shard_map/pallas_call | solution.py:270
  3.0 0.0 copy-start.1
  3.0 7.2 %all-to-all-start.1 = ((bf16[8,7,16,128]{3,2,1,0:T(8,128)(2,1)}), bf16[8,7,16,128]{3,2,1,0:T(8,128)(2,1)S(1)}, u32[]{:S(2)}, u32[]{:S(2)}) async-start(bf16[8,7,16,128]{3,2,1,0:T(8,128)(2,1)} %get-tuple-element.17), calls=%async_computation.1 | async-start | bytes 458752 | tf_op jit(solution)/shard_map/all_to_all | solution.py:291
  10.3 0.4 shard_map.114
  10.8 1.9 %collective-permute-start = (f32[64,7]{1,0:T(8,128)S(1)}, f32[64,7]{1,0:T(8,128)S(1)}, u32[]{:S(2)}, u32[]{:S(2)}) collective-permute-start(f32[64,7]{1,0:T(8,128)S(1)} %shard_map.114), channel_id=1, source_target_pairs={{0,8},{8,0},{16,24},{24,16},{32,40},{40,32},{48,56},{56,48},{64,72... | collective-permute-start | bytes 5384 | tf_op jit(solution)/shard_map/ppermute | solution.py:304
  12.7 1.2 %collective-permute-done = f32[64,7]{1,0:T(8,128)S(1)} collective-permute-done((f32[64,7]{1,0:T(8,128)S(1)}, f32[64,7]{1,0:T(8,128)S(1)}, u32[]{:S(2)}, u32[]{:S(2)}) %collective-permute-start) | collective-permute-done | bytes 1824 | tf_op jit(solution)/shard_map/ppermute | solution.py:304
  13.9 2.7 %collective-permute-start.1 = (f32[64,7]{1,0:T(8,128)S(1)}, f32[64,7]{1,0:T(8,128)S(1)}, u32[]{:S(2)}, u32[]{:S(2)}) collective-permute-start(f32[64,7]{1,0:T(8,128)S(1)} %add.17), channel_id=1, source_target_pairs={{0,128},{8,136},{16,144},{24,152},{32,160},{40,168},{48,176},{56,1... | collective-permute-start | bytes 5384 | tf_op jit(solution)/shard_map/ppermute | solution.py:304
  16.6 3.1 %collective-permute-done.1 = f32[64,7]{1,0:T(8,128)S(1)} collective-permute-done((f32[64,7]{1,0:T(8,128)S(1)}, f32[64,7]{1,0:T(8,128)S(1)}, u32[]{:S(2)}, u32[]{:S(2)}) %collective-permute-start.1) | collective-permute-done | bytes 1824 | tf_op jit(solution)/shard_map/ppermute | solution.py:304
  19.7 1.8 %all-to-all-done.1 = bf16[8,7,16,128]{3,2,1,0:T(8,128)(2,1)S(1)} async-done(((bf16[8,7,16,128]{3,2,1,0:T(8,128)(2,1)}), bf16[8,7,16,128]{3,2,1,0:T(8,128)(2,1)S(1)}, u32[]{:S(2)}, u32[]{:S(2)}) %all-to-all-start.1) | async-done | bytes 229408 | tf_op jit(solution)/shard_map/all_to_all | solution.py:291
  21.5 0.4 shard_map.115
  21.8 0.7 %convert_element_type.4 = f16[56,16,128]{2,1,0:T(8,128)(2,1)} convert(f32[56,16,128]{2,1,0:T(8,128)S(1)} %shard_map.115) | non-fusion elementwise | flops 114688 | bytes 688128 | tf_op jit(solution)/shard_map/convert_element_type | solution.py:317
  22.6 5.4 %all-to-all-start.2 = ((f16[8,7,16,128]{3,2,1,0:T(8,128)(2,1)}), f16[8,7,16,128]{3,2,1,0:T(8,128)(2,1)S(1)}, u32[]{:S(2)}, u32[]{:S(2)}) async-start(f16[8,7,16,128]{3,2,1,0:T(8,128)(2,1)} %bitcast.22), calls=%async_computation.2 | async-start | bytes 458752 | tf_op jit(solution)/shard_map/all_to_all | solution.py:318
  28.0 3.4 %collective-permute-start.2 = (f32[64,7]{1,0:T(8,128)S(1)}, f32[64,7]{1,0:T(8,128)S(1)}, u32[]{:S(2)}, u32[]{:S(2)}) collective-permute-start(f32[64,7]{1,0:T(8,128)S(1)} %add.18), channel_id=1, source_target_pairs={{0,256},{8,264},{16,272},{24,280},{32,288},{40,296},{48,304},{56,3... | collective-permute-start | bytes 5384 | tf_op jit(solution)/shard_map/ppermute | solution.py:304
  31.4 3.9 %collective-permute-done.2 = f32[64,7]{1,0:T(8,128)S(1)} collective-permute-done((f32[64,7]{1,0:T(8,128)S(1)}, f32[64,7]{1,0:T(8,128)S(1)}, u32[]{:S(2)}, u32[]{:S(2)}) %collective-permute-start.2) | collective-permute-done | bytes 1824 | tf_op jit(solution)/shard_map/ppermute | solution.py:304
  35.3 0.6 add.19
  35.9 2.6 %all-to-all-done.2 = f16[8,7,16,128]{3,2,1,0:T(8,128)(2,1)S(1)} async-done(((f16[8,7,16,128]{3,2,1,0:T(8,128)(2,1)}), f16[8,7,16,128]{3,2,1,0:T(8,128)(2,1)S(1)}, u32[]{:S(2)}, u32[]{:S(2)}) %all-to-all-start.2) | async-done | bytes 229408 | tf_op jit(solution)/shard_map/all_to_all | solution.py:318
  38.5 0.5 shard_map.116
  39.0 1.9 %collective-permute-start.3 = (bf16[113,16,128]{2,1,0:T(8,128)(2,1)S(1)}, bf16[113,16,128]{2,1,0:T(8,128)(2,1)S(1)}, u32[]{:S(2)}, u32[]{:S(2)}) collective-permute-start(bf16[113,16,128]{2,1,0:T(8,128)(2,1)S(1)} %get-tuple-element.21), channel_id=1, source_target_pairs={{0,8},{8,16},{16,24},{24,32},{32,40},{40,48},{48,56},{56,64},{64,7... | collective-permute-start | bytes 1388552 | tf_op jit(solution)/shard_map/ppermute | solution.py:327
  41.0 8.1 %collective-permute-start.4 = (bf16[113,16,128]{2,1,0:T(8,128)(2,1)S(1)}, bf16[113,16,128]{2,1,0:T(8,128)(2,1)S(1)}, u32[]{:S(2)}, u32[]{:S(2)}) collective-permute-start(bf16[113,16,128]{2,1,0:T(8,128)(2,1)S(1)} %get-tuple-element.21), channel_id=1, source_target_pairs={{8,0},{16,8},{24,16},{32,24},{40,32},{48,40},{56,48},{64,56},{72,6... | collective-permute-start | bytes 1388552 | tf_op jit(solution)/shard_map/ppermute | solution.py:328
  49.1 7.1 %all-to-all-start = ((f32[8,8,7]{2,1,0:T(8,128)}), f32[8,8,7]{2,1,0:T(8,128)S(1)}, u32[]{:S(2)}, u32[]{:S(2)}) async-start(f32[8,8,7]{2,1,0:T(8,128)} %bitcast.18), calls=%async_computation | async-start | bytes 65536 | tf_op jit(solution)/shard_map/all_to_all | solution.py:332
  56.2 0.1 iota.12
  56.3 3.7 %shard_map.117 = f32[1792,128]{1,0:T(8,128)} custom-call(f32[112,16,128]{2,1,0:T(8,128)S(1)} %get-tuple-element.20.col_ref, bf16[113,16,128]{2,1,0:T(8,128)(2,1)S(1)} %collective-permute-done.3.south_ref, bf16[113,16,128]{2,1,0:T(8,128)(2,1)S(1)} %collective-permute-done.4.north_ref, s32[16,128]{1,0:T(8,128)S(1)} %get-tuple-element.14.depth_ref, ...), custom_call_target="tpu_custom_call" | custom-call | flops 1000000 | bytes 2000000 | tf_op jit(solution)/shard_map/pallas_call | solution.py:333
  60.0 4.2 %all-to-all-done = f32[8,8,7]{2,1,0:T(8,128)S(1)} async-done(((f32[8,8,7]{2,1,0:T(8,128)}), f32[8,8,7]{2,1,0:T(8,128)S(1)}, u32[]{:S(2)}, u32[]{:S(2)}) %all-to-all-start) | async-done | bytes 1824 | tf_op jit(solution)/shard_map/all_to_all | solution.py:332
  64.2 0.6 select_reduce_fusion
  (12 shorter events, 0.1 us)
Async XLA Ops:
  0.6 9.7 %copy-start = (f32[7,16,2,1024]{3,2,1,0:T(2,128)S(1)}, f32[7,16,2,1024]{3,2,1,0:T(2,128)}, u32[]{:S(2)}) copy-start(f32[7,16,2,1024]{3,2,1,0:T(2,128)} %param.10) | copy-start | bytes 2752516
  3.0 7.3 %copy-start.1 = (bf16[7,8,2,1024]{3,2,1,0:T(2,128)(2,1)S(1)}, bf16[7,8,2,1024]{3,2,1,0:T(2,128)(2,1)}, u32[]{:S(2)}) copy-start(bf16[7,8,2,1024]{3,2,1,0:T(2,128)(2,1)} %param.11) | copy-start | bytes 688132
  3.0 18.4 %all-to-all-start.1 = ((bf16[8,7,16,128]{3,2,1,0:T(8,128)(2,1)}), bf16[8,7,16,128]{3,2,1,0:T(8,128)(2,1)S(1)}, u32[]{:S(2)}, u32[]{:S(2)}) async-start(bf16[8,7,16,128]{3,2,1,0:T(8,128)(2,1)} %get-tuple-element.17), calls=%async_computation.1 | async-start | bytes 458752 | tf_op jit(solution)/shard_map/all_to_all | solution.py:291
  10.8 3.1 %collective-permute-start = (f32[64,7]{1,0:T(8,128)S(1)}, f32[64,7]{1,0:T(8,128)S(1)}, u32[]{:S(2)}, u32[]{:S(2)}) collective-permute-start(f32[64,7]{1,0:T(8,128)S(1)} %shard_map.114), channel_id=1, source_target_pairs={{0,8},{8,0},{16,24},{24,16},{32,40},{40,32},{48,56},{56,48},{64,72... | collective-permute-start | bytes 5384 | tf_op jit(solution)/shard_map/ppermute | solution.py:304
  13.9 7.6 %copy-start.2 = (bf16[56,56]{1,0:T(8,128)(2,1)S(1)}, bf16[56,56]{1,0:T(8,128)(2,1)}, u32[]{:S(2)}) copy-start(bf16[56,56]{1,0:T(8,128)(2,1)} %matrix_ref.1) | copy-start | bytes 18820
  13.9 5.8 %collective-permute-start.1 = (f32[64,7]{1,0:T(8,128)S(1)}, f32[64,7]{1,0:T(8,128)S(1)}, u32[]{:S(2)}, u32[]{:S(2)}) collective-permute-start(f32[64,7]{1,0:T(8,128)S(1)} %add.17), channel_id=1, source_target_pairs={{0,128},{8,136},{16,144},{24,152},{32,160},{40,168},{48,176},{56,1... | collective-permute-start | bytes 5384 | tf_op jit(solution)/shard_map/ppermute | solution.py:304
  22.6 15.9 %all-to-all-start.2 = ((f16[8,7,16,128]{3,2,1,0:T(8,128)(2,1)}), f16[8,7,16,128]{3,2,1,0:T(8,128)(2,1)S(1)}, u32[]{:S(2)}, u32[]{:S(2)}) async-start(f16[8,7,16,128]{3,2,1,0:T(8,128)(2,1)} %bitcast.22), calls=%async_computation.2 | async-start | bytes 458752 | tf_op jit(solution)/shard_map/all_to_all | solution.py:318
  28.0 7.3 %collective-permute-start.2 = (f32[64,7]{1,0:T(8,128)S(1)}, f32[64,7]{1,0:T(8,128)S(1)}, u32[]{:S(2)}, u32[]{:S(2)}) collective-permute-start(f32[64,7]{1,0:T(8,128)S(1)} %add.18), channel_id=1, source_target_pairs={{0,256},{8,264},{16,272},{24,280},{32,288},{40,296},{48,304},{56,3... | collective-permute-start | bytes 5384 | tf_op jit(solution)/shard_map/ppermute | solution.py:304
  39.0 17.2 %collective-permute-start.3 = (bf16[113,16,128]{2,1,0:T(8,128)(2,1)S(1)}, bf16[113,16,128]{2,1,0:T(8,128)(2,1)S(1)}, u32[]{:S(2)}, u32[]{:S(2)}) collective-permute-start(bf16[113,16,128]{2,1,0:T(8,128)(2,1)S(1)} %get-tuple-element.21), channel_id=1, source_target_pairs={{0,8},{8,16},{16,24},{24,32},{32,40},{40,48},{48,56},{56,64},{64,7... | collective-permute-start | bytes 1388552 | tf_op jit(solution)/shard_map/ppermute | solution.py:327
  41.0 15.3 %collective-permute-start.4 = (bf16[113,16,128]{2,1,0:T(8,128)(2,1)S(1)}, bf16[113,16,128]{2,1,0:T(8,128)(2,1)S(1)}, u32[]{:S(2)}, u32[]{:S(2)}) collective-permute-start(bf16[113,16,128]{2,1,0:T(8,128)(2,1)S(1)} %get-tuple-element.21), channel_id=1, source_target_pairs={{8,0},{16,8},{24,16},{32,24},{40,32},{48,40},{56,48},{64,56},{72,6... | collective-permute-start | bytes 1388552 | tf_op jit(solution)/shard_map/ppermute | solution.py:328
  49.1 15.1 %all-to-all-start = ((f32[8,8,7]{2,1,0:T(8,128)}), f32[8,8,7]{2,1,0:T(8,128)S(1)}, u32[]{:S(2)}, u32[]{:S(2)}) async-start(f32[8,8,7]{2,1,0:T(8,128)} %bitcast.18), calls=%async_computation | async-start | bytes 65536 | tf_op jit(solution)/shard_map/all_to_all | solution.py:332

commit v7 on v6

--- a/solution.py
+++ b/solution.py
@@ -30,9 +30,9 @@
 def weighted_kernel(
     cot_hbm, nutrient_hbm, depth_hbm, region_hbm, rates_hbm, half_hbm, sinking_hbm, mixing_hbm,
     out_ref, params_ref, nutrient_ref, depth_ref, region_ref,
-    cot_ref, rates_ref, half_ref, sinking_ref, mixing_ref, sems,
+    cot_ref, rates_ref, half_ref, sinking_ref, mixing_ref, held_ref, sems, out_sems,
 ):
-    own, sunlit = out_ref.shape[1], out_ref.shape[0]
+    own, sunlit = held_ref.shape[1], held_ref.shape[0]
     blocks = cot_ref.shape[2] // ROWS
     pairs = [
         (depth_hbm, depth_ref), (region_hbm, region_ref), (rates_hbm, rates_ref), (nutrient_hbm, nutrient_ref),
@@ -62,7 +62,11 @@
                 limiter = food / (food + half)
                 grad = row(cot_ref, t, k, r) * wet_at(depth[r], k)
                 rows.append(rates[r] * limiter * grad)
-            out_ref[k, t] = jnp.concatenate(rows, axis=0).astype(BF16)
+            held_ref[k, t] = jnp.concatenate(rows, axis=0).astype(BF16)
+        copies.append(pltpu.make_async_copy(held_ref.at[:, t], out_ref.at[:, t], out_sems.at[t]))
+        copies[-1].start()
+    for copy in copies[-own:]:
+        copy.wait()
 
 
 def province_kernel(cot_ref, uptake_ref, nutrient_ref, depth_ref, region_ref, params_ref, out_ref, hot_ref, term_ref, parts_ref):
@@ -146,6 +150,8 @@
     own = col_ref.shape[0] // lines
     blocks = lines // ROWS
     levels = col_ref.shape[1]
+    flip = lax.axis_index("tile") & 1
+    order = [r ^ flip for r in range(ROWS)]
     halves = levels // SUB
     ids = lax.broadcasted_iota(jnp.int32, (SUB, LANES), 0)
     lane_ids = lax.broadcasted_iota(jnp.int32, (SUB, LANES), 1)
@@ -161,13 +167,14 @@
 
     def own_depth(n):
         r, b = n // blocks, n % blocks
-        return jnp.broadcast_to(depth_ref[b * ROWS + r : b * ROWS + r + 1, :], (SUB, LANES)).astype(F32)
+        return jnp.broadcast_to(depth_ref[pl.ds(b * ROWS + order[r], 1), :], (SUB, LANES)).astype(F32)
 
     def field(which, at, h):
         ref = (south_ref, col_ref, north_ref)[at // ROWS]
-        return [ref[which * lines + (at % ROWS) * blocks + b, h * SUB : (h + 1) * SUB, :].astype(F32) for b in range(blocks)]
+        return [ref[which * lines + order[at % ROWS] * blocks + b, h * SUB : (h + 1) * SUB, :].astype(F32) for b in range(blocks)]
 
     far = [ref[own * lines].astype(F32) for ref in (south_ref, north_ref)]
+    far = [jnp.where(flip == 1, jnp.concatenate([x[blocks:], x[:blocks]], axis=0), x) for x in far]
     for h in range(halves):
         at = (ids + h * SUB).astype(F32)
         wet = []
@@ -210,7 +217,7 @@
             for r in range(ROWS):
                 for b in range(blocks):
                     value = rows[ROWS + r][b] - mixing * twice[r][b]
-                    out_ref[pl.ds((t * levels + h * SUB) * lines + b * ROWS + r, SUB, stride=lines), :] = value
+                    out_ref[pl.ds((t * levels + h * SUB) * lines + b * ROWS + order[r], SUB, stride=lines), :] = value
         copy_out(t).start()
 
     for t in range(own):
@@ -260,8 +267,8 @@
     provinces = province_rates.shape[0]
     tracers = uptake_matrix.shape[0]
     tiles = lax.axis_size("tile")
-    up = [(i, i + 1) for i in range(tiles - 1)]
-    down = [(i + 1, i) for i in range(tiles - 1)]
+    within = [(i, i ^ 1) for i in range(tiles)]
+    across = [(i, ((i + 1) ^ 1) - 1) for i in range(1, tiles - 1)]
     shape = jax.ShapeDtypeStruct
     cot, uptake, nutrient = dense(cotangent), dense(uptake_rate), dense(nutrient)
     depth, region = dense(depth_levels), dense(region_ids)
@@ -277,14 +284,16 @@
             shape(region.shape, jnp.int32),
         ),
         [HBM] * 8,
-        (VMEM,) * 5,
+        (HBM,) + (VMEM,) * 4,
         [
             pltpu.VMEM((own, sunlit, lines, LANES), F32),
             pltpu.VMEM((own, provinces), F32),
             pltpu.SMEM((own,), F32),
             pltpu.SMEM((own,), F32),
             pltpu.SMEM((own,), F32),
+            pltpu.VMEM((sunlit, own, lines, LANES), BF16),
             pltpu.SemaphoreType.DMA((own + 7,)),
+            pltpu.SemaphoreType.DMA((own,)),
         ],
         None,
     )(*(pltpu.with_memory_space_constraint(a, pltpu.HBM) for a in inputs))
@@ -324,8 +333,8 @@
         [VMEM] * 4,
         (VMEM, VMEM),
     )(cot.reshape(-1, LANES), fed.reshape(-1, LANES), depth, params)
-    south = lax.ppermute(halo, "tile", up)
-    north = lax.ppermute(halo, "tile", down)
+    south = lax.ppermute(halo, "tile", across)
+    north = lax.ppermute(halo, "tile", within)
     groups = [
         [(x * CHIPS_Z + z) * CORES + core for z in range(CHIPS_Z)] for x in range(CHIPS_X) for core in range(CORES)
     ]

time: 65.3 us -> 63.9 us (0.979)
  the two profiles are of different devices: /device:TPU:6 before, /device:TPU:1 now
where the time goes in v7:
time: 63.9 us; the launch traced here: 63 us
  starting transfers between devices  40.6 us (64%)
  waiting for transfers between devices  12.1 us (19%)
  Pallas kernels  7.45 us (12%)
  other arithmetic  2 us (3%)
  between operations  0.79 us (1%)
    ppermute x3, starting transfers between devices, exchanged(): lax.ppermute(part, 'tile', [(i, i ^ step) for i in range(tiles)])  9.63 us
    all_to_all x1, starting transfers between devices, body(): lax.all_to_all(line_sum, 'tile', 0, 0, axis_index_groups=groups, tiled=True)  9.14 us
    all_to_all x1, starting transfers between devices, body(): lax.all_to_all(weighted, 'trc', 0, 0, tiled=True)  7.79 us
    ppermute x3, waiting for transfers between devices, exchanged(): lax.ppermute(part, 'tile', [(i, i ^ step) for i in range(tiles)])  6.97 us
    all_to_all x1, starting transfers between devices, body(): fed = lax.all_to_all(fed, 'trc', 0, 0, tiled=True)  6.53 us
    ppermute x1, starting transfers between devices, body(): south = lax.ppermute(halo, 'tile', across)  5.54 us
    pallas_call x1, Pallas kernels, body(): call(mixing_kernel, shape((own * levels * lines, LANES), F32), [VMEM] * 5...  3.77 us
    all_to_all x1, waiting for transfers between devices, body(): lax.all_to_all(line_sum, 'tile', 0, 0, axis_index_groups=groups, tiled=True)  2.98 us
  transfers between devices with their start and end apart: 8, of which 5 were waited for; matrix products, arithmetic and copies ran while one was open for 1% of the time, Pallas kernels for 7%

profile of v7, /device:TPU:1, one launch (start us, length us, event | category | flops | bytes accessed | tf_op | source)
XLA Modules:
  0.0 63.0 jit_solution(5631427146921764344)
XLA Ops:
  0.6 2.3 %shard_map.113 = (bf16[8,7,16,128]{3,2,1,0:T(8,128)(2,1)}, f32[24,128]{1,0:T(8,128)S(1)}, f32[8,16,128]{2,1,0:T(8,128)S(1)}, s32[16,128]{1,0:T(8,128)S(1)}, s32[16,128]{1,0:T(8,128)S(1)}) custom-call(f32[7,16,16,128]{3,2,1,0:T(8,128)} %bitcast.41, f32[8,16,128]{2,1,0:T(8,128)} %bitcast.48, s32[16,128]{1,0:T(8,128)} %bitcast.49, s32[16,128]{1,0:T(8,128)} %bitcast.50, ...), custom_call_target="tpu_custom_call" | custom-call | tf_op jit(solution)/shard_map/pallas_call | solution.py:277
  3.0 0.0 copy-start.1
  3.0 7.8 %all-to-all-start.1 = ((bf16[8,7,16,128]{3,2,1,0:T(8,128)(2,1)}), bf16[8,7,16,128]{3,2,1,0:T(8,128)(2,1)S(1)}, u32[]{:S(2)}, u32[]{:S(2)}) async-start(bf16[8,7,16,128]{3,2,1,0:T(8,128)(2,1)} %get-tuple-element.17), calls=%async_computation.1 | async-start | bytes 458752 | tf_op jit(solution)/shard_map/all_to_all | solution.py:300
  10.8 0.4 shard_map.114
  11.3 4.6 %collective-permute-start = (f32[64,7]{1,0:T(8,128)S(1)}, f32[64,7]{1,0:T(8,128)S(1)}, u32[]{:S(2)}, u32[]{:S(2)}) collective-permute-start(f32[64,7]{1,0:T(8,128)S(1)} %shard_map.114), channel_id=1, source_target_pairs={{0,8},{8,0},{16,24},{24,16},{32,40},{40,32},{48,56},{56,48},{64,72... | collective-permute-start | bytes 5384 | tf_op jit(solution)/shard_map/ppermute | solution.py:313
  15.8 0.8 %collective-permute-done = f32[64,7]{1,0:T(8,128)S(1)} collective-permute-done((f32[64,7]{1,0:T(8,128)S(1)}, f32[64,7]{1,0:T(8,128)S(1)}, u32[]{:S(2)}, u32[]{:S(2)}) %collective-permute-start) | collective-permute-done | bytes 1824 | tf_op jit(solution)/shard_map/ppermute | solution.py:313
  16.7 2.0 %collective-permute-start.1 = (f32[64,7]{1,0:T(8,128)S(1)}, f32[64,7]{1,0:T(8,128)S(1)}, u32[]{:S(2)}, u32[]{:S(2)}) collective-permute-start(f32[64,7]{1,0:T(8,128)S(1)} %add.17), channel_id=1, source_target_pairs={{0,128},{8,136},{16,144},{24,152},{32,160},{40,168},{48,176},{56,1... | collective-permute-start | bytes 5384 | tf_op jit(solution)/shard_map/ppermute | solution.py:313
  18.7 3.0 %collective-permute-done.1 = f32[64,7]{1,0:T(8,128)S(1)} collective-permute-done((f32[64,7]{1,0:T(8,128)S(1)}, f32[64,7]{1,0:T(8,128)S(1)}, u32[]{:S(2)}, u32[]{:S(2)}) %collective-permute-start.1) | collective-permute-done | bytes 1824 | tf_op jit(solution)/shard_map/ppermute | solution.py:313
  21.8 0.4 shard_map.115
  22.1 0.7 %convert_element_type.4 = f16[56,16,128]{2,1,0:T(8,128)(2,1)} convert(f32[56,16,128]{2,1,0:T(8,128)S(1)} %shard_map.115) | non-fusion elementwise | flops 114688 | bytes 688128 | tf_op jit(solution)/shard_map/convert_element_type | solution.py:326
  22.9 6.5 %all-to-all-start.2 = ((f16[8,7,16,128]{3,2,1,0:T(8,128)(2,1)}), f16[8,7,16,128]{3,2,1,0:T(8,128)(2,1)S(1)}, u32[]{:S(2)}, u32[]{:S(2)}) async-start(f16[8,7,16,128]{3,2,1,0:T(8,128)(2,1)} %bitcast.22), calls=%async_computation.2 | async-start | bytes 458752 | tf_op jit(solution)/shard_map/all_to_all | solution.py:327
  29.4 3.0 %collective-permute-start.2 = (f32[64,7]{1,0:T(8,128)S(1)}, f32[64,7]{1,0:T(8,128)S(1)}, u32[]{:S(2)}, u32[]{:S(2)}) collective-permute-start(f32[64,7]{1,0:T(8,128)S(1)} %add.18), channel_id=1, source_target_pairs={{0,256},{8,264},{16,272},{24,280},{32,288},{40,296},{48,304},{56,3... | collective-permute-start | bytes 5384 | tf_op jit(solution)/shard_map/ppermute | solution.py:313
  32.4 3.1 %collective-permute-done.2 = f32[64,7]{1,0:T(8,128)S(1)} collective-permute-done((f32[64,7]{1,0:T(8,128)S(1)}, f32[64,7]{1,0:T(8,128)S(1)}, u32[]{:S(2)}, u32[]{:S(2)}) %collective-permute-start.2) | collective-permute-done | bytes 1824 | tf_op jit(solution)/shard_map/ppermute | solution.py:313
  35.5 0.6 add.19
  36.2 2.1 %all-to-all-done.2 = f16[8,7,16,128]{3,2,1,0:T(8,128)(2,1)S(1)} async-done(((f16[8,7,16,128]{3,2,1,0:T(8,128)(2,1)}), f16[8,7,16,128]{3,2,1,0:T(8,128)(2,1)S(1)}, u32[]{:S(2)}, u32[]{:S(2)}) %all-to-all-start.2) | async-done | bytes 229408 | tf_op jit(solution)/shard_map/all_to_all | solution.py:327
  38.3 0.5 shard_map.116
  38.8 5.5 %collective-permute-start.3 = (bf16[113,16,128]{2,1,0:T(8,128)(2,1)S(1)}, bf16[113,16,128]{2,1,0:T(8,128)(2,1)S(1)}, u32[]{:S(2)}, u32[]{:S(2)}) collective-permute-start(bf16[113,16,128]{2,1,0:T(8,128)(2,1)S(1)} %get-tuple-element.21), channel_id=1, source_target_pairs={{8,16},{16,8},{24,32},{32,24},{40,48},{48,40},{56,64},{64,56},{72,... | collective-permute-start | bytes 1388552 | tf_op jit(solution)/shard_map/ppermute | solution.py:336
  44.4 1.9 %collective-permute-start.4 = (bf16[113,16,128]{2,1,0:T(8,128)(2,1)S(1)}, bf16[113,16,128]{2,1,0:T(8,128)(2,1)S(1)}, u32[]{:S(2)}, u32[]{:S(2)}) collective-permute-start(bf16[113,16,128]{2,1,0:T(8,128)(2,1)S(1)} %get-tuple-element.21), channel_id=1, source_target_pairs={{0,8},{8,0},{16,24},{24,16},{32,40},{40,32},{48,56},{56,48},{64,72... | collective-permute-start | bytes 1388552 | tf_op jit(solution)/shard_map/ppermute | solution.py:337
  46.3 9.1 %all-to-all-start = ((f32[8,8,7]{2,1,0:T(8,128)}), f32[8,8,7]{2,1,0:T(8,128)S(1)}, u32[]{:S(2)}, u32[]{:S(2)}) async-start(f32[8,8,7]{2,1,0:T(8,128)} %bitcast.18), calls=%async_computation | async-start | bytes 65536 | tf_op jit(solution)/shard_map/all_to_all | solution.py:341
  55.5 0.1 iota.12
  55.6 0.0 collective-permute-done.3.south_ref
  55.6 3.8 %shard_map.117 = f32[1792,128]{1,0:T(8,128)} custom-call(f32[112,16,128]{2,1,0:T(8,128)S(1)} %get-tuple-element.20.col_ref, bf16[113,16,128]{2,1,0:T(8,128)(2,1)S(1)} %collective-permute-done.3.south_ref, bf16[113,16,128]{2,1,0:T(8,128)(2,1)S(1)} %collective-permute-done.4.north_ref, s32[16,128]{1,0:T(8,128)S(1)} %get-tuple-element.14.depth_ref, ...), custom_call_target="tpu_custom_call" | custom-call | flops 1000000 | bytes 2000000 | tf_op jit(solution)/shard_map/pallas_call | solution.py:342
  59.4 3.0 %all-to-all-done = f32[8,8,7]{2,1,0:T(8,128)S(1)} async-done(((f32[8,8,7]{2,1,0:T(8,128)}), f32[8,8,7]{2,1,0:T(8,128)S(1)}, u32[]{:S(2)}, u32[]{:S(2)}) %all-to-all-start) | async-done | bytes 1824 | tf_op jit(solution)/shard_map/all_to_all | solution.py:341
  62.4 0.6 select_reduce_fusion
  (12 shorter events, 0.1 us)
Async XLA Ops:
  0.6 10.2 %copy-start = (f32[7,16,2,1024]{3,2,1,0:T(2,128)S(1)}, f32[7,16,2,1024]{3,2,1,0:T(2,128)}, u32[]{:S(2)}) copy-start(f32[7,16,2,1024]{3,2,1,0:T(2,128)} %param.10) | copy-start | bytes 2752516
  3.0 7.8 %copy-start.1 = (bf16[7,8,2,1024]{3,2,1,0:T(2,128)(2,1)S(1)}, bf16[7,8,2,1024]{3,2,1,0:T(2,128)(2,1)}, u32[]{:S(2)}) copy-start(bf16[7,8,2,1024]{3,2,1,0:T(2,128)(2,1)} %param.11) | copy-start | bytes 688132
  3.0 18.7 %all-to-all-start.1 = ((bf16[8,7,16,128]{3,2,1,0:T(8,128)(2,1)}), bf16[8,7,16,128]{3,2,1,0:T(8,128)(2,1)S(1)}, u32[]{:S(2)}, u32[]{:S(2)}) async-start(bf16[8,7,16,128]{3,2,1,0:T(8,128)(2,1)} %get-tuple-element.17), calls=%async_computation.1 | async-start | bytes 458752 | tf_op jit(solution)/shard_map/all_to_all | solution.py:300
  11.3 5.4 %collective-permute-start = (f32[64,7]{1,0:T(8,128)S(1)}, f32[64,7]{1,0:T(8,128)S(1)}, u32[]{:S(2)}, u32[]{:S(2)}) collective-permute-start(f32[64,7]{1,0:T(8,128)S(1)} %shard_map.114), channel_id=1, source_target_pairs={{0,8},{8,0},{16,24},{24,16},{32,40},{40,32},{48,56},{56,48},{64,72... | collective-permute-start | bytes 5384 | tf_op jit(solution)/shard_map/ppermute | solution.py:313
  16.7 5.1 %copy-start.2 = (bf16[56,56]{1,0:T(8,128)(2,1)S(1)}, bf16[56,56]{1,0:T(8,128)(2,1)}, u32[]{:S(2)}) copy-start(bf16[56,56]{1,0:T(8,128)(2,1)} %matrix_ref.1) | copy-start | bytes 18820
  16.7 5.1 %collective-permute-start.1 = (f32[64,7]{1,0:T(8,128)S(1)}, f32[64,7]{1,0:T(8,128)S(1)}, u32[]{:S(2)}, u32[]{:S(2)}) collective-permute-start(f32[64,7]{1,0:T(8,128)S(1)} %add.17), channel_id=1, source_target_pairs={{0,128},{8,136},{16,144},{24,152},{32,160},{40,168},{48,176},{56,1... | collective-permute-start | bytes 5384 | tf_op jit(solution)/shard_map/ppermute | solution.py:313
  22.9 15.4 %all-to-all-start.2 = ((f16[8,7,16,128]{3,2,1,0:T(8,128)(2,1)}), f16[8,7,16,128]{3,2,1,0:T(8,128)(2,1)S(1)}, u32[]{:S(2)}, u32[]{:S(2)}) async-start(f16[8,7,16,128]{3,2,1,0:T(8,128)(2,1)} %bitcast.22), calls=%async_computation.2 | async-start | bytes 458752 | tf_op jit(solution)/shard_map/all_to_all | solution.py:327
  29.4 6.2 %collective-permute-start.2 = (f32[64,7]{1,0:T(8,128)S(1)}, f32[64,7]{1,0:T(8,128)S(1)}, u32[]{:S(2)}, u32[]{:S(2)}) collective-permute-start(f32[64,7]{1,0:T(8,128)S(1)} %add.18), channel_id=1, source_target_pairs={{0,256},{8,264},{16,272},{24,280},{32,288},{40,296},{48,304},{56,3... | collective-permute-start | bytes 5384 | tf_op jit(solution)/shard_map/ppermute | solution.py:313
  38.8 16.7 %collective-permute-start.3 = (bf16[113,16,128]{2,1,0:T(8,128)(2,1)S(1)}, bf16[113,16,128]{2,1,0:T(8,128)(2,1)S(1)}, u32[]{:S(2)}, u32[]{:S(2)}) collective-permute-start(bf16[113,16,128]{2,1,0:T(8,128)(2,1)S(1)} %get-tuple-element.21), channel_id=1, source_target_pairs={{8,16},{16,8},{24,32},{32,24},{40,48},{48,40},{56,64},{64,56},{72,... | collective-permute-start | bytes 1388552 | tf_op jit(solution)/shard_map/ppermute | solution.py:336
  44.4 11.2 %collective-permute-start.4 = (bf16[113,16,128]{2,1,0:T(8,128)(2,1)S(1)}, bf16[113,16,128]{2,1,0:T(8,128)(2,1)S(1)}, u32[]{:S(2)}, u32[]{:S(2)}) collective-permute-start(bf16[113,16,128]{2,1,0:T(8,128)(2,1)S(1)} %get-tuple-element.21), channel_id=1, source_target_pairs={{0,8},{8,0},{16,24},{24,16},{32,40},{40,32},{48,56},{56,48},{64,72... | collective-permute-start | bytes 1388552 | tf_op jit(solution)/shard_map/ppermute | solution.py:337
  46.3 16.0 %all-to-all-start = ((f32[8,8,7]{2,1,0:T(8,128)}), f32[8,8,7]{2,1,0:T(8,128)S(1)}, u32[]{:S(2)}, u32[]{:S(2)}) async-start(f32[8,8,7]{2,1,0:T(8,128)} %bitcast.18), calls=%async_computation | async-start | bytes 65536 | tf_op jit(solution)/shard_map/all_to_all | solution.py:341

commit v8 on v7

--- a/solution.py
+++ b/solution.py
@@ -85,7 +85,7 @@
             total = total + limiter * uptake_ref[t, k].astype(F32) * grad
         term_ref[pl.ds(t, lines, stride=8), :] = total
     place = lax.broadcasted_iota(jnp.int32, (provinces, LANES), 0)
-    z, x, core = place // (CHIPS_X * CORES), (place // CORES) % CHIPS_X, place % CORES
+    z, x, core = CHIPS_Z - 1 - place // (CHIPS_X * CORES), (place // CORES) % CHIPS_X, place % CORES
     ids = (x * CHIPS_Z + z) * CORES + core
     for s in range(lines):
         line = jnp.broadcast_to(region_ref[s : s + 1, :], (provinces, LANES))
@@ -313,9 +313,8 @@
         return part + lax.ppermute(part, "tile", [(i, i ^ step) for i in range(tiles)])
 
     chip_sum = exchanged(province_part, 1)
-    half_sum = exchanged(chip_sum, CHIPS_Z * CORES)
-    all_tracers, _ = lax.optimization_barrier((all_tracers, half_sum))
-    line_sum = exchanged(half_sum, 2 * CHIPS_Z * CORES)
+    other_half = lax.ppermute(chip_sum, "tile", [(i, i ^ (CHIPS_Z * CORES)) for i in range(tiles)])
+    all_tracers, _ = lax.optimization_barrier((all_tracers, chip_sum))
     fed = call(
         feed_kernel,
         shape((tracers, lines, LANES), F32),
@@ -324,6 +323,10 @@
         [pltpu.VMEM((tracers * lines, LANES), F32), pltpu.VMEM((tracers * lines, LANES), F32)],
     )(uptake_matrix, all_tracers)
     fed = fed.astype(jnp.float16).reshape(sunlit, own, lines, LANES)
+    fed, chip_sum = lax.optimization_barrier((fed, chip_sum))
+    half_sum = chip_sum + other_half
+    fed, half_sum = lax.optimization_barrier((fed, half_sum))
+    line_sum = exchanged(half_sum, 2 * CHIPS_Z * CORES)
     fed = lax.all_to_all(fed, "trc", 0, 0, tiled=True)
     fed, _ = lax.optimization_barrier((fed, line_sum))
     fed = fed.astype(F32)
@@ -336,7 +339,7 @@
     south = lax.ppermute(halo, "tile", across)
     north = lax.ppermute(halo, "tile", within)
     groups = [
-        [(x * CHIPS_Z + z) * CORES + core for z in range(CHIPS_Z)] for x in range(CHIPS_X) for core in range(CORES)
+        [(x * CHIPS_Z + z) * CORES + core for z in reversed(range(CHIPS_Z))] for x in range(CHIPS_X) for core in range(CORES)
     ]
     own_parts = lax.all_to_all(line_sum, "tile", 0, 0, axis_index_groups=groups, tiled=True)
     tracer_grad = call(

time: 63.9 us -> 61.6 us (0.964)
  waiting for transfers between devices: 12.1 us -> 8.57 us
  starting transfers between devices: 40.6 us -> 41.9 us
    ppermute x3 -> x2, waiting for transfers between devices: 6.97 us -> 3.94 us  [exchanged(): lax.ppermute(part, 'tile', [(i, i ^ step) for i in range(tiles)])]
    all_to_all x1, waiting for transfers between devices: 2.98 us -> 0.58 us  [body(): lax.all_to_all(line_sum, 'tile', 0, 0, axis_index_groups=groups, tiled=True)]
    ppermute x3 -> x2, starting transfers between devices: 9.63 us -> 7.59 us  [exchanged(): lax.ppermute(part, 'tile', [(i, i ^ step) for i in range(tiles)])]
    ppermute x0 -> x1, starting transfers between devices: none -> 1.91 us  [body(): lax.ppermute(chip_sum, 'tile', [(i, i ^ CHIPS_Z * CORES) for i in range(t...]
    all_to_all x1, starting transfers between devices: 9.14 us -> 10.6 us  [body(): lax.all_to_all(line_sum, 'tile', 0, 0, axis_index_groups=groups, tiled=True)]
    all_to_all x1, waiting for transfers between devices: 0.01 us -> 1.22 us  [body(): lax.all_to_all(weighted, 'trc', 0, 0, tiled=True)]
    ppermute x0 -> x1, waiting for transfers between devices: none -> 0.71 us  [body(): lax.ppermute(chip_sum, 'tile', [(i, i ^ CHIPS_Z * CORES) for i in range(t...]
  transfers between devices with their start and end apart: 8 -> 8, of which waited for: 5 -> 6; matrix products, arithmetic and copies ran while one was open for 1% -> 2% of each run, Pallas kernels for 7% -> 8%
where the time goes in v8:
time: 61.6 us; the launch traced here: 60.8 us
  starting transfers between devices  41.9 us (68%)
  waiting for transfers between devices  8.57 us (14%)
  Pallas kernels  7.45 us (12%)
  other arithmetic  2 us (3%)
  between operations  0.78 us (1%)
    all_to_all x1, starting transfers between devices, body(): lax.all_to_all(line_sum, 'tile', 0, 0, axis_index_groups=groups, tiled=True)  10.6 us
    all_to_all x1, starting transfers between devices, body(): lax.all_to_all(weighted, 'trc', 0, 0, tiled=True)  7.79 us
    ppermute x2, starting transfers between devices, exchanged(): lax.ppermute(part, 'tile', [(i, i ^ step) for i in range(tiles)])  7.59 us
    all_to_all x1, starting transfers between devices, body(): fed = lax.all_to_all(fed, 'trc', 0, 0, tiled=True)  6.54 us
    ppermute x1, starting transfers between devices, body(): south = lax.ppermute(halo, 'tile', across)  5.56 us
    ppermute x2, waiting for transfers between devices, exchanged(): lax.ppermute(part, 'tile', [(i, i ^ step) for i in range(tiles)])  3.94 us
    pallas_call x1, Pallas kernels, body(): call(mixing_kernel, shape((own * levels * lines, LANES), F32), [VMEM] * 5...  3.77 us
    pallas_call x1, Pallas kernels, body(): call(weighted_kernel, (shape((sunlit, own, lines, LANES), BF16), shape((3...  2.34 us
  transfers between devices with their start and end apart: 8, of which 6 were waited for; matrix products, arithmetic and copies ran while one was open for 2% of the time, Pallas kernels for 8%

profile of v8, /device:TPU:1, one launch (start us, length us, event | category | flops | bytes accessed | tf_op | source)
XLA Modules:
  0.0 60.8 jit_solution(10452457813392833813)
XLA Ops:
  0.6 2.3 %shard_map.113 = (bf16[8,7,16,128]{3,2,1,0:T(8,128)(2,1)}, f32[24,128]{1,0:T(8,128)S(1)}, f32[8,16,128]{2,1,0:T(8,128)S(1)}, s32[16,128]{1,0:T(8,128)S(1)}, s32[16,128]{1,0:T(8,128)S(1)}) custom-call(f32[7,16,16,128]{3,2,1,0:T(8,128)} %bitcast.41, f32[8,16,128]{2,1,0:T(8,128)} %bitcast.48, s32[16,128]{1,0:T(8,128)} %bitcast.49, s32[16,128]{1,0:T(8,128)} %bitcast.50, ...), custom_call_target="tpu_custom_call" | custom-call | tf_op jit(solution)/shard_map/pallas_call | solution.py:277
  3.0 0.0 copy-start.1
  3.0 7.8 %all-to-all-start = ((bf16[8,7,16,128]{3,2,1,0:T(8,128)(2,1)}), bf16[8,7,16,128]{3,2,1,0:T(8,128)(2,1)S(1)}, u32[]{:S(2)}, u32[]{:S(2)}) async-start(bf16[8,7,16,128]{3,2,1,0:T(8,128)(2,1)} %get-tuple-element.17), calls=%async_computation | async-start | bytes 458752 | tf_op jit(solution)/shard_map/all_to_all | solution.py:300
  10.8 0.4 shard_map.114
  11.3 4.6 %collective-permute-start = (f32[64,7]{1,0:T(8,128)S(1)}, f32[64,7]{1,0:T(8,128)S(1)}, u32[]{:S(2)}, u32[]{:S(2)}) collective-permute-start(f32[64,7]{1,0:T(8,128)S(1)} %shard_map.114), channel_id=1, source_target_pairs={{0,8},{8,0},{16,24},{24,16},{32,40},{40,32},{48,56},{56,48},{64,72... | collective-permute-start | bytes 5384 | tf_op jit(solution)/shard_map/ppermute | solution.py:313
  15.8 0.8 %collective-permute-done = f32[64,7]{1,0:T(8,128)S(1)} collective-permute-done((f32[64,7]{1,0:T(8,128)S(1)}, f32[64,7]{1,0:T(8,128)S(1)}, u32[]{:S(2)}, u32[]{:S(2)}) %collective-permute-start) | collective-permute-done | bytes 1824 | tf_op jit(solution)/shard_map/ppermute | solution.py:313
  16.7 1.9 %collective-permute-start.1 = (f32[64,7]{1,0:T(8,128)S(1)}, f32[64,7]{1,0:T(8,128)S(1)}, u32[]{:S(2)}, u32[]{:S(2)}) collective-permute-start(f32[64,7]{1,0:T(8,128)S(1)} %add.17), channel_id=1, source_target_pairs={{0,128},{8,136},{16,144},{24,152},{32,160},{40,168},{48,176},{56,1... | collective-permute-start | bytes 5384 | tf_op jit(solution)/shard_map/ppermute | solution.py:316
  18.6 1.2 %all-to-all-done = bf16[8,7,16,128]{3,2,1,0:T(8,128)(2,1)S(1)} async-done(((bf16[8,7,16,128]{3,2,1,0:T(8,128)(2,1)}), bf16[8,7,16,128]{3,2,1,0:T(8,128)(2,1)S(1)}, u32[]{:S(2)}, u32[]{:S(2)}) %all-to-all-start) | async-done | bytes 229408 | tf_op jit(solution)/shard_map/all_to_all | solution.py:300
  19.8 0.4 shard_map.115
  20.2 0.7 %convert_element_type.4 = f16[56,16,128]{2,1,0:T(8,128)(2,1)} convert(f32[56,16,128]{2,1,0:T(8,128)S(1)} %shard_map.115) | non-fusion elementwise | flops 114688 | bytes 688128 | tf_op jit(solution)/shard_map/convert_element_type | solution.py:325
  20.9 0.7 %collective-permute-done.1 = f32[64,7]{1,0:T(8,128)S(1)} collective-permute-done((f32[64,7]{1,0:T(8,128)S(1)}, f32[64,7]{1,0:T(8,128)S(1)}, u32[]{:S(2)}, u32[]{:S(2)}) %collective-permute-start.1) | collective-permute-done | bytes 1824 | tf_op jit(solution)/shard_map/ppermute | solution.py:316
  21.6 6.5 %all-to-all-start.2 = ((f16[8,7,16,128]{3,2,1,0:T(8,128)(2,1)}), f16[8,7,16,128]{3,2,1,0:T(8,128)(2,1)S(1)}, u32[]{:S(2)}, u32[]{:S(2)}) async-start(f16[8,7,16,128]{3,2,1,0:T(8,128)(2,1)} %bitcast.19), calls=%async_computation.2 | async-start | bytes 458752 | tf_op jit(solution)/shard_map/all_to_all | solution.py:330
  28.2 3.0 %collective-permute-start.2 = (f32[64,7]{1,0:T(8,128)S(1)}, f32[64,7]{1,0:T(8,128)S(1)}, u32[]{:S(2)}, u32[]{:S(2)}) collective-permute-start(f32[64,7]{1,0:T(8,128)S(1)} %add.18), channel_id=1, source_target_pairs={{0,256},{8,264},{16,272},{24,280},{32,288},{40,296},{48,304},{56,3... | collective-permute-start | bytes 5384 | tf_op jit(solution)/shard_map/ppermute | solution.py:313
  31.2 3.1 %collective-permute-done.2 = f32[64,7]{1,0:T(8,128)S(1)} collective-permute-done((f32[64,7]{1,0:T(8,128)S(1)}, f32[64,7]{1,0:T(8,128)S(1)}, u32[]{:S(2)}, u32[]{:S(2)}) %collective-permute-start.2) | collective-permute-done | bytes 1824 | tf_op jit(solution)/shard_map/ppermute | solution.py:313
  34.3 0.6 %add.19 = f32[64,7]{1,0:T(8,128)} add(f32[64,7]{1,0:T(8,128)S(1)} %add.18, f32[64,7]{1,0:T(8,128)S(1)} %collective-permute-done.2) | non-fusion elementwise | flops 448 | bytes 5376 | tf_op jit(solution)/shard_map/add | solution.py:313
  34.9 2.1 %all-to-all-done.2 = f16[8,7,16,128]{3,2,1,0:T(8,128)(2,1)S(1)} async-done(((f16[8,7,16,128]{3,2,1,0:T(8,128)(2,1)}), f16[8,7,16,128]{3,2,1,0:T(8,128)(2,1)S(1)}, u32[]{:S(2)}, u32[]{:S(2)}) %all-to-all-start.2) | async-done | bytes 229408 | tf_op jit(solution)/shard_map/all_to_all | solution.py:330
  37.1 0.5 shard_map.116
  37.6 5.6 %collective-permute-start.3 = (bf16[113,16,128]{2,1,0:T(8,128)(2,1)S(1)}, bf16[113,16,128]{2,1,0:T(8,128)(2,1)S(1)}, u32[]{:S(2)}, u32[]{:S(2)}) collective-permute-start(bf16[113,16,128]{2,1,0:T(8,128)(2,1)S(1)} %get-tuple-element.29), channel_id=1, source_target_pairs={{8,16},{16,8},{24,32},{32,24},{40,48},{48,40},{56,64},{64,56},{72,... | collective-permute-start | bytes 1388552 | tf_op jit(solution)/shard_map/ppermute | solution.py:339
  43.2 1.9 %collective-permute-start.4 = (bf16[113,16,128]{2,1,0:T(8,128)(2,1)S(1)}, bf16[113,16,128]{2,1,0:T(8,128)(2,1)S(1)}, u32[]{:S(2)}, u32[]{:S(2)}) collective-permute-start(bf16[113,16,128]{2,1,0:T(8,128)(2,1)S(1)} %get-tuple-element.29), channel_id=1, source_target_pairs={{0,8},{8,0},{16,24},{24,16},{32,40},{40,32},{48,56},{56,48},{64,72... | collective-permute-start | bytes 1388552 | tf_op jit(solution)/shard_map/ppermute | solution.py:340
  45.1 10.6 %all-to-all-start.1 = ((f32[8,8,7]{2,1,0:T(8,128)}), f32[8,8,7]{2,1,0:T(8,128)S(1)}, u32[]{:S(2)}, u32[]{:S(2)}) async-start(f32[8,8,7]{2,1,0:T(8,128)} %bitcast.20), calls=%async_computation.1 | async-start | bytes 65536 | tf_op jit(solution)/shard_map/all_to_all | solution.py:344
  55.8 0.1 iota.12
  55.9 3.8 %shard_map.117 = f32[1792,128]{1,0:T(8,128)} custom-call(f32[112,16,128]{2,1,0:T(8,128)S(1)} %get-tuple-element.28.col_ref, bf16[113,16,128]{2,1,0:T(8,128)(2,1)S(1)} %collective-permute-done.3.south_ref, bf16[113,16,128]{2,1,0:T(8,128)(2,1)S(1)} %collective-permute-done.4.north_ref, s32[16,128]{1,0:T(8,128)S(1)} %get-tuple-element.19.depth_ref, ...), custom_call_target="tpu_custom_call" | custom-call | flops 1000000 | bytes 2000000 | tf_op jit(solution)/shard_map/pallas_call | solution.py:345
  59.6 0.6 all-to-all-done.1
  60.2 0.6 select_reduce_fusion
  (12 shorter events, 0.1 us)
Async XLA Ops:
  0.6 10.2 %copy-start = (f32[7,16,2,1024]{3,2,1,0:T(2,128)S(1)}, f32[7,16,2,1024]{3,2,1,0:T(2,128)}, u32[]{:S(2)}) copy-start(f32[7,16,2,1024]{3,2,1,0:T(2,128)} %param.10) | copy-start | bytes 2752516
  3.0 7.8 %copy-start.1 = (bf16[7,8,2,1024]{3,2,1,0:T(2,128)(2,1)S(1)}, bf16[7,8,2,1024]{3,2,1,0:T(2,128)(2,1)}, u32[]{:S(2)}) copy-start(bf16[7,8,2,1024]{3,2,1,0:T(2,128)(2,1)} %param.11) | copy-start | bytes 688132
  3.0 16.8 %all-to-all-start = ((bf16[8,7,16,128]{3,2,1,0:T(8,128)(2,1)}), bf16[8,7,16,128]{3,2,1,0:T(8,128)(2,1)S(1)}, u32[]{:S(2)}, u32[]{:S(2)}) async-start(bf16[8,7,16,128]{3,2,1,0:T(8,128)(2,1)} %get-tuple-element.17), calls=%async_computation | async-start | bytes 458752 | tf_op jit(solution)/shard_map/all_to_all | solution.py:300
  11.3 8.6 %copy-start.2 = (bf16[56,56]{1,0:T(8,128)(2,1)S(1)}, bf16[56,56]{1,0:T(8,128)(2,1)}, u32[]{:S(2)}) copy-start(bf16[56,56]{1,0:T(8,128)(2,1)} %matrix_ref.1) | copy-start | bytes 18820
  11.3 5.4 %collective-permute-start = (f32[64,7]{1,0:T(8,128)S(1)}, f32[64,7]{1,0:T(8,128)S(1)}, u32[]{:S(2)}, u32[]{:S(2)}) collective-permute-start(f32[64,7]{1,0:T(8,128)S(1)} %shard_map.114), channel_id=1, source_target_pairs={{0,8},{8,0},{16,24},{24,16},{32,40},{40,32},{48,56},{56,48},{64,72... | collective-permute-start | bytes 5384 | tf_op jit(solution)/shard_map/ppermute | solution.py:313
  16.7 4.9 %collective-permute-start.1 = (f32[64,7]{1,0:T(8,128)S(1)}, f32[64,7]{1,0:T(8,128)S(1)}, u32[]{:S(2)}, u32[]{:S(2)}) collective-permute-start(f32[64,7]{1,0:T(8,128)S(1)} %add.17), channel_id=1, source_target_pairs={{0,128},{8,136},{16,144},{24,152},{32,160},{40,168},{48,176},{56,1... | collective-permute-start | bytes 5384 | tf_op jit(solution)/shard_map/ppermute | solution.py:316
  21.6 15.4 %all-to-all-start.2 = ((f16[8,7,16,128]{3,2,1,0:T(8,128)(2,1)}), f16[8,7,16,128]{3,2,1,0:T(8,128)(2,1)S(1)}, u32[]{:S(2)}, u32[]{:S(2)}) async-start(f16[8,7,16,128]{3,2,1,0:T(8,128)(2,1)} %bitcast.19), calls=%async_computation.2 | async-start | bytes 458752 | tf_op jit(solution)/shard_map/all_to_all | solution.py:330
  28.2 6.2 %collective-permute-start.2 = (f32[64,7]{1,0:T(8,128)S(1)}, f32[64,7]{1,0:T(8,128)S(1)}, u32[]{:S(2)}, u32[]{:S(2)}) collective-permute-start(f32[64,7]{1,0:T(8,128)S(1)} %add.18), channel_id=1, source_target_pairs={{0,256},{8,264},{16,272},{24,280},{32,288},{40,296},{48,304},{56,3... | collective-permute-start | bytes 5384 | tf_op jit(solution)/shard_map/ppermute | solution.py:313
  37.6 18.2 %collective-permute-start.3 = (bf16[113,16,128]{2,1,0:T(8,128)(2,1)S(1)}, bf16[113,16,128]{2,1,0:T(8,128)(2,1)S(1)}, u32[]{:S(2)}, u32[]{:S(2)}) collective-permute-start(bf16[113,16,128]{2,1,0:T(8,128)(2,1)S(1)} %get-tuple-element.29), channel_id=1, source_target_pairs={{8,16},{16,8},{24,32},{32,24},{40,48},{48,40},{56,64},{64,56},{72,... | collective-permute-start | bytes 1388552 | tf_op jit(solution)/shard_map/ppermute | solution.py:339
  43.2 12.7 %collective-permute-start.4 = (bf16[113,16,128]{2,1,0:T(8,128)(2,1)S(1)}, bf16[113,16,128]{2,1,0:T(8,128)(2,1)S(1)}, u32[]{:S(2)}, u32[]{:S(2)}) collective-permute-start(bf16[113,16,128]{2,1,0:T(8,128)(2,1)S(1)} %get-tuple-element.29), channel_id=1, source_target_pairs={{0,8},{8,0},{16,24},{24,16},{32,40},{40,32},{48,56},{56,48},{64,72... | collective-permute-start | bytes 1388552 | tf_op jit(solution)/shard_map/ppermute | solution.py:340
  45.1 15.1 %all-to-all-start.1 = ((f32[8,8,7]{2,1,0:T(8,128)}), f32[8,8,7]{2,1,0:T(8,128)S(1)}, u32[]{:S(2)}, u32[]{:S(2)}) async-start(f32[8,8,7]{2,1,0:T(8,128)} %bitcast.20), calls=%async_computation.1 | async-start | bytes 65536 | tf_op jit(solution)/shard_map/all_to_all | solution.py:344

commit v9 on v8

--- a/solution.py
+++ b/solution.py
@@ -69,8 +69,13 @@
         copy.wait()
 
 
-def province_kernel(cot_ref, uptake_ref, nutrient_ref, depth_ref, region_ref, params_ref, out_ref, hot_ref, term_ref, parts_ref):
+def province_kernel(cot_ref, uptake_ref, nutrient_ref, depth_ref, region_ref, params_ref, matrix_ref, out_ref, turned_ref, hot_ref, term_ref, parts_ref):
     provinces, own = out_ref.shape
+
+    def reversed_blocks(m):
+        return jnp.concatenate([m[i : i + own] for i in range(m.shape[0] - own, -1, -own)], axis=0)
+
+    turned_ref[...] = reversed_blocks(reversed_blocks(matrix_ref[...].astype(F32)).T).astype(BF16)
     sunlit = nutrient_ref.shape[0]
     lines = depth_ref.shape[0]
     depth = depth_ref[...]
@@ -101,7 +106,7 @@
 
 def feed_kernel(matrix_ref, weighted_ref, out_ref, wide_ref, fed_ref):
     tracers, lines = weighted_ref.shape[0], weighted_ref.shape[1]
-    matrix = matrix_ref[...].astype(F32).T.astype(BF16)
+    matrix = matrix_ref[...]
     for t in range(tracers):
         wide_ref[t * lines : (t + 1) * lines, :] = weighted_ref[t].astype(F32)
     for s in range(0, lines, 2):
@@ -297,18 +302,19 @@
         ],
         None,
     )(*(pltpu.with_memory_space_constraint(a, pltpu.HBM) for a in inputs))
-    all_tracers = lax.all_to_all(weighted, "trc", 0, 0, tiled=True).reshape(tracers, lines, LANES)
-    province_part = call(
+    order_y = [list(reversed(range(lax.axis_size("trc"))))]
+    all_tracers = lax.all_to_all(weighted, "trc", 0, 0, axis_index_groups=order_y, tiled=True).reshape(tracers, lines, LANES)
+    province_part, turned = call(
         province_kernel,
-        shape((provinces, own), F32),
-        [VMEM] * 6,
-        VMEM,
+        (shape((provinces, own), F32), shape(uptake_matrix.shape, BF16)),
+        [VMEM] * 7,
+        (VMEM,) * 2,
         [
             pltpu.VMEM((provinces, columns), BF16),
             pltpu.VMEM((lines * SUB, LANES), F32),
             pltpu.VMEM((2 * SUB, columns), BF16),
         ],
-    )(cot, uptake, nutrient, depth, region, params)
+    )(cot, uptake, nutrient, depth, region, params, uptake_matrix)
     def exchanged(part, step):
         return part + lax.ppermute(part, "tile", [(i, i ^ step) for i in range(tiles)])
 
@@ -321,13 +327,13 @@
         [VMEM, VMEM],
         VMEM,
         [pltpu.VMEM((tracers * lines, LANES), F32), pltpu.VMEM((tracers * lines, LANES), F32)],
-    )(uptake_matrix, all_tracers)
+    )(turned, all_tracers)
     fed = fed.astype(jnp.float16).reshape(sunlit, own, lines, LANES)
     fed, chip_sum = lax.optimization_barrier((fed, chip_sum))
     half_sum = chip_sum + other_half
     fed, half_sum = lax.optimization_barrier((fed, half_sum))
     line_sum = exchanged(half_sum, 2 * CHIPS_Z * CORES)
-    fed = lax.all_to_all(fed, "trc", 0, 0, tiled=True)
+    fed = lax.all_to_all(fed, "trc", 0, 0, axis_index_groups=order_y, tiled=True)
     fed, _ = lax.optimization_barrier((fed, line_sum))
     fed = fed.astype(F32)
     col, halo = call(

time: 61.6 us -> 59.7 us (0.969)
  waiting for transfers between devices: 8.57 us -> 7.06 us
    all_to_all x2, waiting for transfers between devices: 3.34 us -> 0.01 us  [the longest x1 0.01 us: body(): lax.all_to_all(weighted, 'trc', 0, 0, axis_index_groups=order_y, tiled=True)]
    ppermute x1, starting transfers between devices: 5.56 us -> 4.58 us  [body(): south = lax.ppermute(halo, 'tile', across)]
    ppermute x2, waiting for transfers between devices: 3.94 us -> 4.86 us  [exchanged(): lax.ppermute(part, 'tile', [(i, i ^ step) for i in range(tiles)])]
    ppermute x1, waiting for transfers between devices: 0.71 us -> 1.61 us  [body(): lax.ppermute(chip_sum, 'tile', [(i, i ^ CHIPS_Z * CORES) for i in range(t...]
  transfers between devices with their start and end apart: 8 -> 8, of which waited for: 6 -> 4; matrix products, arithmetic and copies ran while one was open for 2% -> 2% of each run, Pallas kernels for 8% -> 8%
where the time goes in v9:
time: 59.7 us; the launch traced here: 59 us
  starting transfers between devices  41.5 us (70%)
  Pallas kernels  7.49 us (13%)
  waiting for transfers between devices  7.06 us (12%)
  other arithmetic  2 us (3%)
  between operations  0.79 us (1%)
    all_to_all x1, starting transfers between devices, body(): lax.all_to_all(line_sum, 'tile', 0, 0, axis_index_groups=groups, tiled=True)  10.6 us
    all_to_all x1, starting transfers between devices, body(): lax.all_to_all(weighted, 'trc', 0, 0, axis_index_groups=order_y, tiled=True)  8.08 us
    ppermute x2, starting transfers between devices, exchanged(): lax.ppermute(part, 'tile', [(i, i ^ step) for i in range(tiles)])  7.78 us
    all_to_all x1, starting transfers between devices, body(): lax.all_to_all(fed, 'trc', 0, 0, axis_index_groups=order_y, tiled=True)  6.65 us
    ppermute x2, waiting for transfers between devices, exchanged(): lax.ppermute(part, 'tile', [(i, i ^ step) for i in range(tiles)])  4.86 us
    ppermute x1, starting transfers between devices, body(): south = lax.ppermute(halo, 'tile', across)  4.58 us
    pallas_call x1, Pallas kernels, body(): call(mixing_kernel, shape((own * levels * lines, LANES), F32), [VMEM] * 5...  3.77 us
    pallas_call x1, Pallas kernels, body(): call(weighted_kernel, (shape((sunlit, own, lines, LANES), BF16), shape((3...  2.34 us
  transfers between devices with their start and end apart: 8, of which 4 were waited for; matrix products, arithmetic and copies ran while one was open for 2% of the time, Pallas kernels for 8%

profile of v9, /device:TPU:1, one launch (start us, length us, event | category | flops | bytes accessed | tf_op | source)
XLA Modules:
  0.0 59.0 jit_solution(6768376626215858795)
XLA Ops:
  0.6 2.3 %shard_map.113 = (bf16[8,7,16,128]{3,2,1,0:T(8,128)(2,1)}, f32[24,128]{1,0:T(8,128)S(1)}, f32[8,16,128]{2,1,0:T(8,128)S(1)}, s32[16,128]{1,0:T(8,128)S(1)}, s32[16,128]{1,0:T(8,128)S(1)}) custom-call(f32[7,16,16,128]{3,2,1,0:T(8,128)} %bitcast.41, f32[8,16,128]{2,1,0:T(8,128)} %bitcast.48, s32[16,128]{1,0:T(8,128)} %bitcast.49, s32[16,128]{1,0:T(8,128)} %bitcast.50, ...), custom_call_target="tpu_custom_call" | custom-call | tf_op jit(solution)/shard_map/pallas_call | solution.py:282
  3.0 0.0 copy-start.1
  3.0 0.0 copy-start.2
  3.0 8.1 %all-to-all-start = ((bf16[8,7,16,128]{3,2,1,0:T(8,128)(2,1)}), bf16[8,7,16,128]{3,2,1,0:T(8,128)(2,1)S(1)}, u32[]{:S(2)}, u32[]{:S(2)}) async-start(bf16[8,7,16,128]{3,2,1,0:T(8,128)(2,1)} %get-tuple-element.24), calls=%async_computation | async-start | bytes 458752 | tf_op jit(solution)/shard_map/all_to_all | solution.py:306
  11.1 0.5 shard_map.114
  11.6 5.4 %collective-permute-start = (f32[64,7]{1,0:T(8,128)S(1)}, f32[64,7]{1,0:T(8,128)S(1)}, u32[]{:S(2)}, u32[]{:S(2)}) collective-permute-start(f32[64,7]{1,0:T(8,128)S(1)} %get-tuple-element.25), channel_id=1, source_target_pairs={{0,8},{8,0},{16,24},{24,16},{32,40},{40,32},{48,56},{56,48},{64,72... | collective-permute-start | bytes 5384 | tf_op jit(solution)/shard_map/ppermute | solution.py:319
  17.0 0.8 %collective-permute-done = f32[64,7]{1,0:T(8,128)S(1)} collective-permute-done((f32[64,7]{1,0:T(8,128)S(1)}, f32[64,7]{1,0:T(8,128)S(1)}, u32[]{:S(2)}, u32[]{:S(2)}) %collective-permute-start) | collective-permute-done | bytes 1824 | tf_op jit(solution)/shard_map/ppermute | solution.py:319
  17.8 1.9 %collective-permute-start.1 = (f32[64,7]{1,0:T(8,128)S(1)}, f32[64,7]{1,0:T(8,128)S(1)}, u32[]{:S(2)}, u32[]{:S(2)}) collective-permute-start(f32[64,7]{1,0:T(8,128)S(1)} %add.17), channel_id=1, source_target_pairs={{0,128},{8,136},{16,144},{24,152},{32,160},{40,168},{48,176},{56,1... | collective-permute-start | bytes 5384 | tf_op jit(solution)/shard_map/ppermute | solution.py:322
  19.7 0.4 shard_map.115
  20.1 0.7 %convert_element_type.4 = f16[56,16,128]{2,1,0:T(8,128)(2,1)} convert(f32[56,16,128]{2,1,0:T(8,128)S(1)} %shard_map.115) | non-fusion elementwise | flops 114688 | bytes 688128 | tf_op jit(solution)/shard_map/convert_element_type | solution.py:331
  20.8 1.6 %collective-permute-done.1 = f32[64,7]{1,0:T(8,128)S(1)} collective-permute-done((f32[64,7]{1,0:T(8,128)S(1)}, f32[64,7]{1,0:T(8,128)S(1)}, u32[]{:S(2)}, u32[]{:S(2)}) %collective-permute-start.1) | collective-permute-done | bytes 1824 | tf_op jit(solution)/shard_map/ppermute | solution.py:322
  22.5 6.6 %all-to-all-start.2 = ((f16[8,7,16,128]{3,2,1,0:T(8,128)(2,1)}), f16[8,7,16,128]{3,2,1,0:T(8,128)(2,1)S(1)}, u32[]{:S(2)}, u32[]{:S(2)}) async-start(f16[8,7,16,128]{3,2,1,0:T(8,128)(2,1)} %bitcast.19), calls=%async_computation.2 | async-start | bytes 458752 | tf_op jit(solution)/shard_map/all_to_all | solution.py:336
  29.1 2.4 %collective-permute-start.2 = (f32[64,7]{1,0:T(8,128)S(1)}, f32[64,7]{1,0:T(8,128)S(1)}, u32[]{:S(2)}, u32[]{:S(2)}) collective-permute-start(f32[64,7]{1,0:T(8,128)S(1)} %add.18), channel_id=1, source_target_pairs={{0,256},{8,264},{16,272},{24,280},{32,288},{40,296},{48,304},{56,3... | collective-permute-start | bytes 5384 | tf_op jit(solution)/shard_map/ppermute | solution.py:319
  31.5 4.0 %collective-permute-done.2 = f32[64,7]{1,0:T(8,128)S(1)} collective-permute-done((f32[64,7]{1,0:T(8,128)S(1)}, f32[64,7]{1,0:T(8,128)S(1)}, u32[]{:S(2)}, u32[]{:S(2)}) %collective-permute-start.2) | collective-permute-done | bytes 1824 | tf_op jit(solution)/shard_map/ppermute | solution.py:319
  35.6 0.6 %add.19 = f32[64,7]{1,0:T(8,128)} add(f32[64,7]{1,0:T(8,128)S(1)} %add.18, f32[64,7]{1,0:T(8,128)S(1)} %collective-permute-done.2) | non-fusion elementwise | flops 448 | bytes 5376 | tf_op jit(solution)/shard_map/add | solution.py:319
  36.2 0.5 shard_map.116
  36.8 4.6 %collective-permute-start.3 = (bf16[113,16,128]{2,1,0:T(8,128)(2,1)S(1)}, bf16[113,16,128]{2,1,0:T(8,128)(2,1)S(1)}, u32[]{:S(2)}, u32[]{:S(2)}) collective-permute-start(bf16[113,16,128]{2,1,0:T(8,128)(2,1)S(1)} %get-tuple-element.33), channel_id=1, source_target_pairs={{8,16},{16,8},{24,32},{32,24},{40,48},{48,40},{56,64},{64,56},{72,... | collective-permute-start | bytes 1388552 | tf_op jit(solution)/shard_map/ppermute | solution.py:345
  41.3 1.9 %collective-permute-start.4 = (bf16[113,16,128]{2,1,0:T(8,128)(2,1)S(1)}, bf16[113,16,128]{2,1,0:T(8,128)(2,1)S(1)}, u32[]{:S(2)}, u32[]{:S(2)}) collective-permute-start(bf16[113,16,128]{2,1,0:T(8,128)(2,1)S(1)} %get-tuple-element.33), channel_id=1, source_target_pairs={{0,8},{8,0},{16,24},{24,16},{32,40},{40,32},{48,56},{56,48},{64,72... | collective-permute-start | bytes 1388552 | tf_op jit(solution)/shard_map/ppermute | solution.py:346
  43.3 10.6 %all-to-all-start.1 = ((f32[8,8,7]{2,1,0:T(8,128)}), f32[8,8,7]{2,1,0:T(8,128)S(1)}, u32[]{:S(2)}, u32[]{:S(2)}) async-start(f32[8,8,7]{2,1,0:T(8,128)} %bitcast.20), calls=%async_computation.1 | async-start | bytes 65536 | tf_op jit(solution)/shard_map/all_to_all | solution.py:350
  53.9 0.1 iota.12
  54.0 0.0 collective-permute-done.3.south_ref
  54.0 3.8 %shard_map.117 = f32[1792,128]{1,0:T(8,128)} custom-call(f32[112,16,128]{2,1,0:T(8,128)S(1)} %get-tuple-element.32.col_ref, bf16[113,16,128]{2,1,0:T(8,128)(2,1)S(1)} %collective-permute-done.3.south_ref, bf16[113,16,128]{2,1,0:T(8,128)(2,1)S(1)} %collective-permute-done.4.north_ref, s32[16,128]{1,0:T(8,128)S(1)} %get-tuple-element.20.depth_ref, ...), custom_call_target="tpu_custom_call" | custom-call | flops 1000000 | bytes 2000000 | tf_op jit(solution)/shard_map/pallas_call | solution.py:351
  57.8 0.6 all-to-all-done.1
  58.4 0.6 %select_reduce_fusion = f32[7]{0:T(128)} fusion(f32[64,7]{1,0:T(8,128)S(1)} %bitcast.47, pred[64]{0:T(512)(128)(4,1)S(1)} %iota.12), kind=kLoop, calls=%fused_computation.1 | loop fusion | flops 889 | bytes 1884 | tf_op jit(solution)/shard_map/reduce_sum | solution.py:369
  (12 shorter events, 0.1 us)
Async XLA Ops:
  0.6 10.5 %copy-start = (f32[7,16,2,1024]{3,2,1,0:T(2,128)S(1)}, f32[7,16,2,1024]{3,2,1,0:T(2,128)}, u32[]{:S(2)}) copy-start(f32[7,16,2,1024]{3,2,1,0:T(2,128)} %param.10) | copy-start | bytes 2752516
  3.0 8.1 %copy-start.1 = (bf16[7,8,2,1024]{3,2,1,0:T(2,128)(2,1)S(1)}, bf16[7,8,2,1024]{3,2,1,0:T(2,128)(2,1)}, u32[]{:S(2)}) copy-start(bf16[7,8,2,1024]{3,2,1,0:T(2,128)(2,1)} %param.11) | copy-start | bytes 688132
  3.0 8.1 %copy-start.2 = (bf16[56,56]{1,0:T(8,128)(2,1)S(1)}, bf16[56,56]{1,0:T(8,128)(2,1)}, u32[]{:S(2)}) copy-start(bf16[56,56]{1,0:T(8,128)(2,1)} %matrix_ref.1) | copy-start | bytes 18820
  3.0 16.7 %all-to-all-start = ((bf16[8,7,16,128]{3,2,1,0:T(8,128)(2,1)}), bf16[8,7,16,128]{3,2,1,0:T(8,128)(2,1)S(1)}, u32[]{:S(2)}, u32[]{:S(2)}) async-start(bf16[8,7,16,128]{3,2,1,0:T(8,128)(2,1)} %get-tuple-element.24), calls=%async_computation | async-start | bytes 458752 | tf_op jit(solution)/shard_map/all_to_all | solution.py:306
  11.6 6.2 %collective-permute-start = (f32[64,7]{1,0:T(8,128)S(1)}, f32[64,7]{1,0:T(8,128)S(1)}, u32[]{:S(2)}, u32[]{:S(2)}) collective-permute-start(f32[64,7]{1,0:T(8,128)S(1)} %get-tuple-element.25), channel_id=1, source_target_pairs={{0,8},{8,0},{16,24},{24,16},{32,40},{40,32},{48,56},{56,48},{64,72... | collective-permute-start | bytes 5384 | tf_op jit(solution)/shard_map/ppermute | solution.py:319
  17.8 4.6 %collective-permute-start.1 = (f32[64,7]{1,0:T(8,128)S(1)}, f32[64,7]{1,0:T(8,128)S(1)}, u32[]{:S(2)}, u32[]{:S(2)}) collective-permute-start(f32[64,7]{1,0:T(8,128)S(1)} %add.17), channel_id=1, source_target_pairs={{0,128},{8,136},{16,144},{24,152},{32,160},{40,168},{48,176},{56,1... | collective-permute-start | bytes 5384 | tf_op jit(solution)/shard_map/ppermute | solution.py:322
  22.5 13.7 %all-to-all-start.2 = ((f16[8,7,16,128]{3,2,1,0:T(8,128)(2,1)}), f16[8,7,16,128]{3,2,1,0:T(8,128)(2,1)S(1)}, u32[]{:S(2)}, u32[]{:S(2)}) async-start(f16[8,7,16,128]{3,2,1,0:T(8,128)(2,1)} %bitcast.19), calls=%async_computation.2 | async-start | bytes 458752 | tf_op jit(solution)/shard_map/all_to_all | solution.py:336
  29.1 6.4 %collective-permute-start.2 = (f32[64,7]{1,0:T(8,128)S(1)}, f32[64,7]{1,0:T(8,128)S(1)}, u32[]{:S(2)}, u32[]{:S(2)}) collective-permute-start(f32[64,7]{1,0:T(8,128)S(1)} %add.18), channel_id=1, source_target_pairs={{0,256},{8,264},{16,272},{24,280},{32,288},{40,296},{48,304},{56,3... | collective-permute-start | bytes 5384 | tf_op jit(solution)/shard_map/ppermute | solution.py:319
  36.8 17.2 %collective-permute-start.3 = (bf16[113,16,128]{2,1,0:T(8,128)(2,1)S(1)}, bf16[113,16,128]{2,1,0:T(8,128)(2,1)S(1)}, u32[]{:S(2)}, u32[]{:S(2)}) collective-permute-start(bf16[113,16,128]{2,1,0:T(8,128)(2,1)S(1)} %get-tuple-element.33), channel_id=1, source_target_pairs={{8,16},{16,8},{24,32},{32,24},{40,48},{48,40},{56,64},{64,56},{72,... | collective-permute-start | bytes 1388552 | tf_op jit(solution)/shard_map/ppermute | solution.py:345
  41.3 12.7 %collective-permute-start.4 = (bf16[113,16,128]{2,1,0:T(8,128)(2,1)S(1)}, bf16[113,16,128]{2,1,0:T(8,128)(2,1)S(1)}, u32[]{:S(2)}, u32[]{:S(2)}) collective-permute-start(bf16[113,16,128]{2,1,0:T(8,128)(2,1)S(1)} %get-tuple-element.33), channel_id=1, source_target_pairs={{0,8},{8,0},{16,24},{24,16},{32,40},{40,32},{48,56},{56,48},{64,72... | collective-permute-start | bytes 1388552 | tf_op jit(solution)/shard_map/ppermute | solution.py:346
  43.3 15.1 %all-to-all-start.1 = ((f32[8,8,7]{2,1,0:T(8,128)}), f32[8,8,7]{2,1,0:T(8,128)S(1)}, u32[]{:S(2)}, u32[]{:S(2)}) async-start(f32[8,8,7]{2,1,0:T(8,128)} %bitcast.20), calls=%async_computation.1 | async-start | bytes 65536 | tf_op jit(solution)/shard_map/all_to_all | solution.py:350

commit v10 on v9

--- a/solution.py
+++ b/solution.py
@@ -38,14 +38,16 @@
         (depth_hbm, depth_ref), (region_hbm, region_ref), (rates_hbm, rates_ref), (nutrient_hbm, nutrient_ref),
         (half_hbm, half_ref), (sinking_hbm, sinking_ref), (mixing_hbm, mixing_ref),
     ]
-    pairs += [(cot_hbm.at[t, 0:sunlit], cot_ref.at[t]) for t in range(own)]
+    cuts = [(0, 3), (3, own)]
+    pairs += [(cot_hbm.at[a:b, 0:sunlit], cot_ref.at[a:b]) for a, b in cuts]
     copies = [pltpu.make_async_copy(here, there, sems.at[n]) for n, (here, there) in enumerate(pairs)]
     for copy in copies:
         copy.start()
-    for copy in copies[: len(pairs) - own]:
+    for copy in copies[: -len(cuts)]:
         copy.wait()
     depth = [row(depth_ref, r) for r in range(ROWS)]
     region = [row(region_ref, r) for r in range(ROWS)]
+    outs = []
     rest = jnp.zeros((1, LANES - rates_ref.shape[1]), F32)
     for t in range(own):
         line = jnp.concatenate([rates_ref[t : t + 1, :], rest], axis=1)
@@ -54,7 +56,9 @@
         half = half_ref[t]
         for n, ref in enumerate((half_ref, sinking_ref, mixing_ref)):
             params_ref[n * SUB + t : n * SUB + t + 1, :] = jnp.full((1, LANES), ref[t], F32)
-        copies[len(pairs) - own + t].wait()
+        for n, (a, _) in enumerate(cuts):
+            if t == a:
+                copies[n - len(cuts)].wait()
         for k in range(sunlit):
             rows = []
             for r in range(ROWS):
@@ -63,9 +67,11 @@
                 grad = row(cot_ref, t, k, r) * wet_at(depth[r], k)
                 rows.append(rates[r] * limiter * grad)
             held_ref[k, t] = jnp.concatenate(rows, axis=0).astype(BF16)
-        copies.append(pltpu.make_async_copy(held_ref.at[:, t], out_ref.at[:, t], out_sems.at[t]))
-        copies[-1].start()
-    for copy in copies[-own:]:
+        for n, (a, b) in enumerate(cuts):
+            if t == b - 1:
+                outs.append(pltpu.make_async_copy(held_ref.at[:, a:b], out_ref.at[:, a:b], out_sems.at[n]))
+                outs[-1].start()
+    for copy in outs:
         copy.wait()
 
 

time: 59.7 us -> 59.5 us (level)
  no operation moved by 1% of the time
where the time goes in v10:
time: 59.5 us; the launch traced here: 58.8 us
  starting transfers between devices  41.5 us (70%)
  Pallas kernels  7.28 us (12%)
  waiting for transfers between devices  7.06 us (12%)
  other arithmetic  2 us (3%)
  between operations  0.79 us (1%)
    all_to_all x1, starting transfers between devices, body(): lax.all_to_all(line_sum, 'tile', 0, 0, axis_index_groups=groups, tiled=True)  10.6 us
    all_to_all x1, starting transfers between devices, body(): lax.all_to_all(weighted, 'trc', 0, 0, axis_index_groups=order_y, tiled=True)  8.08 us
    ppermute x2, starting transfers between devices, exchanged(): lax.ppermute(part, 'tile', [(i, i ^ step) for i in range(tiles)])  7.78 us
    all_to_all x1, starting transfers between devices, body(): lax.all_to_all(fed, 'trc', 0, 0, axis_index_groups=order_y, tiled=True)  6.65 us
    ppermute x2, waiting for transfers between devices, exchanged(): lax.ppermute(part, 'tile', [(i, i ^ step) for i in range(tiles)])  4.86 us
    ppermute x1, starting transfers between devices, body(): south = lax.ppermute(halo, 'tile', across)  4.58 us
    pallas_call x1, Pallas kernels, body(): call(mixing_kernel, shape((own * levels * lines, LANES), F32), [VMEM] * 5...  3.77 us
    pallas_call x1, Pallas kernels, body(): call(weighted_kernel, (shape((sunlit, own, lines, LANES), BF16), shape((3...  2.13 us
  transfers between devices with their start and end apart: 8, of which 4 were waited for; matrix products, arithmetic and copies ran while one was open for 2% of the time, Pallas kernels for 8%

profile of v10, /device:TPU:1, one launch (start us, length us, event | category | flops | bytes accessed | tf_op | source)
XLA Modules:
  0.0 58.8 jit_solution(158681909963696711)
XLA Ops:
  0.6 2.1 %shard_map.113 = (bf16[8,7,16,128]{3,2,1,0:T(8,128)(2,1)}, f32[24,128]{1,0:T(8,128)S(1)}, f32[8,16,128]{2,1,0:T(8,128)S(1)}, s32[16,128]{1,0:T(8,128)S(1)}, s32[16,128]{1,0:T(8,128)S(1)}) custom-call(f32[7,16,16,128]{3,2,1,0:T(8,128)} %bitcast.41, f32[8,16,128]{2,1,0:T(8,128)} %bitcast.48, s32[16,128]{1,0:T(8,128)} %bitcast.49, s32[16,128]{1,0:T(8,128)} %bitcast.50, ...), custom_call_target="tpu_custom_call" | custom-call | tf_op jit(solution)/shard_map/pallas_call | solution.py:288
  2.8 0.0 copy-start.1
  2.8 0.0 copy-start.2
  2.8 8.1 %all-to-all-start = ((bf16[8,7,16,128]{3,2,1,0:T(8,128)(2,1)}), bf16[8,7,16,128]{3,2,1,0:T(8,128)(2,1)S(1)}, u32[]{:S(2)}, u32[]{:S(2)}) async-start(bf16[8,7,16,128]{3,2,1,0:T(8,128)(2,1)} %get-tuple-element.24), calls=%async_computation | async-start | bytes 458752 | tf_op jit(solution)/shard_map/all_to_all | solution.py:312
  10.9 0.5 shard_map.114
  11.4 5.4 %collective-permute-start = (f32[64,7]{1,0:T(8,128)S(1)}, f32[64,7]{1,0:T(8,128)S(1)}, u32[]{:S(2)}, u32[]{:S(2)}) collective-permute-start(f32[64,7]{1,0:T(8,128)S(1)} %get-tuple-element.25), channel_id=1, source_target_pairs={{0,8},{8,0},{16,24},{24,16},{32,40},{40,32},{48,56},{56,48},{64,72... | collective-permute-start | bytes 5384 | tf_op jit(solution)/shard_map/ppermute | solution.py:325
  16.8 0.8 %collective-permute-done = f32[64,7]{1,0:T(8,128)S(1)} collective-permute-done((f32[64,7]{1,0:T(8,128)S(1)}, f32[64,7]{1,0:T(8,128)S(1)}, u32[]{:S(2)}, u32[]{:S(2)}) %collective-permute-start) | collective-permute-done | bytes 1824 | tf_op jit(solution)/shard_map/ppermute | solution.py:325
  17.6 1.9 %collective-permute-start.1 = (f32[64,7]{1,0:T(8,128)S(1)}, f32[64,7]{1,0:T(8,128)S(1)}, u32[]{:S(2)}, u32[]{:S(2)}) collective-permute-start(f32[64,7]{1,0:T(8,128)S(1)} %add.17), channel_id=1, source_target_pairs={{0,128},{8,136},{16,144},{24,152},{32,160},{40,168},{48,176},{56,1... | collective-permute-start | bytes 5384 | tf_op jit(solution)/shard_map/ppermute | solution.py:328
  19.5 0.0 all-to-all-done
  19.5 0.4 shard_map.115
  19.9 0.7 %convert_element_type.4 = f16[56,16,128]{2,1,0:T(8,128)(2,1)} convert(f32[56,16,128]{2,1,0:T(8,128)S(1)} %shard_map.115) | non-fusion elementwise | flops 114688 | bytes 688128 | tf_op jit(solution)/shard_map/convert_element_type | solution.py:337
  20.6 1.6 %collective-permute-done.1 = f32[64,7]{1,0:T(8,128)S(1)} collective-permute-done((f32[64,7]{1,0:T(8,128)S(1)}, f32[64,7]{1,0:T(8,128)S(1)}, u32[]{:S(2)}, u32[]{:S(2)}) %collective-permute-start.1) | collective-permute-done | bytes 1824 | tf_op jit(solution)/shard_map/ppermute | solution.py:328
  22.3 6.6 %all-to-all-start.2 = ((f16[8,7,16,128]{3,2,1,0:T(8,128)(2,1)}), f16[8,7,16,128]{3,2,1,0:T(8,128)(2,1)S(1)}, u32[]{:S(2)}, u32[]{:S(2)}) async-start(f16[8,7,16,128]{3,2,1,0:T(8,128)(2,1)} %bitcast.19), calls=%async_computation.2 | async-start | bytes 458752 | tf_op jit(solution)/shard_map/all_to_all | solution.py:342
  28.9 2.4 %collective-permute-start.2 = (f32[64,7]{1,0:T(8,128)S(1)}, f32[64,7]{1,0:T(8,128)S(1)}, u32[]{:S(2)}, u32[]{:S(2)}) collective-permute-start(f32[64,7]{1,0:T(8,128)S(1)} %add.18), channel_id=1, source_target_pairs={{0,256},{8,264},{16,272},{24,280},{32,288},{40,296},{48,304},{56,3... | collective-permute-start | bytes 5384 | tf_op jit(solution)/shard_map/ppermute | solution.py:325
  31.3 4.0 %collective-permute-done.2 = f32[64,7]{1,0:T(8,128)S(1)} collective-permute-done((f32[64,7]{1,0:T(8,128)S(1)}, f32[64,7]{1,0:T(8,128)S(1)}, u32[]{:S(2)}, u32[]{:S(2)}) %collective-permute-start.2) | collective-permute-done | bytes 1824 | tf_op jit(solution)/shard_map/ppermute | solution.py:325
  35.3 0.6 %add.19 = f32[64,7]{1,0:T(8,128)} add(f32[64,7]{1,0:T(8,128)S(1)} %add.18, f32[64,7]{1,0:T(8,128)S(1)} %collective-permute-done.2) | non-fusion elementwise | flops 448 | bytes 5376 | tf_op jit(solution)/shard_map/add | solution.py:325
  36.0 0.5 shard_map.116
  36.5 4.6 %collective-permute-start.3 = (bf16[113,16,128]{2,1,0:T(8,128)(2,1)S(1)}, bf16[113,16,128]{2,1,0:T(8,128)(2,1)S(1)}, u32[]{:S(2)}, u32[]{:S(2)}) collective-permute-start(bf16[113,16,128]{2,1,0:T(8,128)(2,1)S(1)} %get-tuple-element.33), channel_id=1, source_target_pairs={{8,16},{16,8},{24,32},{32,24},{40,48},{48,40},{56,64},{64,56},{72,... | collective-permute-start | bytes 1388552 | tf_op jit(solution)/shard_map/ppermute | solution.py:351
  41.1 1.9 %collective-permute-start.4 = (bf16[113,16,128]{2,1,0:T(8,128)(2,1)S(1)}, bf16[113,16,128]{2,1,0:T(8,128)(2,1)S(1)}, u32[]{:S(2)}, u32[]{:S(2)}) collective-permute-start(bf16[113,16,128]{2,1,0:T(8,128)(2,1)S(1)} %get-tuple-element.33), channel_id=1, source_target_pairs={{0,8},{8,0},{16,24},{24,16},{32,40},{40,32},{48,56},{56,48},{64,72... | collective-permute-start | bytes 1388552 | tf_op jit(solution)/shard_map/ppermute | solution.py:352
  43.1 10.6 %all-to-all-start.1 = ((f32[8,8,7]{2,1,0:T(8,128)}), f32[8,8,7]{2,1,0:T(8,128)S(1)}, u32[]{:S(2)}, u32[]{:S(2)}) async-start(f32[8,8,7]{2,1,0:T(8,128)} %bitcast.20), calls=%async_computation.1 | async-start | bytes 65536 | tf_op jit(solution)/shard_map/all_to_all | solution.py:356
  53.7 0.1 iota.12
  53.8 3.8 %shard_map.117 = f32[1792,128]{1,0:T(8,128)} custom-call(f32[112,16,128]{2,1,0:T(8,128)S(1)} %get-tuple-element.32.col_ref, bf16[113,16,128]{2,1,0:T(8,128)(2,1)S(1)} %collective-permute-done.3.south_ref, bf16[113,16,128]{2,1,0:T(8,128)(2,1)S(1)} %collective-permute-done.4.north_ref, s32[16,128]{1,0:T(8,128)S(1)} %get-tuple-element.20.depth_ref, ...), custom_call_target="tpu_custom_call" | custom-call | flops 1000000 | bytes 2000000 | tf_op jit(solution)/shard_map/pallas_call | solution.py:357
  57.6 0.6 all-to-all-done.1
  58.2 0.6 %select_reduce_fusion = f32[7]{0:T(128)} fusion(f32[64,7]{1,0:T(8,128)S(1)} %bitcast.47, pred[64]{0:T(512)(128)(4,1)S(1)} %iota.12), kind=kLoop, calls=%fused_computation.1 | loop fusion | flops 889 | bytes 1884 | tf_op jit(solution)/shard_map/reduce_sum | solution.py:375
  (12 shorter events, 0.1 us)
Async XLA Ops:
  0.6 10.3 %copy-start = (f32[7,16,2,1024]{3,2,1,0:T(2,128)S(1)}, f32[7,16,2,1024]{3,2,1,0:T(2,128)}, u32[]{:S(2)}) copy-start(f32[7,16,2,1024]{3,2,1,0:T(2,128)} %param.10) | copy-start | bytes 2752516
  2.8 8.1 %copy-start.1 = (bf16[7,8,2,1024]{3,2,1,0:T(2,128)(2,1)S(1)}, bf16[7,8,2,1024]{3,2,1,0:T(2,128)(2,1)}, u32[]{:S(2)}) copy-start(bf16[7,8,2,1024]{3,2,1,0:T(2,128)(2,1)} %param.11) | copy-start | bytes 688132
  2.8 8.1 %copy-start.2 = (bf16[56,56]{1,0:T(8,128)(2,1)S(1)}, bf16[56,56]{1,0:T(8,128)(2,1)}, u32[]{:S(2)}) copy-start(bf16[56,56]{1,0:T(8,128)(2,1)} %matrix_ref.1) | copy-start | bytes 18820
  2.8 16.7 %all-to-all-start = ((bf16[8,7,16,128]{3,2,1,0:T(8,128)(2,1)}), bf16[8,7,16,128]{3,2,1,0:T(8,128)(2,1)S(1)}, u32[]{:S(2)}, u32[]{:S(2)}) async-start(bf16[8,7,16,128]{3,2,1,0:T(8,128)(2,1)} %get-tuple-element.24), calls=%async_computation | async-start | bytes 458752 | tf_op jit(solution)/shard_map/all_to_all | solution.py:312
  11.4 6.2 %collective-permute-start = (f32[64,7]{1,0:T(8,128)S(1)}, f32[64,7]{1,0:T(8,128)S(1)}, u32[]{:S(2)}, u32[]{:S(2)}) collective-permute-start(f32[64,7]{1,0:T(8,128)S(1)} %get-tuple-element.25), channel_id=1, source_target_pairs={{0,8},{8,0},{16,24},{24,16},{32,40},{40,32},{48,56},{56,48},{64,72... | collective-permute-start | bytes 5384 | tf_op jit(solution)/shard_map/ppermute | solution.py:325
  17.6 4.6 %collective-permute-start.1 = (f32[64,7]{1,0:T(8,128)S(1)}, f32[64,7]{1,0:T(8,128)S(1)}, u32[]{:S(2)}, u32[]{:S(2)}) collective-permute-start(f32[64,7]{1,0:T(8,128)S(1)} %add.17), channel_id=1, source_target_pairs={{0,128},{8,136},{16,144},{24,152},{32,160},{40,168},{48,176},{56,1... | collective-permute-start | bytes 5384 | tf_op jit(solution)/shard_map/ppermute | solution.py:328
  22.3 13.7 %all-to-all-start.2 = ((f16[8,7,16,128]{3,2,1,0:T(8,128)(2,1)}), f16[8,7,16,128]{3,2,1,0:T(8,128)(2,1)S(1)}, u32[]{:S(2)}, u32[]{:S(2)}) async-start(f16[8,7,16,128]{3,2,1,0:T(8,128)(2,1)} %bitcast.19), calls=%async_computation.2 | async-start | bytes 458752 | tf_op jit(solution)/shard_map/all_to_all | solution.py:342
  28.9 6.4 %collective-permute-start.2 = (f32[64,7]{1,0:T(8,128)S(1)}, f32[64,7]{1,0:T(8,128)S(1)}, u32[]{:S(2)}, u32[]{:S(2)}) collective-permute-start(f32[64,7]{1,0:T(8,128)S(1)} %add.18), channel_id=1, source_target_pairs={{0,256},{8,264},{16,272},{24,280},{32,288},{40,296},{48,304},{56,3... | collective-permute-start | bytes 5384 | tf_op jit(solution)/shard_map/ppermute | solution.py:325
  36.5 17.2 %collective-permute-start.3 = (bf16[113,16,128]{2,1,0:T(8,128)(2,1)S(1)}, bf16[113,16,128]{2,1,0:T(8,128)(2,1)S(1)}, u32[]{:S(2)}, u32[]{:S(2)}) collective-permute-start(bf16[113,16,128]{2,1,0:T(8,128)(2,1)S(1)} %get-tuple-element.33), channel_id=1, source_target_pairs={{8,16},{16,8},{24,32},{32,24},{40,48},{48,40},{56,64},{64,56},{72,... | collective-permute-start | bytes 1388552 | tf_op jit(solution)/shard_map/ppermute | solution.py:351
  41.1 12.7 %collective-permute-start.4 = (bf16[113,16,128]{2,1,0:T(8,128)(2,1)S(1)}, bf16[113,16,128]{2,1,0:T(8,128)(2,1)S(1)}, u32[]{:S(2)}, u32[]{:S(2)}) collective-permute-start(bf16[113,16,128]{2,1,0:T(8,128)(2,1)S(1)} %get-tuple-element.33), channel_id=1, source_target_pairs={{0,8},{8,0},{16,24},{24,16},{32,40},{40,32},{48,56},{56,48},{64,72... | collective-permute-start | bytes 1388552 | tf_op jit(solution)/shard_map/ppermute | solution.py:352
  43.1 15.1 %all-to-all-start.1 = ((f32[8,8,7]{2,1,0:T(8,128)}), f32[8,8,7]{2,1,0:T(8,128)S(1)}, u32[]{:S(2)}, u32[]{:S(2)}) async-start(f32[8,8,7]{2,1,0:T(8,128)} %bitcast.20), calls=%async_computation.1 | async-start | bytes 65536 | tf_op jit(solution)/shard_map/all_to_all | solution.py:356

commit v11 on v10

--- a/solution.py
+++ b/solution.py
@@ -76,7 +76,7 @@
 
 
 def province_kernel(cot_ref, uptake_ref, nutrient_ref, depth_ref, region_ref, params_ref, matrix_ref, out_ref, turned_ref, hot_ref, term_ref, parts_ref):
-    provinces, own = out_ref.shape
+    own, provinces = out_ref.shape
 
     def reversed_blocks(m):
         return jnp.concatenate([m[i : i + own] for i in range(m.shape[0] - own, -1, -own)], axis=0)
@@ -105,9 +105,9 @@
         high = term.astype(BF16).astype(F32)
         both = jnp.concatenate([high, term - high], axis=0)
         parts_ref[:, s * LANES : (s + 1) * LANES] = both.astype(BF16)
-    sums = lax.dot_general(hot_ref[...], parts_ref[...], (((1,), (1,)), ((), ())), preferred_element_type=F32)
+    sums = lax.dot_general(parts_ref[...], hot_ref[...], (((1,), (1,)), ((), ())), preferred_element_type=F32)
     scale = 1.0 / (sunlit * lines * LANES)
-    out_ref[...] = (sums[:, 0:own] + sums[:, SUB : SUB + own]) * scale
+    out_ref[...] = (sums[0:own] + sums[SUB : SUB + own]) * scale
 
 
 def feed_kernel(matrix_ref, weighted_ref, out_ref, wide_ref, fed_ref):
@@ -312,7 +312,7 @@
     all_tracers = lax.all_to_all(weighted, "trc", 0, 0, axis_index_groups=order_y, tiled=True).reshape(tracers, lines, LANES)
     province_part, turned = call(
         province_kernel,
-        (shape((provinces, own), F32), shape(uptake_matrix.shape, BF16)),
+        (shape((own, provinces), F32), shape(uptake_matrix.shape, BF16)),
         [VMEM] * 7,
         (VMEM,) * 2,
         [
@@ -353,7 +353,7 @@
     groups = [
         [(x * CHIPS_Z + z) * CORES + core for z in reversed(range(CHIPS_Z))] for x in range(CHIPS_X) for core in range(CORES)
     ]
-    own_parts = lax.all_to_all(line_sum, "tile", 0, 0, axis_index_groups=groups, tiled=True)
+    own_parts = lax.all_to_all(line_sum.T, "tile", 0, 0, axis_index_groups=groups, tiled=True)
     tracer_grad = call(
         mixing_kernel,
         shape((own * levels * lines, LANES), F32),

time: 59.5 us -> 63.2 us (1.062)
  waiting for transfers between devices: 7.06 us -> 10.2 us
  local copies, waits for them, and re-layouts: 0.11 us -> 0.9 us
    all_to_all x1, waiting for transfers between devices: 0.58 us -> 4.37 us  [body(): lax.all_to_all(line_sum.T, 'tile', 0, 0, axis_index_groups=groups, tiled=...]
    all_to_all x0 -> x4, local copies, waits for them, and re-layouts: none -> 0.78 us  [body(): lax.all_to_all(line_sum.T, 'tile', 0, 0, axis_index_groups=groups, tiled=...]
  transfers between devices with their start and end apart: 8 -> 8, of which waited for: 4 -> 4; matrix products, arithmetic and copies ran while one was open for 2% -> 2% of each run, Pallas kernels for 8% -> 1%
where the time goes in v11:
time: 63.2 us; the launch traced here: 62.4 us
  starting transfers between devices  42 us (66%)
  waiting for transfers between devices  10.2 us (16%)
  Pallas kernels  7.17 us (11%)
  other arithmetic  1.41 us (2%)
  local copies, waits for them, and re-layouts  0.9 us (1%)
  between operations  0.78 us (1%)
    all_to_all x1, starting transfers between devices, body(): lax.all_to_all(line_sum.T, 'tile', 0, 0, axis_index_groups=groups, tiled=...  10.6 us
    all_to_all x1, starting transfers between devices, body(): lax.all_to_all(weighted, 'trc', 0, 0, axis_index_groups=order_y, tiled=True)  8.08 us
    ppermute x2, starting transfers between devices, exchanged(): lax.ppermute(part, 'tile', [(i, i ^ step) for i in range(tiles)])  7.79 us
    all_to_all x1, starting transfers between devices, body(): lax.all_to_all(fed, 'trc', 0, 0, axis_index_groups=order_y, tiled=True)  6.65 us
    ppermute x1, starting transfers between devices, body(): south = lax.ppermute(halo, 'tile', across)  5.03 us
    ppermute x2, waiting for transfers between devices, exchanged(): lax.ppermute(part, 'tile', [(i, i ^ step) for i in range(tiles)])  4.51 us
    all_to_all x1, waiting for transfers between devices, body(): lax.all_to_all(line_sum.T, 'tile', 0, 0, axis_index_groups=groups, tiled=...  4.37 us
    pallas_call x1, Pallas kernels, body(): call(mixing_kernel, shape((own * levels * lines, LANES), F32), [VMEM] * 5...  3.77 us
  transfers between devices with their start and end apart: 8, of which 4 were waited for; matrix products, arithmetic and copies ran while one was open for 2% of the time, Pallas kernels for 1%

profile of v11, /device:TPU:1, one launch (start us, length us, event | category | flops | bytes accessed | tf_op | source)
XLA Modules:
  0.0 62.4 jit_solution(15982441633735877517)
XLA Ops:
  0.6 2.1 %shard_map.113 = (bf16[8,7,16,128]{3,2,1,0:T(8,128)(2,1)}, f32[24,128]{1,0:T(8,128)S(1)}, f32[8,16,128]{2,1,0:T(8,128)S(1)}, s32[16,128]{1,0:T(8,128)S(1)}, s32[16,128]{1,0:T(8,128)S(1)}) custom-call(f32[7,16,16,128]{3,2,1,0:T(8,128)} %bitcast.44, f32[8,16,128]{2,1,0:T(8,128)} %bitcast.50, s32[16,128]{1,0:T(8,128)} %bitcast.52, s32[16,128]{1,0:T(8,128)} %bitcast.53, ...), custom_call_target="tpu_custom_call" | custom-call | tf_op jit(solution)/shard_map/pallas_call | solution.py:288
  2.8 0.0 copy-start.1
  2.8 8.1 %all-to-all-start = ((bf16[8,7,16,128]{3,2,1,0:T(8,128)(2,1)}), bf16[8,7,16,128]{3,2,1,0:T(8,128)(2,1)S(1)}, u32[]{:S(2)}, u32[]{:S(2)}) async-start(bf16[8,7,16,128]{3,2,1,0:T(8,128)(2,1)} %get-tuple-element.24), calls=%async_computation | async-start | bytes 458752 | tf_op jit(solution)/shard_map/all_to_all | solution.py:312
  10.9 0.4 shard_map.114
  11.3 5.4 %collective-permute-start = (f32[7,64]{1,0:T(8,128)S(1)}, f32[7,64]{1,0:T(8,128)S(1)}, u32[]{:S(2)}, u32[]{:S(2)}) collective-permute-start(f32[7,64]{1,0:T(8,128)S(1)} %get-tuple-element.25), channel_id=1, source_target_pairs={{0,8},{8,0},{16,24},{24,16},{32,40},{40,32},{48,56},{56,48},{64,72... | collective-permute-start | bytes 5384 | tf_op jit(solution)/shard_map/ppermute | solution.py:325
  16.6 0.8 %collective-permute-done = f32[7,64]{1,0:T(8,128)S(1)} collective-permute-done((f32[7,64]{1,0:T(8,128)S(1)}, f32[7,64]{1,0:T(8,128)S(1)}, u32[]{:S(2)}, u32[]{:S(2)}) %collective-permute-start) | collective-permute-done | bytes 1824 | tf_op jit(solution)/shard_map/ppermute | solution.py:325
  17.5 1.9 %collective-permute-start.1 = (f32[7,64]{1,0:T(8,128)S(1)}, f32[7,64]{1,0:T(8,128)S(1)}, u32[]{:S(2)}, u32[]{:S(2)}) collective-permute-start(f32[7,64]{1,0:T(8,128)S(1)} %add.17), channel_id=1, source_target_pairs={{0,128},{8,136},{16,144},{24,152},{32,160},{40,168},{48,176},{56,1... | collective-permute-start | bytes 5384 | tf_op jit(solution)/shard_map/ppermute | solution.py:328
  19.4 0.4 shard_map.115
  19.8 0.7 %convert_element_type.4 = f16[56,16,128]{2,1,0:T(8,128)(2,1)} convert(f32[56,16,128]{2,1,0:T(8,128)S(1)} %shard_map.115) | non-fusion elementwise | flops 114688 | bytes 688128 | tf_op jit(solution)/shard_map/convert_element_type | solution.py:337
  20.5 1.3 %collective-permute-done.1 = f32[7,64]{1,0:T(8,128)S(1)} collective-permute-done((f32[7,64]{1,0:T(8,128)S(1)}, f32[7,64]{1,0:T(8,128)S(1)}, u32[]{:S(2)}, u32[]{:S(2)}) %collective-permute-start.1) | collective-permute-done | bytes 1824 | tf_op jit(solution)/shard_map/ppermute | solution.py:328
  21.8 6.6 %all-to-all-start.2 = ((f16[8,7,16,128]{3,2,1,0:T(8,128)(2,1)}), f16[8,7,16,128]{3,2,1,0:T(8,128)(2,1)S(1)}, u32[]{:S(2)}, u32[]{:S(2)}) async-start(f16[8,7,16,128]{3,2,1,0:T(8,128)(2,1)} %bitcast.19), calls=%async_computation.2 | async-start | bytes 458752 | tf_op jit(solution)/shard_map/all_to_all | solution.py:342
  28.4 2.4 %collective-permute-start.2 = (f32[7,64]{1,0:T(8,128)S(1)}, f32[7,64]{1,0:T(8,128)S(1)}, u32[]{:S(2)}, u32[]{:S(2)}) collective-permute-start(f32[7,64]{1,0:T(8,128)S(1)} %add.18), channel_id=1, source_target_pairs={{0,256},{8,264},{16,272},{24,280},{32,288},{40,296},{48,304},{56,3... | collective-permute-start | bytes 5384 | tf_op jit(solution)/shard_map/ppermute | solution.py:325
  30.9 3.7 %collective-permute-done.2 = f32[7,64]{1,0:T(8,128)S(1)} collective-permute-done((f32[7,64]{1,0:T(8,128)S(1)}, f32[7,64]{1,0:T(8,128)S(1)}, u32[]{:S(2)}, u32[]{:S(2)}) %collective-permute-start.2) | collective-permute-done | bytes 1824 | tf_op jit(solution)/shard_map/ppermute | solution.py:325
  34.6 0.5 shard_map.116
  35.2 5.0 %collective-permute-start.3 = (bf16[113,16,128]{2,1,0:T(8,128)(2,1)S(1)}, bf16[113,16,128]{2,1,0:T(8,128)(2,1)S(1)}, u32[]{:S(2)}, u32[]{:S(2)}) collective-permute-start(bf16[113,16,128]{2,1,0:T(8,128)(2,1)S(1)} %get-tuple-element.33), channel_id=1, source_target_pairs={{8,16},{16,8},{24,32},{32,24},{40,48},{48,40},{56,64},{64,56},{72,... | collective-permute-start | bytes 1388552 | tf_op jit(solution)/shard_map/ppermute | solution.py:351
  40.2 1.9 %collective-permute-start.4 = (bf16[113,16,128]{2,1,0:T(8,128)(2,1)S(1)}, bf16[113,16,128]{2,1,0:T(8,128)(2,1)S(1)}, u32[]{:S(2)}, u32[]{:S(2)}) collective-permute-start(bf16[113,16,128]{2,1,0:T(8,128)(2,1)S(1)} %get-tuple-element.33), channel_id=1, source_target_pairs={{0,8},{8,0},{16,24},{24,16},{32,40},{40,32},{48,56},{56,48},{64,72... | collective-permute-start | bytes 1388552 | tf_op jit(solution)/shard_map/ppermute | solution.py:352
  42.2 0.1 all_to_all.15
  42.2 0.6 %copy.30 = f32[8,8,7]{1,2,0:T(8,128)} copy(f32[8,8,7]{1,0,2:T(8,128)S(1)} %all_to_all.15) | data formatting | bytes 3584 | tf_op jit(solution)/shard_map/all_to_all | solution.py:356
  42.9 10.6 %all-to-all-start.1 = ((f32[8,8,7]{1,2,0:T(8,128)}), f32[8,8,7]{1,2,0:T(8,128)S(1)}, u32[]{:S(2)}, u32[]{:S(2)}) async-start(f32[8,8,7]{1,2,0:T(8,128)} %copy.30), calls=%async_computation.1 | async-start | bytes 65536 | tf_op jit(solution)/shard_map/all_to_all | solution.py:356
  53.5 0.1 iota.12
  53.5 4.4 %all-to-all-done.1 = f32[8,8,7]{1,2,0:T(8,128)S(1)} async-done(((f32[8,8,7]{1,2,0:T(8,128)}), f32[8,8,7]{1,2,0:T(8,128)S(1)}, u32[]{:S(2)}, u32[]{:S(2)}) %all-to-all-start.1) | async-done | bytes 1824 | tf_op jit(solution)/shard_map/all_to_all | solution.py:356
  57.9 0.1 all_to_all.17
  58.0 3.8 %shard_map.117 = f32[1792,128]{1,0:T(8,128)} custom-call(f32[112,16,128]{2,1,0:T(8,128)S(1)} %get-tuple-element.32.col_ref, bf16[113,16,128]{2,1,0:T(8,128)(2,1)S(1)} %collective-permute-done.3.south_ref, bf16[113,16,128]{2,1,0:T(8,128)(2,1)S(1)} %collective-permute-done.4.north_ref, s32[16,128]{1,0:T(8,128)S(1)} %get-tuple-element.20.depth_ref, ...), custom_call_target="tpu_custom_call" | custom-call | flops 1000000 | bytes 2000000 | tf_op jit(solution)/shard_map/pallas_call | solution.py:357
  61.8 0.6 %select_reduce_fusion = f32[7]{0:T(128)} fusion(f32[64,7]{0,1:T(8,128)S(1)} %all_to_all.17, pred[64]{0:T(512)(128)(4,1)S(1)} %iota.12), kind=kLoop, calls=%fused_computation.1 | loop fusion | flops 889 | bytes 1884 | tf_op jit(solution)/shard_map/reduce_sum | solution.py:375
  (16 shorter events, 0.1 us)
Async XLA Ops:
  0.6 10.3 %copy-start = (f32[7,16,2,1024]{3,2,1,0:T(2,128)S(1)}, f32[7,16,2,1024]{3,2,1,0:T(2,128)}, u32[]{:S(2)}) copy-start(f32[7,16,2,1024]{3,2,1,0:T(2,128)} %param.10) | copy-start | bytes 2752516
  2.8 8.1 %copy-start.1 = (bf16[7,8,2,1024]{3,2,1,0:T(2,128)(2,1)S(1)}, bf16[7,8,2,1024]{3,2,1,0:T(2,128)(2,1)}, u32[]{:S(2)}) copy-start(bf16[7,8,2,1024]{3,2,1,0:T(2,128)(2,1)} %param.11) | copy-start | bytes 688132
  2.8 8.1 %copy-start.2 = (bf16[56,56]{1,0:T(8,128)(2,1)S(1)}, bf16[56,56]{1,0:T(8,128)(2,1)}, u32[]{:S(2)}) copy-start(bf16[56,56]{1,0:T(8,128)(2,1)} %matrix_ref.1) | copy-start | bytes 18820
  2.8 16.6 %all-to-all-start = ((bf16[8,7,16,128]{3,2,1,0:T(8,128)(2,1)}), bf16[8,7,16,128]{3,2,1,0:T(8,128)(2,1)S(1)}, u32[]{:S(2)}, u32[]{:S(2)}) async-start(bf16[8,7,16,128]{3,2,1,0:T(8,128)(2,1)} %get-tuple-element.24), calls=%async_computation | async-start | bytes 458752 | tf_op jit(solution)/shard_map/all_to_all | solution.py:312
  11.3 6.2 %collective-permute-start = (f32[7,64]{1,0:T(8,128)S(1)}, f32[7,64]{1,0:T(8,128)S(1)}, u32[]{:S(2)}, u32[]{:S(2)}) collective-permute-start(f32[7,64]{1,0:T(8,128)S(1)} %get-tuple-element.25), channel_id=1, source_target_pairs={{0,8},{8,0},{16,24},{24,16},{32,40},{40,32},{48,56},{56,48},{64,72... | collective-permute-start | bytes 5384 | tf_op jit(solution)/shard_map/ppermute | solution.py:325
  17.5 4.3 %collective-permute-start.1 = (f32[7,64]{1,0:T(8,128)S(1)}, f32[7,64]{1,0:T(8,128)S(1)}, u32[]{:S(2)}, u32[]{:S(2)}) collective-permute-start(f32[7,64]{1,0:T(8,128)S(1)} %add.17), channel_id=1, source_target_pairs={{0,128},{8,136},{16,144},{24,152},{32,160},{40,168},{48,176},{56,1... | collective-permute-start | bytes 5384 | tf_op jit(solution)/shard_map/ppermute | solution.py:328
  21.8 12.8 %all-to-all-start.2 = ((f16[8,7,16,128]{3,2,1,0:T(8,128)(2,1)}), f16[8,7,16,128]{3,2,1,0:T(8,128)(2,1)S(1)}, u32[]{:S(2)}, u32[]{:S(2)}) async-start(f16[8,7,16,128]{3,2,1,0:T(8,128)(2,1)} %bitcast.19), calls=%async_computation.2 | async-start | bytes 458752 | tf_op jit(solution)/shard_map/all_to_all | solution.py:342
  28.4 6.1 %collective-permute-start.2 = (f32[7,64]{1,0:T(8,128)S(1)}, f32[7,64]{1,0:T(8,128)S(1)}, u32[]{:S(2)}, u32[]{:S(2)}) collective-permute-start(f32[7,64]{1,0:T(8,128)S(1)} %add.18), channel_id=1, source_target_pairs={{0,256},{8,264},{16,272},{24,280},{32,288},{40,296},{48,304},{56,3... | collective-permute-start | bytes 5384 | tf_op jit(solution)/shard_map/ppermute | solution.py:325
  35.2 22.8 %collective-permute-start.3 = (bf16[113,16,128]{2,1,0:T(8,128)(2,1)S(1)}, bf16[113,16,128]{2,1,0:T(8,128)(2,1)S(1)}, u32[]{:S(2)}, u32[]{:S(2)}) collective-permute-start(bf16[113,16,128]{2,1,0:T(8,128)(2,1)S(1)} %get-tuple-element.33), channel_id=1, source_target_pairs={{8,16},{16,8},{24,32},{32,24},{40,48},{48,40},{56,64},{64,56},{72,... | collective-permute-start | bytes 1388552 | tf_op jit(solution)/shard_map/ppermute | solution.py:351
  40.2 17.8 %collective-permute-start.4 = (bf16[113,16,128]{2,1,0:T(8,128)(2,1)S(1)}, bf16[113,16,128]{2,1,0:T(8,128)(2,1)S(1)}, u32[]{:S(2)}, u32[]{:S(2)}) collective-permute-start(bf16[113,16,128]{2,1,0:T(8,128)(2,1)S(1)} %get-tuple-element.33), channel_id=1, source_target_pairs={{0,8},{8,0},{16,24},{24,16},{32,40},{40,32},{48,56},{56,48},{64,72... | collective-permute-start | bytes 1388552 | tf_op jit(solution)/shard_map/ppermute | solution.py:352
  42.9 15.1 %all-to-all-start.1 = ((f32[8,8,7]{1,2,0:T(8,128)}), f32[8,8,7]{1,2,0:T(8,128)S(1)}, u32[]{:S(2)}, u32[]{:S(2)}) async-start(f32[8,8,7]{1,2,0:T(8,128)} %copy.30), calls=%async_computation.1 | async-start | bytes 65536 | tf_op jit(solution)/shard_map/all_to_all | solution.py:356
